TPU v7x, 32 devices: a whole 2x2x4 slice. The times are simulated.
32 devices in a mesh: dp: 16 (over z, y, x), mp: 2 (over core).
Axes of the slice: x: 2, y: 2, z: 4, core: 2. Of those that a mesh axis runs over, the one named last changes fastest.
Arguments:
- inputs: float32 [50176, 1024], P(('dp', 'mp')), may hold values from -6 to 6
- patch_keep: int32 [256, 196], P('dp'), may hold values from 0 to 1, as said below
- patch_gainone: float32 [1024], replicated, may hold values from 0.25 to 1.75
- patch_project: bfloat16 [3, 1024, 1024], P(None, None, 'mp'), may hold values from -0.1875 to 0.1875
- patch_outproj: bfloat16 [1024, 1024], P('mp'), may hold values from -1 to 1
- patch_gaintwo: float32 [1024], replicated, may hold values from 0.25 to 1.75
- patch_upward: bfloat16 [1024, 4096], P(None, 'mp'), may hold values from -0.1875 to 0.1875
- patch_downward: bfloat16 [4096, 1024], P('mp'), may hold values from -0.09375 to 0.09375
- learner_gain: float32 [1024], replicated, may hold values from 0.25 to 1.75
- learner_weight: float32 [1024, 8], replicated, may hold values from -0.375 to 0.375
- token_gainone: float32 [1024], replicated, may hold values from 0.25 to 1.75
- token_project: bfloat16 [3, 1024, 1024], P(None, None, 'mp'), may hold values from -0.1875 to 0.1875
- token_outproj: bfloat16 [1024, 1024], P('mp'), may hold values from -0.375 to 0.375
- token_gaintwo: float32 [1024], replicated, may hold values from 0.25 to 1.75
- token_upward: bfloat16 [1024, 4096], P(None, 'mp'), may hold values from -0.1875 to 0.1875
- token_downward: bfloat16 [4096, 1024], P('mp'), may hold values from -0.09375 to 0.09375
- output_grad: float32 [2048, 1024], P(('dp', 'mp')), may hold values from -6 to 6
Outputs:
- token_output: float32 [2048, 1024], P(('dp', 'mp'))
- input_grad: float32 [50176, 1024], P(('dp', 'mp'))
- patch_gainone_grad: float32 [1024], replicated
- patch_project_grad: float32 [3, 1024, 1024], P(None, None, 'mp')
- patch_outproj_grad: float32 [1024, 1024], P('mp')
- patch_gaintwo_grad: float32 [1024], replicated
- patch_upward_grad: float32 [1024, 4096], P(None, 'mp')
- patch_downward_grad: float32 [4096, 1024], P('mp')
- learner_gain_grad: float32 [1024], replicated
- learner_weight_grad: float32 [1024, 8], replicated
- token_gainone_grad: float32 [1024], replicated
- token_project_grad: float32 [3, 1024, 1024], P(None, None, 'mp')
- token_outproj_grad: float32 [1024, 1024], P('mp')
- token_gaintwo_grad: float32 [1024], replicated
- token_upward_grad: float32 [1024, 4096], P(None, 'mp')
- token_downward_grad: float32 [4096, 1024], P('mp')
Inputs may be any that keep to these rules, and one draw needn't show every extreme that they name: `patch_keep`: each image keeps between 98 and 196 of its patches, the count and the kept places drawn afresh for every image.
All inputs are finite; a program needn't handle non-finite values.
Results may differ from a plain program's by a relative error of at most 0.03.
Values may be sent and summed in bfloat16 or wider, within the bound.
No kernel may reach another device: no remote copies, remote signals or barrier semaphores. Data moves between devices by JAX's collectives and lax.ppermute only.
A program may use at most 384 MiB of HBM per device.

v0:
```python
from functools import partial

import jax
import jax.numpy as jnp
from jax import lax
from jax.sharding import PartitionSpec as P

HEAD_DIM = 64
P_SIZE = 196
S = 8


epsilon = 1e-06
highest = lax.Precision.HIGHEST


def norm_rows(matrix, scales):
    center = matrix - jnp.mean(matrix, axis=-1, keepdims=True)
    spread = jnp.mean(center * center, axis=-1, keepdims=True)
    return center * lax.rsqrt(spread + epsilon) * scales


def attend(queries, key_rows, values, visible):
    factor = HEAD_DIM ** (-0.5)
    scores = (
        jnp.einsum("bqhe,bkhe->bhqk", queries, key_rows, preferred_element_type=jnp.float32)
        * factor
    )
    scores = jnp.where(visible[:, None, None, :], scores, -1e30)
    highest_score = jnp.max(scores, axis=-1, keepdims=True)
    totals = highest_score + jnp.log(
        jnp.sum(jnp.exp(scores - highest_score), axis=-1, keepdims=True)
    )
    shares = jnp.exp(scores - totals)
    attended = jnp.einsum(
        "bhqk,bkhe->bqhe", shares.astype(jnp.bfloat16), values, preferred_element_type=jnp.float32
    )
    return (attended, totals)


def attend_back(queries, key_rows, values, visible, totals, grad_context):
    factor = HEAD_DIM ** (-0.5)
    scores = (
        jnp.einsum("bqhe,bkhe->bhqk", queries, key_rows, preferred_element_type=jnp.float32)
        * factor
    )
    scores = jnp.where(visible[:, None, None, :], scores, -1e30)
    shares = jnp.exp(scores - totals)
    grad_values = jnp.einsum(
        "bhqk,bqhe->bkhe",
        shares.astype(jnp.bfloat16),
        grad_context,
        preferred_element_type=jnp.float32,
    ).astype(jnp.bfloat16)
    grad_shares = jnp.einsum(
        "bqhe,bkhe->bhqk", grad_context, values, preferred_element_type=jnp.float32
    )
    inner = jnp.sum(shares * grad_shares, axis=-1, keepdims=True)
    grad_scores = (shares * (grad_shares - inner)).astype(jnp.bfloat16)
    grad_query = (
        factor
        * jnp.einsum("bhqk,bkhe->bqhe", grad_scores, key_rows, preferred_element_type=jnp.float32)
    ).astype(jnp.bfloat16)
    grad_keys = (
        factor
        * jnp.einsum("bhqk,bqhe->bkhe", grad_scores, queries, preferred_element_type=jnp.float32)
    ).astype(jnp.bfloat16)
    return (grad_query, grad_keys, grad_values)


def gelu_exact(tensor):
    return jax.nn.gelu(tensor, approximate=False)


def gelu_back(upward, grad_active):
    return jax.vjp(gelu_exact, upward)[1](grad_active)[0]


def forward(inputs, weights, visible, length, transfer):
    gain_one, weight_qkv, weight_out, gain_two, weight_up, weight_down = weights
    row_count = inputs.shape[0]
    across = transfer[0](norm_rows(inputs, gain_one).astype(jnp.bfloat16))
    projected = jnp.einsum(
        "rd,tdc->trc", across, weight_qkv, preferred_element_type=jnp.float32
    ).astype(jnp.bfloat16)
    head_shape = (across.shape[0] // length, length, projected.shape[2] // HEAD_DIM, HEAD_DIM)
    heads_view = projected.reshape((3,) + head_shape)
    attended, totals = attend(heads_view[0], heads_view[1], heads_view[2], visible)
    context = attended.reshape(across.shape[0], projected.shape[2]).astype(jnp.bfloat16)

    def attention_term(offset, number):
        return jnp.dot(context, weight_out, preferred_element_type=jnp.float32)

    hidden = inputs + transfer[1](attention_term, row_count)
    second = transfer[2](norm_rows(hidden, gain_two).astype(jnp.bfloat16))
    upward = jnp.dot(second, weight_up, preferred_element_type=jnp.float32)
    active = gelu_exact(upward).astype(jnp.bfloat16)

    def mlp_term(offset, number):
        return jnp.dot(active, weight_down, preferred_element_type=jnp.float32)

    result = hidden + transfer[3](mlp_term, row_count)
    return (result, (inputs, hidden, across, projected, totals, context, second, upward, active))


def backward(grad_out, stored, weights, visible, length, transfer):
    gain_one, weight_qkv, weight_out, gain_two, weight_up, weight_down = weights
    inputs, hidden, across, projected, totals, context, second, upward, active = stored
    row_count = inputs.shape[0]
    grad_mix = transfer[4](grad_out.astype(jnp.bfloat16))
    grad_down = jnp.einsum("rf,rd->fd", active, grad_mix, preferred_element_type=jnp.float32)
    grad_active = jnp.einsum("rd,fd->rf", grad_mix, weight_down, preferred_element_type=jnp.float32)
    grad_upin = gelu_back(upward, grad_active).astype(jnp.bfloat16)
    grad_upw = jnp.einsum("rd,rf->df", second, grad_upin, preferred_element_type=jnp.float32)

    def upward_term(offset, number):
        return jnp.einsum("rf,df->rd", grad_upin, weight_up, preferred_element_type=jnp.float32)

    grad_second = transfer[5](upward_term, row_count)
    pull_two = jax.vjp(norm_rows, hidden, gain_two)[1]
    back_hidden, grad_gain_two = pull_two(grad_second)
    grad_hidden = grad_out + back_hidden
    grad_branch = transfer[6](grad_hidden.astype(jnp.bfloat16))
    grad_wout = jnp.einsum("rc,rd->cd", context, grad_branch, preferred_element_type=jnp.float32)
    grad_context = jnp.einsum(
        "rd,cd->rc", grad_branch, weight_out, preferred_element_type=jnp.float32
    ).astype(jnp.bfloat16)
    head_shape = (across.shape[0] // length, length, projected.shape[2] // HEAD_DIM, HEAD_DIM)
    heads_view = projected.reshape((3,) + head_shape)
    grad_query, grad_keys, grad_values = attend_back(
        heads_view[0],
        heads_view[1],
        heads_view[2],
        visible,
        totals,
        grad_context.reshape(head_shape),
    )
    grad_projected = jnp.stack((grad_query, grad_keys, grad_values)).reshape(projected.shape)
    grad_wqkv = jnp.einsum(
        "rd,trc->tdc", across, grad_projected, preferred_element_type=jnp.float32
    )

    def project_term(offset, number):
        return jnp.einsum(
            "trc,tdc->rd", grad_projected, weight_qkv, preferred_element_type=jnp.float32
        )

    grad_normed = transfer[7](project_term, row_count)
    pull_one = jax.vjp(norm_rows, inputs, gain_one)[1]
    back_input, grad_gain_one = pull_one(grad_normed)
    return (
        grad_hidden + back_input,
        (grad_gain_one, grad_wqkv, grad_wout, grad_gain_two, grad_upw, grad_down),
    )


def learn_local(local_keep, outputs, gain, weight):
    images_here = local_keep.shape[0]
    normed = norm_rows(outputs, gain).reshape(images_here, P_SIZE, outputs.shape[1])
    logits = jnp.einsum("ipd,ds->ips", normed, weight, precision=highest)
    logits = jnp.where(local_keep[:, :, None], logits, -1e30)
    shares = jax.nn.softmax(logits, axis=1)
    tokens = jnp.einsum(
        "ips,ipd->isd",
        shares,
        outputs.reshape(images_here, P_SIZE, outputs.shape[1]),
        precision=highest,
    )
    return tokens.reshape(images_here * S, outputs.shape[1])


def local(
    inputs,
    patch_keep,
    patch_gainone,
    patch_project,
    patch_outproj,
    patch_gaintwo,
    patch_upward,
    patch_downward,
    learner_gain,
    learner_weight,
    token_gainone,
    token_project,
    token_outproj,
    token_gaintwo,
    token_upward,
    token_downward,
    output_grad,
):
    shards = lax.axis_size("mp")
    images_here = patch_keep.shape[0] // shards
    local_keep = (
        lax.dynamic_slice_in_dim(patch_keep, lax.axis_index("mp") * images_here, images_here, 0) > 0
    )
    lower_params = (
        patch_gainone,
        patch_project,
        patch_outproj,
        patch_gaintwo,
        patch_upward,
        patch_downward,
    )
    upper_params = (
        token_gainone,
        token_project,
        token_outproj,
        token_gaintwo,
        token_upward,
        token_downward,
    )
    transfer = (
        lambda tensor: lax.all_gather(tensor, "mp", axis=0, tiled=True),
        lambda producer, row_count: lax.psum_scatter(
            producer(jnp.int32(0), lax.axis_size("mp") * row_count).astype(jnp.bfloat16),
            "mp",
            scatter_dimension=0,
            tiled=True,
        ).astype(jnp.float32),
        lambda tensor: lax.all_gather(tensor, "mp", axis=0, tiled=True),
        lambda producer, row_count: lax.psum_scatter(
            producer(jnp.int32(0), lax.axis_size("mp") * row_count).astype(jnp.bfloat16),
            "mp",
            scatter_dimension=0,
            tiled=True,
        ).astype(jnp.float32),
        lambda tensor: lax.all_gather(tensor, "mp", axis=0, tiled=True),
        lambda producer, row_count: lax.psum_scatter(
            producer(jnp.int32(0), lax.axis_size("mp") * row_count).astype(jnp.bfloat16),
            "mp",
            scatter_dimension=0,
            tiled=True,
        ).astype(jnp.float32),
        lambda tensor: lax.all_gather(tensor, "mp", axis=0, tiled=True),
        lambda producer, row_count: lax.psum_scatter(
            producer(jnp.int32(0), lax.axis_size("mp") * row_count).astype(jnp.bfloat16),
            "mp",
            scatter_dimension=0,
            tiled=True,
        ).astype(jnp.float32),
    )
    lower_visible = patch_keep > 0
    upper_visible = jnp.ones((patch_keep.shape[0], S), jnp.bool_)
    lower_ready = lower_params
    patched, lower_stored = forward(inputs, lower_ready, lower_visible, P_SIZE, transfer)
    tokens, learn_pull = jax.vjp(
        partial(learn_local, local_keep), patched, learner_gain, learner_weight
    )
    token_output, upper_stored = forward(tokens, upper_params, upper_visible, S, transfer)
    token_grad, upper_grads = backward(
        output_grad, upper_stored, upper_params, upper_visible, S, transfer
    )
    patched_grad, learner_gain_grad, learner_weight_grad = learn_pull(token_grad)
    lower_ready = lower_params
    patched_again, lower_stored = forward(inputs, lower_ready, lower_visible, P_SIZE, transfer)
    input_grad, lower_grads = backward(
        patched_grad, lower_stored, lower_ready, lower_visible, P_SIZE, transfer
    )
    matrices = (
        lower_grads[1],
        lower_grads[2],
        lower_grads[4],
        lower_grads[5],
        upper_grads[1],
        upper_grads[2],
        upper_grads[4],
        upper_grads[5],
    )
    matrices = (
        lax.psum(matrices[0].astype(jnp.bfloat16), "dp").astype(jnp.float32),
        lax.psum(matrices[1].astype(jnp.bfloat16), "dp").astype(jnp.float32),
        lax.psum(matrices[2].astype(jnp.bfloat16), "dp").astype(jnp.float32),
        lax.psum(matrices[3].astype(jnp.bfloat16), "dp").astype(jnp.float32),
        lax.psum(matrices[4].astype(jnp.bfloat16), "dp").astype(jnp.float32),
        lax.psum(matrices[5].astype(jnp.bfloat16), "dp").astype(jnp.float32),
        lax.psum(matrices[6].astype(jnp.bfloat16), "dp").astype(jnp.float32),
        lax.psum(matrices[7].astype(jnp.bfloat16), "dp").astype(jnp.float32),
    )
    smalls = lax.psum(
        (
            lower_grads[0],
            lower_grads[3],
            learner_gain_grad,
            learner_weight_grad,
            upper_grads[0],
            upper_grads[3],
        ),
        ("dp", "mp"),
    )
    return (
        token_output,
        input_grad,
        smalls[0],
        matrices[0],
        matrices[1],
        smalls[1],
        matrices[2],
        matrices[3],
        smalls[2],
        smalls[3],
        smalls[4],
        matrices[4],
        matrices[5],
        smalls[5],
        matrices[6],
        matrices[7],
    )


def solution(mesh):
    in_specs = (
        P(("dp", "mp"), None),
        P("dp", None),
        P(),
        P(None, None, "mp"),
        P("mp", None),
        P(),
        P(None, "mp"),
        P("mp", None),
        P(),
        P(),
        P(),
        P(None, None, "mp"),
        P("mp", None),
        P(),
        P(None, "mp"),
        P("mp", None),
        P(("dp", "mp"), None),
    )
    out_specs = (
        P(("dp", "mp"), None),
        P(("dp", "mp"), None),
        P(),
        P(None, None, "mp"),
        P("mp", None),
        P(),
        P(None, "mp"),
        P("mp", None),
        P(),
        P(),
        P(),
        P(None, None, "mp"),
        P("mp", None),
        P(),
        P(None, "mp"),
        P("mp", None),
    )
    return jax.shard_map(local, mesh=mesh, in_specs=in_specs, out_specs=out_specs, check_vma=False)
```

profile of v0, /device:TPU:0, one launch (start us, length us, event | category | flops | bytes accessed | tf_op | source)
XLA Modules:
  0.0 1795.9 jit_solution(2121201470391023016)
XLA Ops:
  18.0 19.7 %all-gather.5.cloned.1.call-done = bf16[3136,1024]{1,0:T(8,128)(2,1)} async-done(((bf16[1568,1024]{1,0:T(8,128)(2,1)}), bf16[3136,1024]{1,0:T(8,128)(2,1)}) %all-gather.5.cloned.1.call-update) | async-done | bytes 6422544 | tf_op jit(solution)/shard_map/all_gather | solution.py:213
  37.7 12.3 convert_bitcast_fusion
  53.9 9.0 reshape.303
  62.8 8.5 copy.61
  71.3 9.0 reshape.304
  80.2 8.5 copy.62
  88.7 14.1 fusion.6
  102.8 9.8 exponential_reduce_fusion
  112.6 9.0 reshape.302
  121.6 8.5 copy.63
  130.1 13.2 convert_bitcast_fusion.2
  148.0 8.9 convert_element_type.238
  156.8 8.5 convolution_convert_fusion
  165.4 15.9 reduce-scatter.9.cloned.1.call-done
  191.5 18.2 %all-gather.7.cloned.1.call-done = bf16[3136,1024]{1,0:T(8,128)(2,1)} async-done(((bf16[1568,1024]{1,0:T(8,128)(2,1)}), bf16[3136,1024]{1,0:T(8,128)(2,1)}) %all-gather.7.cloned.1.call-update) | async-done | bytes 6422544 | tf_op jit(solution)/shard_map/all_gather | solution.py:220
  209.7 71.1 %multiply_convert_fusion.1 = (bf16[3136,2048]{1,0:T(8,128)(2,1)S(1)}, f32[3136,2048]{1,0:T(8,128)}, f32[3136,2048]{1,0:T(8,128)}) fusion(bf16[3136,1024]{1,0:T(8,128)(2,1)} %all-gather.7.cloned.1.call-done, bf16[1024,2048]{1,0:T(8,128)(2,1)} %param.23), kind=kOutput, calls=%fused_computation.8 | convolution fusion | flops 13570801664 | bytes 74842112 | tf_op jit(solution)/shard_map/dot_general | solution.py:96
  285.4 15.3 convolution_convert_fusion.2
  301.4 15.3 reduce-scatter.11.cloned.1.call-done
  415.8 8.7 reduce-scatter.15.cloned.1.call-done
  460.1 8.9 reduce-scatter.19.cloned.1.call-done
  516.8 9.2 fusion.87
  531.2 18.2 %all-gather.9.cloned.1.call-done = bf16[3136,1024]{1,0:T(8,128)(2,1)} async-done(((bf16[1568,1024]{1,0:T(8,128)(2,1)}), bf16[3136,1024]{1,0:T(8,128)(2,1)}) %all-gather.9.cloned.1.call-update) | async-done | bytes 6422544 | tf_op jit(solution)/shard_map/all_gather | solution.py:227
  549.5 34.3 %add_convert_fusion = bf16[3136,2048]{1,0:T(8,128)(2,1)} fusion(f32[3136,2048]{1,0:T(8,128)} %get-tuple-element.85, f32[3136,2048]{1,0:T(8,128)} %get-tuple-element.97, bf16[3136,1024]{1,0:T(8,128)(2,1)} %all-gather.9.cloned.1.call-done, bf16[2048,1024]{1,0:T(8,128)(2,1)} %param.24), kind=kOutput, calls=%fused_computation.7 | convolution fusion | flops 13243252736 | bytes 74842112 | tf_op jit(solution)/shard_map/rd,fd->rf/dot_general | solution.py:112
  583.8 18.9 %convolution_convert_fusion.1 = bf16[3136,1024]{1,0:T(8,128)(2,1)} fusion(bf16[3136,2048]{1,0:T(8,128)(2,1)} %add_convert_fusion, bf16[1024,2048]{1,0:T(8,128)(2,1)} %param.23), kind=kOutput, calls=%fused_computation.40 | convolution fusion | flops 13156548608 | bytes 23461888 | tf_op jit(solution)/shard_map/rf,df->rd/dot_general | solution.py:117
  603.2 15.5 reduce-scatter.21.cloned.1.call-done
  630.4 8.2 fusion.86
  638.7 18.2 %all-gather.11.cloned.1.call-done = bf16[3136,1024]{1,0:T(8,128)(2,1)} async-done(((bf16[1568,1024]{1,0:T(8,128)(2,1)}), bf16[3136,1024]{1,0:T(8,128)(2,1)}) %all-gather.11.cloned.1.call-update) | async-done | bytes 6422544 | tf_op jit(solution)/shard_map/all_gather | solution.py:234
  657.0 8.3 convolution_convert_fusion.3
  665.3 9.1 reshape.305
  674.4 8.5 copy.81
  682.9 14.7 convert_bitcast_fusion.1
  697.6 24.5 %multiply_reduce_fusion = (f32[16,8,196]{2,1,0:T(8,128)S(1)}, f32[16,8,196,196]{2,3,1,0:T(8,128)}) fusion(f32[16,8,196,196]{2,3,1,0:T(8,128)} %get-tuple-element.96, f32[16,8,196]{2,1,0:T(8,128)S(1)} %copy-done.34, pred[16,196]{1,0:T(8,128)(4,1)S(1)} %copy-done.42, bf16[16,196,8,64]{1,3,2,0:T(8,128)(2,1)} %copy.81, bf16[16,196,8,64]{1,3,2,0:T(8,128)(2,1)} %copy.63), kind=kOutput, calls=%fused_computation.2 | convolution fusion | flops 653968896 | bytes 45964352 | tf_op jit(solution)/shard_map/bqhe,bkhe->bhqk/dot_general | solution.py:55
  722.1 22.5 %multiply_convert_fusion = bf16[16,8,196,196]{2,3,1,0:T(8,128)(2,1)} fusion(f32[16,8,196,196]{2,3,1,0:T(8,128)} %get-tuple-element.109, f32[16,8,196,196]{2,3,1,0:T(8,128)} %get-tuple-element.96, f32[16,8,196]{2,1,0:T(8,128)S(1)} %get-tuple-element.108, f32[16,8,196]{2,1,0:T(8,128)S(1)} %copy-done.34, pred[16,196]{1,0:T(8,128)(4,1)S(1)} %copy-done.42), kind=kLoop, calls=%fused_computation.1 | loop fusion | flops 29503488 | bytes 49376320 | tf_op jit(solution)/shard_map/convert_element_type | solution.py:59
  744.6 14.9 fusion.20
  759.5 10.7 fusion.19
  770.2 8.4 copy.107
  778.6 9.6 reshape.301
  788.2 8.4 copy.106
  796.6 9.4 reshape.300
  806.0 8.4 copy.105
  814.4 9.4 reshape.299
  831.6 12.0 bitcast_convert_fusion
  856.7 18.9 %convolution_convert_fusion.4 = bf16[1024,2048]{1,0:T(8,128)(2,1)} fusion(bf16[3136,1024]{1,0:T(8,128)(2,1)S(1)} %bitcast.161, bf16[3136,2048]{1,0:T(8,128)(2,1)} %add_convert_fusion), kind=kOutput, calls=%fused_computation.67 | convolution fusion | flops 13155434496 | bytes 23461888 | tf_op jit(solution)/shard_map/rd,rf->df/dot_general | solution.py:114
  875.6 18.0 %convolution_convert_fusion.5 = bf16[2048,1024]{1,0:T(8,128)(2,1)} fusion(bf16[3136,2048]{1,0:T(8,128)(2,1)} %copy-done.91, bf16[3136,1024]{1,0:T(8,128)(2,1)S(1)} %bitcast.163), kind=kOutput, calls=%fused_computation.68 | convolution fusion | flops 13155434496 | bytes 23461888 | tf_op jit(solution)/shard_map/rf,rd->fd/dot_general | solution.py:111
  898.4 12.5 convert_bitcast_fusion.4
  929.4 45.9 %all-reduce = (f32[1024]{0:T(1024)}, f32[1024]{0:T(1024)}, f32[1024]{0:T(1024)}, f32[1024,8]{0,1:T(8,128)}, f32[1024]{0:T(1024)}, /*index=5*/f32[1024]{0:T(1024)}) all-reduce(f32[1024]{0:T(1024)S(1)} %get-tuple-element.52, f32[1024]{0:T(1024)S(1)} %copy-done.82, ...), channel_id=1, replica_groups=mesh['dp'=16,'mp'=2] {'dp','mp'}, use_global_device_ids=true, to_apply=%region_38.39 | all-reduce | flops 13312 | bytes 106496 | tf_op jit(solution)/shard_map/psum | solution.py:279
  975.3 9.0 add_add_fusion.3
  984.3 768.4 %all-reduce.4.cloned.1.call-done = (bf16[3,1024,512]{1,2,0:T(8,128)(2,1)}, bf16[3,1024,512]{1,2,0:T(8,128)(2,1)}, bf16[512,1024]{1,0:T(8,128)(2,1)}, bf16[1024,2...) async-done(((bf16[3,1024,512]{1,2,0:T(8,128)(2,1)}, ...) | async-done | bytes 25165840 | tf_op jit(solution)/shard_map/psum | solution.py:270
  (372 shorter events, 314.4 us)
Async XLA Ops:
  7.2 30.6 %copy-start = (bf16[3,1024,512]{2,1,0:T(8,128)(2,1)S(1)}, bf16[3,1024,512]{2,1,0:T(8,128)(2,1)}, u32[]{:S(2)}) copy-start(bf16[3,1024,512]{2,1,0:T(8,128)(2,1)} %param.20) | copy-start | bytes 9437188
  7.2 8.4 copy-start.68
  7.2 30.5 %all-gather.5.cloned.1.call-start = ((), (), s32[]{:S(2)}) async-start(), calls=%async_computation.8 | async-start | bytes 9633792 | tf_op jit(solution)/shard_map/all_gather | solution.py:213
  17.9 163.4 %reduce-scatter.9.cloned.1.call-start = ((), (), s32[]{:S(2)}) async-start(), calls=%async_computation.9 | async-start | bytes 9633792 | tf_op jit(solution)/shard_map/reduce_scatter | solution.py:214
  18.0 112.1 %copy-start.41 = (pred[16,196]{1,0:T(8,128)(4,1)}, pred[16,196]{1,0:T(8,128)(4,1)S(1)}, u32[]{:S(2)}) copy-start(pred[16,196]{1,0:T(8,128)(4,1)S(1)} %broadcast_compare_fusion) | copy-start | bytes 9412
  112.6 17.5 copy-start.33
  165.4 44.4 %all-gather.7.cloned.1.call-start = ((), (), s32[]{:S(2)}) async-start(), calls=%async_computation.10 | async-start | bytes 9633792 | tf_op jit(solution)/shard_map/all_gather | solution.py:220
  191.4 125.3 %reduce-scatter.11.cloned.1.call-start = ((), (), s32[]{:S(2)}) async-start(), calls=%async_computation.11 | async-start | bytes 9633792 | tf_op jit(solution)/shard_map/reduce_scatter | solution.py:221
  209.7 75.7 %copy-start.90 = (bf16[2048,1024]{1,0:T(8,128)(2,1)S(1)}, bf16[2048,1024]{1,0:T(8,128)(2,1)}, u32[]{:S(2)}) copy-start(bf16[2048,1024]{1,0:T(8,128)(2,1)} %param.24) | copy-start | bytes 12582916
  300.7 86.8 %reduce-scatter.13.cloned.1.call-start = ((), (), s32[]{:S(2)}) async-start(), calls=%async_computation.12 | async-start | bytes 393216 | tf_op jit(solution)/shard_map/reduce_scatter | solution.py:214
  301.4 43.1 %copy-start.76 = (pred[8,196]{1,0:T(8,128)(4,1)}, pred[8,196]{1,0:T(8,128)(4,1)S(1)}, u32[]{:S(2)}) copy-start(pred[8,196]{1,0:T(8,128)(4,1)S(1)} %dynamic-slice_compare_fusion) | copy-start | bytes 4708
  344.6 13.8 copy-start.65
  352.3 143.6 %copy-start.21 = (f32[8,196,8]{1,2,0:T(8,128)}, f32[8,196,8]{1,2,0:T(8,128)S(1)}, u32[]{:S(2)}) copy-start(f32[8,196,8]{1,2,0:T(8,128)S(1)} %get-tuple-element.99) | copy-start | bytes 150532
  352.3 143.7 %copy-start.47 = (f32[8,8]{1,0:T(8,128)}, f32[8,8]{1,0:T(8,128)S(1)}, u32[]{:S(2)}) copy-start(f32[8,8]{1,0:T(8,128)S(1)} %get-tuple-element.98) | copy-start | bytes 772
  352.5 143.5 %copy-start.49 = (f32[8,8]{1,0:T(8,128)}, f32[8,8]{1,0:T(8,128)S(1)}, u32[]{:S(2)}) copy-start(f32[8,8]{1,0:T(8,128)S(1)} %fusion.65) | copy-start | bytes 772
  358.0 11.3 copy-start.83
  358.3 11.0 copy-start.89
  358.3 11.0 copy-start.85
  378.6 34.3 %reduce-scatter.17.cloned.1.call-start = ((), (), s32[]{:S(2)}) async-start(), calls=%async_computation.14 | async-start | bytes 393216 | tf_op jit(solution)/shard_map/reduce_scatter | solution.py:228
  403.9 20.6 %reduce-scatter.15.cloned.1.call-start = ((), (), s32[]{:S(2)}) async-start(), calls=%async_computation.13 | async-start | bytes 393216 | tf_op jit(solution)/shard_map/reduce_scatter | solution.py:221
  410.1 58.9 %reduce-scatter.19.cloned.1.call-start = ((), (), s32[]{:S(2)}) async-start(), calls=%async_computation.15 | async-start | bytes 393216 | tf_op jit(solution)/shard_map/reduce_scatter | solution.py:235
  460.0 89.4 %all-gather.9.cloned.1.call-start = ((), (), s32[]{:S(2)}) async-start(), calls=%async_computation.16 | async-start | bytes 9633792 | tf_op jit(solution)/shard_map/all_gather | solution.py:227
  488.1 8.4 copy-start.52
  488.2 8.4 copy-start.77
  496.0 14.3 copy-start.74
  510.3 15.7 slice-start.2
  516.8 9.2 slice-start.3
  531.2 87.5 %reduce-scatter.21.cloned.1.call-start = ((), (), s32[]{:S(2)}) async-start(), calls=%async_computation.17 | async-start | bytes 9633792 | tf_op jit(solution)/shard_map/reduce_scatter | solution.py:228
  602.7 16.0 copy-start.46
  602.7 16.0 copy-start.67
  602.7 21.2 %copy-start.62 = (f32[1568]{0:T(1024)S(1)}, f32[1568]{0:T(1024)}, u32[]{:S(2)}) copy-start(f32[1568]{0:T(1024)} %copy-done.61) | copy-start | bytes 18820
  602.7 21.2 %copy-start.58 = (f32[1568]{0:T(1024)S(1)}, f32[1568]{0:T(1024)}, u32[]{:S(2)}) copy-start(f32[1568]{0:T(1024)} %copy-done.57) | copy-start | bytes 18820
  602.7 54.2 %all-gather.11.cloned.1.call-start = ((), (), s32[]{:S(2)}) async-start(), calls=%async_computation.18 | async-start | bytes 9633792 | tf_op jit(solution)/shard_map/all_gather | solution.py:234
  618.7 11.8 slice-start
  638.7 279.3 %reduce-scatter.23.cloned.1.call-start = ((), (), s32[]{:S(2)}) async-start(), calls=%async_computation.19 | async-start | bytes 9633792 | tf_op jit(solution)/shard_map/reduce_scatter | solution.py:235
  674.4 8.5 copy-start.34
  674.4 8.5 copy-start.42
  843.7 909.0 %all-reduce.4.cloned.1.call-start = ((), (), s32[]{:S(2)}) async-start(), calls=%async_computation.20 | async-start | bytes 50331648 | tf_op jit(solution)/shard_map/psum | solution.py:270
  844.6 12.1 slice-start.9
  852.5 23.0 %slice-start.11 = ((s8[6422528]{0:T(1024)(128)(4,1)}), s8[4194304]{0:T(1024)(128)(4,1)S(1)}, s32[]{:S(2)}) async-start(s8[6422528]{0:T(1024)(128)(4,1)} %bitcast.162), calls=%async_computation.32 | async-start | bytes 8388608
  856.7 18.9 %slice-start.12 = ((s8[6422528]{0:T(1024)(128)(4,1)}), s8[2228224]{0:T(1024)(128)(4,1)S(1)}, s32[]{:S(2)}) async-start(s8[6422528]{0:T(1024)(128)(4,1)} %bitcast.162), calls=%async_computation.33 | async-start | bytes 4456448
  856.7 37.0 %slice-start.13 = ((s8[6422528]{0:T(1024)(128)(4,1)}), s8[4194304]{0:T(1024)(128)(4,1)S(1)}, s32[]{:S(2)}) async-start(s8[6422528]{0:T(1024)(128)(4,1)} %bitcast.164), calls=%async_computation.34 | async-start | bytes 8388608
  856.7 41.6 %slice-start.7 = ((s8[6422528]{0:T(1024)(128)(4,1)}), s8[4194304]{0:T(1024)(128)(4,1)S(1)}, s32[]{:S(2)}) async-start(s8[6422528]{0:T(1024)(128)(4,1)} %bitcast.158), calls=%async_computation.28 | async-start | bytes 8388608
  875.6 18.1 %copy-start.20 = (bf16[3136,512]{0,1:T(8,128)(2,1)S(1)}, bf16[3136,512]{0,1:T(8,128)(2,1)}, u32[]{:S(2)}) copy-start(bf16[3136,512]{0,1:T(8,128)(2,1)} %convert_element_type.238) | copy-start | bytes 9633796
  875.6 18.1 %slice-start.14 = ((s8[6422528]{0:T(1024)(128)(4,1)}), s8[2228224]{0:T(1024)(128)(4,1)S(1)}, s32[]{:S(2)}) async-start(s8[6422528]{0:T(1024)(128)(4,1)} %bitcast.164), calls=%async_computation.35 | async-start | bytes 4456448
  875.6 22.7 %slice-start.4 = ((s8[9633792]{0:T(1024)(128)(4,1)}), s8[4194304]{0:T(1024)(128)(4,1)S(1)}, s32[]{:S(2)}) async-start(s8[9633792]{0:T(1024)(128)(4,1)} %bitcast.156), calls=%async_computation.25 | async-start | bytes 8388608
  875.6 22.7 %slice-start.5 = ((s8[9633792]{0:T(1024)(128)(4,1)}), s8[4194304]{0:T(1024)(128)(4,1)S(1)}, s32[]{:S(2)}) async-start(s8[9633792]{0:T(1024)(128)(4,1)} %bitcast.156), calls=%async_computation.26 | async-start | bytes 8388608
  875.6 22.7 %slice-start.8 = ((s8[6422528]{0:T(1024)(128)(4,1)}), s8[2228224]{0:T(1024)(128)(4,1)S(1)}, s32[]{:S(2)}) async-start(s8[6422528]{0:T(1024)(128)(4,1)} %bitcast.158), calls=%async_computation.29 | async-start | bytes 4456448
  (72 other events, 244.9 us)
Sparse Core Ops, SparseCore 0:
  18.0 19.6 all-gather.4
  165.5 15.8 reduce-scatter.8
  191.5 18.1 all-gather.6
  300.9 15.8 reduce-scatter.10
  378.7 8.8 reduce-scatter.12
  404.0 8.8 reduce-scatter.16
  415.7 8.8 reduce-scatter.14
  460.2 8.7 reduce-scatter.18
  531.3 18.1 all-gather.8
  602.8 15.8 reduce-scatter.20
  638.8 18.1 all-gather.10
  843.8 15.8 reduce-scatter.22
  911.1 841.6 all-reduce.3
where the time goes:
time: 1810 us; the launch traced here: 1800 us
  waiting for transfers between devices  916 us (51%)
  matrix products  415 us (23%)
  local copies, waits for them, and re-layouts  227 us (13%)
  other arithmetic  167 us (9%)
  blocking collectives  54 us (3%)
    psum x1, waiting for transfers between devices, local(): lax.psum(matrices[0].astype(jnp.bfloat16), 'dp').astype(jnp.float32)  768 us
    all_gather x4, waiting for transfers between devices, local(): lax.all_gather(tensor, 'mp', axis=0, tiled=True)  74.4 us
    dot_general x2, matrix products, forward(): upward = jnp.dot(second, weight_up, preferred_element_type=jnp.float32)  74 us
    reduce_scatter x8, waiting for transfers between devices, local(): lax.psum_scatter(producer(jnp.int32(0), lax.axis_size('mp') * row_count)....  72.9 us
    another operation x11, local copies, waits for them, and re-layouts, backward(): jnp.stack((grad_query, grad_keys, grad_values)).reshape(projected.shape)  60.2 us
    psum x1, blocking collectives, local(): lax.psum((lower_grads[0], lower_grads[3], learner_gain_grad, learner_weig...  45.9 us
    unnamed x220, local copies, waits for them, and re-layouts  40 us
    dot_general x2, matrix products, backward(): jnp.einsum('rd,fd->rf', grad_mix, weight_down, preferred_element_type=jnp...  39.2 us
  transfers between devices with their start and end apart: 13, of which 12 were waited for; matrix products, arithmetic and copies ran while one was open for 6% of the time, Pallas kernels for 0%

commit v1 on v0

v1 whole, which is shorter than its diff:
```python
import math
from functools import partial

import jax
import jax.numpy as jnp
from jax import lax
from jax.experimental import pallas as pl
from jax.experimental.pallas import tpu as pltpu
from jax.sharding import PartitionSpec as P

HEAD_DIM = 64
P_SIZE = 196
S = 8


epsilon = 1e-06
highest = lax.Precision.HIGHEST


WINDOW = 208


def key_bias(keep):
    pieces = []
    for place in range(keep.shape[0]):
        offset = place * P_SIZE % 16
        row = jnp.where(keep[place], 0.0, -1e30).astype(jnp.float32)
        pieces.append(jnp.pad(row, (offset, WINDOW - P_SIZE - offset), constant_values=-1e30))
    return jnp.stack(pieces)[:, :, None]


def nt(left, right):
    return lax.dot_general(
        left, right, (((1,), (1,)), ((), ())), preferred_element_type=jnp.float32
    )


def mm(left, right):
    return jnp.dot(left, right, preferred_element_type=jnp.float32)


def only(head, tensor):
    lane = lax.broadcasted_iota(jnp.int32, tensor.shape, 1)
    return jnp.where((lane < HEAD_DIM) == (head == 0), tensor, jnp.zeros_like(tensor))


def pick(pair):
    lane = lax.broadcasted_iota(jnp.int32, pair[0].shape, 1)
    return jnp.where(lane < HEAD_DIM, pair[0], pair[1])


def mix(query, keys, values, bias):
    turned = values.T
    pieces = []
    for head in range(2):
        scores = nt(only(head, keys), query) + bias
        weights = jnp.exp(scores - jnp.max(scores, axis=0, keepdims=True))
        total = jnp.sum(weights, axis=0, keepdims=True)
        mixed = mm(turned[head * HEAD_DIM : (head + 1) * HEAD_DIM], weights.astype(jnp.bfloat16))
        pieces.append(mixed * (1.0 / total))
    return jnp.concatenate(pieces, axis=0).T.astype(jnp.bfloat16)


def mix_back(query, keys, values, grad, bias):
    turned = keys.T
    by_query, by_key, by_value = [], [], []
    for head in range(2):
        scores = nt(only(head, keys), query) + bias
        weights = jnp.exp(scores - jnp.max(scores, axis=0, keepdims=True))
        total = jnp.sum(weights, axis=0, keepdims=True)
        shares = weights * (1.0 / total)
        product = shares * nt(only(head, values), grad)
        inner = jnp.sum(product, axis=0, keepdims=True)
        grad_scores = (product - shares * inner).astype(jnp.bfloat16)
        by_value.append(mm(shares.astype(jnp.bfloat16), grad))
        by_key.append(mm(grad_scores, query))
        by_query.append(mm(turned[head * HEAD_DIM : (head + 1) * HEAD_DIM], grad_scores))
    grad_query = jnp.concatenate(by_query, axis=0).T * HEAD_DIM**-0.5
    return tuple(value.astype(jnp.bfloat16) for value in (grad_query, pick(by_key), pick(by_value)))


def scaled(query):
    return query * jnp.bfloat16(HEAD_DIM**-0.5)


def window_of(place):
    first = place * P_SIZE
    start = first // 16 * 16
    row = lax.broadcasted_iota(jnp.int32, (WINDOW, 2 * HEAD_DIM), 0)
    offset = first - start
    return pl.ds(start, WINDOW), (row >= offset) & (row < offset + P_SIZE)


def attend_kernel(images, bias_ref, qkv_ref, out_ref):
    for place in range(images):
        window, inside = window_of(place)
        mixed = mix(
            scaled(qkv_ref[0, window, :]),
            qkv_ref[1, window, :],
            qkv_ref[2, window, :],
            bias_ref[place],
        )
        out_ref[window, :] = jnp.where(inside, mixed, out_ref[window, :])


def attend_back_kernel(images, bias_ref, qkv_ref, grad_ref, out_ref):
    for place in range(images):
        window, inside = window_of(place)
        grad = grad_ref[window, :]
        parts = mix_back(
            scaled(qkv_ref[0, window, :]),
            qkv_ref[1, window, :],
            qkv_ref[2, window, :],
            jnp.where(inside, grad, jnp.zeros_like(grad)),
            bias_ref[place],
        )
        for at, value in enumerate(parts):
            out_ref[at, window, :] = jnp.where(inside, value, out_ref[at, window, :])


def attention(kernel, bias, projected, grads, panel, panels):
    rows, columns = projected.shape[1:]
    spare = -rows % 16
    if spare:
        projected = jnp.pad(projected, ((0, 0), (0, spare), (0, 0)))
        grads = [jnp.pad(grad, ((0, spare), (0, 0))) for grad in grads]
    wide, columns = 2 * HEAD_DIM, columns // panels
    pairs = columns // wide
    first = panel * pairs
    rows += spare
    plane = pl.BlockSpec((rows, wide), lambda pair: (0, pair))
    triple = pl.BlockSpec((3, rows, wide), lambda pair: (0, 0, pair))
    shape = (rows, columns)
    out = pl.pallas_call(
        kernel,
        grid=(pairs,),
        in_specs=[
            pl.BlockSpec(bias.shape, lambda pair: (0,) * bias.ndim),
            pl.BlockSpec((3, rows, wide), lambda pair: (0, 0, first + pair)),
        ]
        + [pl.BlockSpec((rows, wide), lambda pair: (0, first + pair))] * len(grads),
        out_specs=triple if grads else plane,
        out_shape=jax.ShapeDtypeStruct((3,) + shape if grads else shape, jnp.bfloat16),
        compiler_params=params(14),
        cost_estimate=light(),
        name="attend_back" if grads else "attend",
    )(bias, projected, *grads)
    return out[..., : rows - spare, :] if spare else out


def attend(bias, projected):
    return attention(partial(attend_kernel, bias.shape[0]), bias, projected, [], 0, 1)


def attend_back(bias, projected, grad_context, panel, panels):
    kernel = partial(attend_back_kernel, bias.shape[0])
    return attention(kernel, bias, projected, [grad_context], panel, panels)


def tn(left, right):
    return lax.dot_general(
        left, right, (((0,), (0,)), ((), ())), preferred_element_type=jnp.float32
    )


def row_mean(matrix):
    width = matrix.shape[1]
    folded = matrix[:, :128]
    for at in range(128, width, 128):
        folded = folded + matrix[:, at : at + 128]
    return jnp.sum(folded, axis=-1, keepdims=True) * (1.0 / width)


def standard(matrix):
    center = matrix - row_mean(matrix)
    spread = row_mean(center * center)
    inverse = lax.rsqrt(spread + epsilon)
    return center * inverse, inverse


def standard_back(grad, normal, inverse, gain):
    scaled_grad = grad * gain
    mean = row_mean(scaled_grad)
    along = row_mean(scaled_grad * normal)
    return (
        inverse * (scaled_grad - mean - normal * along),
        jnp.sum((grad * normal).reshape(-1, 8, grad.shape[1]), axis=0),
    )


def gelu_pair(upward):
    bell = jnp.exp(upward * upward * -0.5)
    base = 1.0 + jnp.abs(upward) * (0.3275911 * 0.5**0.5)
    ratio = pl.reciprocal(base, approx=True)
    ratio = ratio * (2.0 - base * ratio)
    series = 0.5 * 1.061405429
    for factor in (-1.453152027, 1.421413741, -0.284496736, 0.254829592):
        series = series * ratio + 0.5 * factor
    tail = series * ratio * bell
    below = jnp.where(upward < 0.0, tail, 1.0 - tail)
    slope = below + upward * bell * (0.5 / math.pi) ** 0.5
    return (upward * below).astype(jnp.bfloat16), slope.astype(jnp.bfloat16)


def spans(rows, most):
    if rows <= most or rows % 16:
        return [(0, rows)]
    parts = -(-rows // most)
    cuts = [rows // 16 * at // parts * 16 for at in range(parts + 1)]
    return list(zip(cuts, cuts[1:]))


def row_block(rows, most):
    for count in range(1, rows + 1):
        if rows % count == 0 and rows // count <= most and rows // count % 16 == 0:
            return rows // count
    return rows


def by_rows(rows, work, step=112):
    size = row_block(rows, 128)

    def run(first):
        for at in range(0, size, step):
            start = first + at
            if not isinstance(start, int):
                start = pl.multiple_of(start, 16)
            work(pl.ds(start, min(step, size - at)))

    if size == rows:
        run(0)
        return

    def one(at, carry):
        run(at * size)
        return carry

    lax.fori_loop(0, rows // size, one, 0)


def light():
    return pl.CostEstimate(flops=1000, bytes_accessed=1000, transcendentals=0)


def params(mebibytes):
    return pltpu.CompilerParams(vmem_limit_bytes=mebibytes * 1024 * 1024)


def eight_spec(width):
    return pl.BlockSpec((8, width), lambda *at: (0, 0))


def whole_spec(array):
    return pl.BlockSpec(array.shape, lambda *at: (0,) * array.ndim)


def norm_kernel(input_ref, gain_ref, out_ref):
    def work(rows):
        normal = standard(input_ref[rows, :])[0]
        out_ref[rows, :] = (normal * gain_ref[...]).astype(jnp.bfloat16)

    by_rows(input_ref.shape[0], work)


def norm(inputs, gain):
    rows, width = inputs.shape
    block = row_block(rows, 400)
    line = pl.BlockSpec((block, width), lambda at: (at, 0))
    gain = gain[None]
    return pl.pallas_call(
        norm_kernel,
        grid=(rows // block,),
        in_specs=[line, whole_spec(gain)],
        out_specs=line,
        out_shape=jax.ShapeDtypeStruct((rows, width), jnp.bfloat16),
        compiler_params=params(8),
        cost_estimate=light(),
        name="norm",
    )(inputs, gain)


def outward_kernel(shares, *refs):
    context_refs, weight_refs = refs[:shares], refs[shares : 2 * shares]
    input_ref, gain_ref, hidden_ref, second_ref = refs[2 * shares :]
    total = input_ref[...]
    for context_ref, weight_ref in zip(context_refs, weight_refs):
        total = total + mm(context_ref[...], weight_ref[...])
    hidden_ref[...] = total

    def work(rows):
        normal = standard(hidden_ref[rows, :])[0]
        second_ref[rows, :] = (normal * gain_ref[...]).astype(jnp.bfloat16)

    by_rows(input_ref.shape[0], work)


def outward(contexts, weights, inputs, gain):
    rows, width = inputs.shape
    block = row_block(rows, 400)
    line = pl.BlockSpec((block, width), lambda at: (at, 0))
    gain = gain[None]
    heads = contexts[0].shape[1]
    return pl.pallas_call(
        partial(outward_kernel, len(contexts)),
        grid=(rows // block,),
        in_specs=[pl.BlockSpec((block, heads), lambda at: (at, 0))] * len(contexts)
        + [whole_spec(weight) for weight in weights]
        + [line, whole_spec(gain)],
        out_specs=[line, line],
        out_shape=[
            jax.ShapeDtypeStruct((rows, width), jnp.float32),
            jax.ShapeDtypeStruct((rows, width), jnp.bfloat16),
        ],
        compiler_params=params(16),
        cost_estimate=light(),
        name="outward",
    )(*contexts, *weights, inputs, gain)


def ff_kernel(shares, per, *refs):
    second_ref, hidden_ref = refs[:2]
    up_refs, down_refs = refs[2 : 2 + shares], refs[2 + shares : 2 + 2 * shares]
    result_ref = refs[2 + 2 * shares]
    active_refs, slope_refs = refs[3 + 2 * shares : 3 + 3 * shares], refs[3 + 3 * shares :]
    chunk = pl.program_id(1)

    @pl.when(chunk == 0)
    def _():
        result_ref[...] = hidden_ref[...]

    for share in range(shares):

        @pl.when((chunk >= share * per) & (chunk < (share + 1) * per))
        def _():
            ranges = spans(second_ref.shape[0], 400)
            up, down = up_refs[share][...], down_refs[share][...]
            ahead = mm(second_ref[ranges[0][0] : ranges[0][1], :], up)
            for at, (start, end) in enumerate(ranges):
                upward = ahead
                if at + 1 < len(ranges):
                    ahead = mm(second_ref[ranges[at + 1][0] : ranges[at + 1][1], :], up)
                active, slope = gelu_pair(upward)
                active_refs[share][start:end, :] = active
                slope_refs[share][start:end, :] = slope
                result_ref[start:end, :] += mm(active, down)


def share_spec(block, place, share, per):
    if place == 1:
        return pl.BlockSpec(block, lambda at, chunk: (0, jnp.clip(chunk - share * per, 0, per - 1)))
    if place == 0:
        return pl.BlockSpec(block, lambda at, chunk: (jnp.clip(chunk - share * per, 0, per - 1), 0))
    return pl.BlockSpec(block, lambda at, chunk: (at, jnp.clip(chunk - share * per, 0, per - 1)))


def ff_sizes(rows, ups, most):
    block = rows // 2 if rows % 32 == 0 and rows > 1024 else rows
    width, units = ups[0].shape
    size = min(most if rows > 128 else 1024, units)
    return block, width, units, size, units // size


def feed(second, hidden, ups, downs):
    rows, shares = second.shape[0], len(ups)
    block, width, units, size, per = ff_sizes(rows, ups, 1024)
    line = pl.BlockSpec((block, width), lambda at, chunk: (at, 0))
    piece = [share_spec((block, size), 2, share, per) for share in range(shares)]
    out = pl.pallas_call(
        partial(ff_kernel, shares, per),
        grid=(rows // block, shares * per),
        in_specs=[line, line]
        + [share_spec((width, size), 1, share, per) for share in range(shares)]
        + [share_spec((size, width), 0, share, per) for share in range(shares)],
        out_specs=[line] + piece + piece,
        out_shape=[jax.ShapeDtypeStruct((rows, width), jnp.float32)]
        + [jax.ShapeDtypeStruct((rows, units), jnp.bfloat16)] * (2 * shares),
        compiler_params=params(56),
        cost_estimate=light(),
        name="feed",
    )(second, hidden, *ups, *downs)
    return out[0], out[1 : 1 + shares], out[1 + shares :]


def ff_back_kernel(shares, per, *refs):
    grad_ref, hidden_ref, gain_ref = refs[:3]
    slope_refs = refs[3 : 3 + shares]
    up_refs, down_refs = refs[3 + shares : 3 + 2 * shares], refs[3 + 2 * shares : 3 + 3 * shares]
    mixed_ref, branch_ref, low_ref, gain_grad_ref = refs[3 + 3 * shares : 7 + 3 * shares]
    inner_refs = refs[7 + 3 * shares :]
    block, chunk = pl.program_id(0), pl.program_id(1)

    @pl.when(chunk == 0)
    def _():
        low_ref[...] = grad_ref[...].astype(jnp.bfloat16)
        mixed_ref[...] = jnp.zeros_like(mixed_ref)

    @pl.when((block == 0) & (chunk == 0))
    def _():
        gain_grad_ref[...] = jnp.zeros_like(gain_grad_ref)

    for share in range(shares):

        @pl.when((chunk >= share * per) & (chunk < (share + 1) * per))
        def _():
            ranges = spans(grad_ref.shape[0], 800)
            up, down = up_refs[share][...], down_refs[share][...]
            ahead = nt(low_ref[ranges[0][0] : ranges[0][1], :], down)
            for at, (start, end) in enumerate(ranges):
                grad_active = ahead
                if at + 1 < len(ranges):
                    ahead = nt(low_ref[ranges[at + 1][0] : ranges[at + 1][1], :], down)
                slope = slope_refs[share][start:end, :].astype(jnp.float32)
                inner = (grad_active * slope).astype(jnp.bfloat16)
                inner_refs[share][start:end, :] = inner
                mixed_ref[start:end, :] += nt(inner, up)

    @pl.when(chunk == shares * per - 1)
    def _():
        def work(rows):
            normal, inverse = standard(hidden_ref[rows, :])
            back, gain_grad = standard_back(mixed_ref[rows, :], normal, inverse, gain_ref[...])
            total = grad_ref[rows, :] + back
            mixed_ref[rows, :] = total
            branch_ref[rows, :] = total.astype(jnp.bfloat16)
            gain_grad_ref[...] += gain_grad

        by_rows(grad_ref.shape[0], work)


def feed_back(grad, hidden, gain, slopes, ups, downs):
    rows, shares = grad.shape[0], len(ups)
    block, width, units, size, per = ff_sizes(rows, ups, 512)
    line = pl.BlockSpec((block, width), lambda at, chunk: (at, 0))
    gain = gain[None]
    piece = [share_spec((block, size), 2, share, per) for share in range(shares)]
    out = pl.pallas_call(
        partial(ff_back_kernel, shares, per),
        grid=(rows // block, shares * per),
        in_specs=[line, line, whole_spec(gain)]
        + piece
        + [share_spec((width, size), 1, share, per) for share in range(shares)]
        + [share_spec((size, width), 0, share, per) for share in range(shares)],
        out_specs=[line, line, line, eight_spec(width)] + piece,
        out_shape=[
            jax.ShapeDtypeStruct((rows, width), jnp.float32),
            jax.ShapeDtypeStruct((rows, width), jnp.bfloat16),
            jax.ShapeDtypeStruct((rows, width), jnp.bfloat16),
            jax.ShapeDtypeStruct((8, width), jnp.float32),
        ]
        + [jax.ShapeDtypeStruct((rows, units), jnp.bfloat16)] * shares,
        compiler_params=params(50),
        cost_estimate=light(),
        name="feed_back",
    )(grad, hidden, gain, *slopes, *ups, *downs)
    return out[0], out[1], out[2], jnp.sum(out[3], axis=0), out[4:]


def split(value):
    high = value.astype(jnp.bfloat16)
    return high, (value - high.astype(jnp.float32)).astype(jnp.bfloat16)


def learn_kernel(bias_ref, input_ref, gain_ref, maps_ref, tokens_ref, shares_ref, high, low_part):
    def work(rows):
        high[rows, :], low_part[rows, :] = split(standard(input_ref[rows, :])[0])

    by_eights(input_ref.shape[0], work)
    maps = jnp.concatenate(split(maps_ref[...] * gain_ref[...]))
    logits = nt(maps, high[...])
    logits = logits[:S] + logits[S:] + nt(maps[:S], low_part[...])
    logits = jnp.concatenate([logits] * (bias_ref.shape[1] // S), axis=0) + bias_ref[0]
    weights = jnp.exp(logits - jnp.max(logits, axis=-1, keepdims=True))
    shares = weights / jnp.sum(weights, axis=-1, keepdims=True)
    shares_ref[0] = shares

    def cut(rows):
        high[rows, :], low_part[rows, :] = split(input_ref[rows, :])

    by_eights(input_ref.shape[0], cut)
    both = jnp.concatenate(split(shares))
    tokens, count = mm(both, high[...]), shares.shape[0]
    tokens_ref[...] = tokens[:count] + tokens[count:] + mm(both[:count], low_part[...])


def by_eights(rows, work):
    for at in range(0, rows, 112):
        work(pl.ds(at, min(112, rows - at)))


def pair_bias(keep):
    step = 4 if keep.shape[0] % 4 == 0 else 2
    seen = keep.reshape(-1, 1, step * P_SIZE)
    own = (jnp.arange(step * S)[:, None] // S) == (jnp.arange(step * P_SIZE)[None] // P_SIZE)
    return jnp.where(seen & own[None], 0.0, -1e30).astype(jnp.float32)


def learn(bias, patched, gain, maps):
    rows, width = patched.shape
    steps, count, span = bias.shape
    gain = gain[None]
    line = pl.BlockSpec((span, width), lambda at: (at, 0))
    mark = pl.BlockSpec((1, count, span), lambda at: (at, 0, 0))
    return pl.pallas_call(
        learn_kernel,
        grid=(steps,),
        in_specs=[mark, line, whole_spec(gain), whole_spec(maps)],
        out_specs=[pl.BlockSpec((count, width), lambda at: (at, 0)), mark],
        out_shape=[
            jax.ShapeDtypeStruct((steps * count, width), jnp.float32),
            jax.ShapeDtypeStruct(bias.shape, jnp.float32),
        ],
        scratch_shapes=[pltpu.VMEM((span, width), jnp.bfloat16)] * 2,
        compiler_params=params(24),
        cost_estimate=light(),
        name="learn",
    )(bias, patched, gain, maps)


def outer(left, right):
    (left_high, left_low), (right_high, right_low) = split(left), split(right)
    return tn(
        jnp.concatenate((left_high, left_high, left_low)),
        jnp.concatenate((right_high, right_low, right_high)),
    )


def learn_back_kernel(
    shares_ref, grad_ref, input_ref, gain_ref, maps_ref,
    out_ref, low_ref, gain_grad_ref, maps_grad_ref, high, low_part, inverses, slope,
):
    @pl.when(pl.program_id(0) == 0)
    def _():
        gain_grad_ref[...] = jnp.zeros_like(gain_grad_ref)
        maps_grad_ref[...] = jnp.zeros_like(maps_grad_ref)

    def cut(rows):
        high[rows, :], low_part[rows, :] = split(input_ref[rows, :])

    by_eights(input_ref.shape[0], cut)
    shares, grad = shares_ref[0], grad_ref[...]
    both = jnp.concatenate(split(grad))
    product, count = nt(both, high[...]), shares.shape[0]
    product = product[:count] + product[count:] + nt(both[:count], low_part[...])
    product = shares * product
    logits = product - shares * jnp.sum(product, axis=-1, keepdims=True)
    logits = sum(logits[at : at + S] for at in range(S, count, S)) + logits[:S]
    slope[...] = outer(logits, maps_ref[...])
    out_ref[...] = outer(shares, grad)

    def before(rows):
        normal, inverse = standard(input_ref[rows, :])
        high[rows, :], low_part[rows, :] = split(normal)
        inverses[rows, :] = jnp.broadcast_to(inverse, inverses[rows, :].shape)

    by_eights(input_ref.shape[0], before)
    both = jnp.concatenate(split(logits))
    maps_grad = mm(both, high[...])
    maps_grad = maps_grad[:S] + maps_grad[S:] + mm(both[:S], low_part[...])
    maps_grad_ref[...] += maps_grad * gain_ref[...]

    def after(rows):
        normal = high[rows, :].astype(jnp.float32) + low_part[rows, :].astype(jnp.float32)
        back, gain_grad = standard_back(
            slope[rows, :], normal, inverses[rows, 0:1], gain_ref[...]
        )
        total = out_ref[rows, :] + back
        out_ref[rows, :] = total
        low_ref[rows, :] = total.astype(jnp.bfloat16)
        gain_grad_ref[...] += gain_grad

    by_eights(input_ref.shape[0], after)


def learn_back(shares, grad, patched, gain, maps):
    rows, width = patched.shape
    steps, count, span = shares.shape
    gain = gain[None]
    line = pl.BlockSpec((span, width), lambda at: (at, 0))
    mark = pl.BlockSpec((1, count, span), lambda at: (at, 0, 0))
    out = pl.pallas_call(
        learn_back_kernel,
        grid=(steps,),
        in_specs=[
            mark,
            pl.BlockSpec((count, width), lambda at: (at, 0)),
            line,
            whole_spec(gain),
            whole_spec(maps),
        ],
        out_specs=[line, line, eight_spec(width), whole_spec(maps)],
        out_shape=[
            jax.ShapeDtypeStruct((rows, width), jnp.float32),
            jax.ShapeDtypeStruct((rows, width), jnp.bfloat16),
            jax.ShapeDtypeStruct((8, width), jnp.float32),
            jax.ShapeDtypeStruct(maps.shape, jnp.float32),
        ],
        scratch_shapes=[
            pltpu.VMEM((span, width), jnp.bfloat16),
            pltpu.VMEM((span, width), jnp.bfloat16),
            pltpu.VMEM((span, 128), jnp.float32),
            pltpu.VMEM((span, width), jnp.float32),
        ],
        compiler_params=params(36),
        cost_estimate=light(),
        name="learn_back",
    )(shares, grad, patched, gain, maps)
    return out[0], out[1], jnp.sum(out[2], axis=0), out[3]


def inward_back_kernel(shares, *refs):
    grad_refs, weight_refs = refs[:shares], refs[shares : 2 * shares]
    later_ref, input_ref, gain_ref, out_ref, gain_grad_ref = refs[2 * shares :]

    @pl.when(pl.program_id(0) == 0)
    def _():
        gain_grad_ref[...] = jnp.zeros_like(gain_grad_ref)

    total = None
    for grad_ref, weight_ref in zip(grad_refs, weight_refs):
        for at in range(3):
            term = nt(grad_ref[at], weight_ref[at])
            total = term if total is None else total + term
    out_ref[...] = total

    def work(rows):
        normal, inverse = standard(input_ref[rows, :])
        back, gain_grad = standard_back(out_ref[rows, :], normal, inverse, gain_ref[...])
        out_ref[rows, :] = later_ref[rows, :] + back
        gain_grad_ref[...] += gain_grad

    by_rows(input_ref.shape[0], work)


def inward_back(grads, weights, later, inputs, gain):
    rows, width = inputs.shape
    block = row_block(rows, 400)
    line = pl.BlockSpec((block, width), lambda at: (at, 0))
    gain = gain[None]
    heads = grads[0].shape[2]
    out = pl.pallas_call(
        partial(inward_back_kernel, len(grads)),
        grid=(rows // block,),
        in_specs=[pl.BlockSpec((3, block, heads), lambda at: (0, at, 0))] * len(grads)
        + [
            pl.BlockSpec((3, width, heads), lambda at, panel=panel: (0, 0, panel))
            for _, panel in weights
        ]
        + [line, line, whole_spec(gain)],
        out_specs=[line, eight_spec(width)],
        out_shape=[
            jax.ShapeDtypeStruct((rows, width), jnp.float32),
            jax.ShapeDtypeStruct((8, width), jnp.float32),
        ],
        compiler_params=params(28),
        cost_estimate=light(),
        name="inward_back",
    )(*grads, *(weight for weight, _ in weights), later, inputs, gain)
    return out[0], jnp.sum(out[1], axis=0)


def few_kernel(shares, *refs):
    input_ref, gain_one_ref, gain_two_ref, bias_ref = refs[:4]
    qkv_refs, out_refs = refs[4 : 4 + shares], refs[4 + shares : 4 + 2 * shares]
    across_ref, hidden_ref, second_ref = refs[4 + 2 * shares : 7 + 2 * shares]
    projected_refs = refs[7 + 2 * shares : 7 + 3 * shares]
    context_refs = refs[7 + 3 * shares :]
    total = input_ref[...]
    across = (standard(total)[0] * gain_one_ref[...]).astype(jnp.bfloat16)
    across_ref[...] = across
    for share in range(shares):
        parts = [mm(across, qkv_refs[share][at]).astype(jnp.bfloat16) for at in range(3)]
        for at, part in enumerate(parts):
            projected_refs[share][at] = part
        for first in range(0, parts[0].shape[1], 2 * HEAD_DIM):
            query, keys, values = (part[:, first : first + 2 * HEAD_DIM] for part in parts)
            context_refs[share][:, first : first + 2 * HEAD_DIM] = mix(
                scaled(query), keys, values, bias_ref[...]
            )
    for share in range(shares):
        total = total + mm(context_refs[share][...], out_refs[share][...])
    hidden_ref[...] = total
    second_ref[...] = (standard(total)[0] * gain_two_ref[...]).astype(jnp.bfloat16)


def few(inputs, gain_one, gain_two, bias, weights_qkv, weights_out):
    rows, width = inputs.shape
    shares, columns = len(weights_qkv), weights_qkv[0].shape[2]
    line = jax.ShapeDtypeStruct((rows, width), jnp.bfloat16)
    out = pl.pallas_call(
        partial(few_kernel, shares),
        out_shape=[line, jax.ShapeDtypeStruct((rows, width), jnp.float32), line]
        + [jax.ShapeDtypeStruct((3, rows, columns), jnp.bfloat16)] * shares
        + [jax.ShapeDtypeStruct((rows, columns), jnp.bfloat16)] * shares,
        compiler_params=params(28),
        cost_estimate=light(),
        name="few",
    )(inputs, gain_one[None], gain_two[None], bias, *weights_qkv, *weights_out)
    return out[0], out[1], out[2], out[3 : 3 + shares], out[3 + shares :]


def few_back_kernel(shares, *refs):
    branch_ref, later_ref, input_ref, gain_ref, bias_ref = refs[:5]
    projected_refs = refs[5 : 5 + shares]
    qkv_refs, out_refs = refs[5 + shares : 5 + 2 * shares], refs[5 + 2 * shares : 5 + 3 * shares]
    grad_ref, gain_grad_ref = refs[5 + 3 * shares : 7 + 3 * shares]
    back_refs = refs[7 + 3 * shares :]
    total = None
    for share in range(shares):
        grad = nt(branch_ref[...], out_refs[share][...]).astype(jnp.bfloat16)
        for first in range(0, grad.shape[1], 2 * HEAD_DIM):
            pair = slice(first, first + 2 * HEAD_DIM)
            query, keys, values = (projected_refs[share][at, :, pair] for at in range(3))
            parts = mix_back(scaled(query), keys, values, grad[:, pair], bias_ref[...])
            for at, part in enumerate(parts):
                back_refs[share][at, :, pair] = part
    for share in range(shares):
        for at in range(3):
            term = nt(back_refs[share][at], qkv_refs[share][at])
            total = term if total is None else total + term
    normal, inverse = standard(input_ref[...])
    back, gain_grad = standard_back(total, normal, inverse, gain_ref[...])
    grad_ref[...] = later_ref[...] + back
    gain_grad_ref[...] = gain_grad


def few_back(branch, later, inputs, gain, bias, projected, weights_qkv, weights_out):
    rows, width = inputs.shape
    shares, columns = len(weights_qkv), weights_qkv[0].shape[2]
    out = pl.pallas_call(
        partial(few_back_kernel, shares),
        out_shape=[
            jax.ShapeDtypeStruct((rows, width), jnp.float32),
            jax.ShapeDtypeStruct((8, width), jnp.float32),
        ]
        + [jax.ShapeDtypeStruct((3, rows, columns), jnp.bfloat16)] * shares,
        compiler_params=params(28),
        cost_estimate=light(),
        name="few_back",
    )(branch, later, inputs, gain[None], bias, *projected, *weights_qkv, *weights_out)
    return out[0], jnp.sum(out[1], axis=0), out[2:]


def again_kernel(rows_refs, up_ref, down_ref, up_grad_ref, down_grad_ref):
    def work(second_ref, grad_ref, begin):
        second, grad = second_ref[...], grad_ref[...]
        up, down = up_ref[...], down_ref[...]
        actives, inners = [], []
        ranges = spans(second.shape[0], 256)
        ahead = mm(second[ranges[0][0] : ranges[0][1]], up)
        for at, (start, end) in enumerate(ranges):
            upward = ahead
            grad_active = nt(grad[start:end], down)
            if at + 1 < len(ranges):
                ahead = mm(second[ranges[at + 1][0] : ranges[at + 1][1]], up)
            active, slope = gelu_pair(upward)
            actives.append(active)
            inners.append((grad_active * slope.astype(jnp.float32)).astype(jnp.bfloat16))
        active, inner = jnp.concatenate(actives), jnp.concatenate(inners)
        if begin:
            down_grad_ref[...] = tn(active, grad)
            up_grad_ref[...] = tn(second, inner)
        else:
            down_grad_ref[...] += tn(active, grad)
            up_grad_ref[...] += tn(second, inner)

    @pl.when(pl.program_id(1) == 0)
    def _():
        work(rows_refs[0], rows_refs[1], True)

    @pl.when(pl.program_id(1) == 1)
    def _():
        work(rows_refs[2], rows_refs[3], False)


def again(piece, pieces, rows, up, down, before):
    width, units = up.shape
    size = min(512, units // pieces)
    first = piece * (units // pieces // size)
    spots = [
        pl.BlockSpec((width, size), lambda chunk, part: (0, first + chunk)),
        pl.BlockSpec((size, width), lambda chunk, part: (first + chunk, 0)),
    ]

    def kernel(*refs):
        again_kernel(refs[:4], *refs[4:6], *refs[-2:])

    return pl.pallas_call(
        kernel,
        grid=(units // pieces // size, 2),
        in_specs=[whole_spec(array) for array in rows]
        + spots
        + [pl.BlockSpec(memory_space=pl.ANY)] * len(before),
        out_specs=spots,
        out_shape=[
            jax.ShapeDtypeStruct(up.shape, jnp.float32),
            jax.ShapeDtypeStruct(down.shape, jnp.float32),
        ],
        input_output_aliases={6: 0, 7: 1} if before else {},
        compiler_params=params(48),
        cost_estimate=light(),
        name="again",
    )(*rows, up, down, *before)


def swap(tensor, bit):
    count = lax.axis_size("dp")
    return lax.ppermute(tensor, "dp", [(place, place ^ (1 << bit)) for place in range(count)])


def my_bit(bit):
    return ((lax.axis_index("dp") >> bit) & 1).astype(jnp.int32).reshape(1)


def meet(value, others):
    if not others:
        return value, []
    value, others = lax.optimization_barrier((value, tuple(others)))
    return value, list(others)


def part_of(number, step, count, mine):
    first = number == mine
    return jnp.where(first, jnp.minimum(step, count - 1), jnp.maximum(step - count, 0))


def divisor(size, most):
    return max(step for step in range(16, most + 1, 16) if size % step == 0)


def fold_kernel(cuts, count, mine_ref, *refs):
    kept_ref, sent_ref = refs[-2:]
    step = pl.program_id(0)
    keep = (step < count) == (mine_ref[0] == 0)
    at = 0
    for first, last, terms in cuts:
        inside = (step >= first) & (step < last)
        sources, at = refs[at : at + terms], at + terms

        def value(sources=sources):
            total = sources[0][...].astype(jnp.float32)
            for source in sources[1:]:
                total = total + source[...].astype(jnp.float32)
            return total.astype(jnp.bfloat16)

        @pl.when(inside & keep)
        def _():
            kept_ref[...] = value()

        @pl.when(inside & jnp.logical_not(keep))
        def _():
            sent_ref[...] = value()


def fold(sources, width, mine):
    total = sum(rows for _, _, rows, _ in sources)
    block = divisor(math.gcd(total // 2, *(value for s in sources for value in s[1:3])), 512)
    count = total // 2 // block
    cuts, specs, terms, at = [], [], [], 0
    for arrays, start, rows, panel in sources:
        steps = rows // block

        def place(step, mine_ref, at=at, steps=steps, start=start // block, panel=panel):
            return start + jnp.clip(step - at, 0, steps - 1), panel

        cuts.append((at, at + steps, len(arrays)))
        specs += [pl.BlockSpec((block, width), place)] * len(arrays)
        terms += arrays
        at += steps
    half = jax.ShapeDtypeStruct((total // 2, width), jnp.bfloat16)
    return pl.pallas_call(
        partial(fold_kernel, cuts, count),
        grid_spec=pltpu.PrefetchScalarGridSpec(
            num_scalar_prefetch=1,
            grid=(2 * count,),
            in_specs=specs,
            out_specs=[
                pl.BlockSpec((block, width), lambda i, m: (part_of(m[0], i, count, 0), 0)),
                pl.BlockSpec((block, width), lambda i, m: (part_of(1 - m[0], i, count, 0), 0)),
            ],
        ),
        out_shape=[half, half],
        compiler_params=params(18),
        cost_estimate=light(),
        name="fold",
    )(mine, *terms)


def put(out_ref, value):
    value = value.astype(out_ref.dtype)
    if len(out_ref.shape) == 2:
        out_ref[...] = value
        return
    wide = out_ref.shape[2]
    for at in range(3):
        out_ref[at] = value[:, at * wide : (at + 1) * wide]


def spread_kernel(cuts, parts, mines_ref, *refs):
    outs = refs[2 * len(parts) :]
    step = pl.program_id(0)
    for at, (begin, count) in enumerate(parts):
        own_ref, got_ref = refs[2 * at : 2 * at + 2]
        own = (step < begin + count) == (mines_ref[at] == 0)
        for first, last, out in cuts[at]:
            inside = (step >= first) & (step < last)

            @pl.when(inside & own)
            def _():
                put(outs[out], own_ref[...])

            @pl.when(inside & jnp.logical_not(own))
            def _():
                put(outs[out], got_ref[...])


def spread(pieces, layouts, outs, dtype):
    width = pieces[0][0].shape[1]
    sizes = [piece[0].shape[0] for piece in pieces]
    sizes += [value for layout in layouts for entry in layout for value in entry[1:3]]
    block = divisor(math.gcd(*sizes), 512)
    parts, cuts, specs, terms, step = [], [], [], [], 0
    visits = [[] for _ in outs]
    for at, (own, got, _) in enumerate(pieces):
        count = own.shape[0] // block
        parts.append((step, count))
        for half in range(2):

            def place(i, m, at=at, half=half, begin=step, count=count):
                i = jnp.clip(i - begin, 0, 2 * count - 1)
                return part_of(m[at] if half == 0 else 1 - m[at], i, count, 0), 0

            specs.append(pl.BlockSpec((block, width), place))
        terms += [own, got]
        mine, first = [], step
        for out, start, rows, panel in layouts[at]:
            steps = rows // block
            mine.append((first, first + steps, out))
            visits[out].append((first, steps, start // block, panel))
            first += steps
        cuts.append(mine)
        step += 2 * count

    def out_spec(seen, shape):
        def place(i, m):
            row, panel = seen[0][2], seen[0][3]
            for first, steps, start, column in seen:
                here = i >= first
                row = jnp.where(here, start + jnp.clip(i - first, 0, steps - 1), row)
                panel = jnp.where(here, column, panel)
            return (row, panel) if len(shape) == 2 else (0, row, panel)

        if len(shape) == 3:
            return pl.BlockSpec((3, block, width // 3), place)
        return pl.BlockSpec((block, width), place)

    return pl.pallas_call(
        partial(spread_kernel, cuts, parts),
        grid_spec=pltpu.PrefetchScalarGridSpec(
            num_scalar_prefetch=1,
            grid=(step,),
            in_specs=specs,
            out_specs=[out_spec(seen, shape) for seen, shape in zip(visits, outs)],
        ),
        out_shape=[jax.ShapeDtypeStruct(shape, dtype) for shape in outs],
        compiler_params=params(22),
        cost_estimate=light(),
        name="spread",
    )(jnp.concatenate([mine for _, _, mine in pieces]), *terms)


def join(own, got, mine):
    rows, width = own.shape
    layout = [(0, 0, 2 * rows, 0)]
    return spread([(own, got, mine)], [layout], [(2 * rows, width)], own.dtype)[0]


class Flow:
    def __init__(self, halves, order, back=False):
        self.order, self.step = order, 0
        self.kept, self.sent = halves
        self.got = swap(self.sent, order[0])
        self.length = 2 * len(order) - 1 if back else len(order)

    def done(self):
        return self.step == self.length

    def advance(self):
        self.step += 1
        bits, turn = self.order, len(self.order)
        if self.step < turn:
            rows, width = self.kept.shape
            bit = bits[self.step]
            self.kept, self.sent = fold([((self.kept, self.got), 0, rows, 0)], width, my_bit(bit))
        elif self.step == turn:
            bit = bits[-1]
            total = self.kept.astype(jnp.float32) + self.got.astype(jnp.float32)
            self.kept = self.sent = total.astype(jnp.bfloat16)
        else:
            bit = bits[2 * turn - 1 - self.step]
            self.kept = self.sent = join(self.kept, self.got, my_bit(bits[2 * turn - self.step]))
        if self.step < self.length or self.length > turn:
            self.got = swap(self.sent, bit)


def in_order(gathered, order):
    count = len(order)
    rows, width = gathered.shape[1:]
    split = gathered.reshape((2,) * count + (rows, width))
    axes = tuple(count - 1 - bit for bit in order) + (count, count + 1)
    return jnp.transpose(split, axes).reshape(-1, width)


class Gather:
    def __init__(self, rows):
        self.step, self.length = 0, lax.axis_size("dp").bit_length()
        self.kept = self.sent = rows
        self.got = swap(rows, 0)

    def done(self):
        return self.step == self.length

    def advance(self):
        self.step += 1
        if self.step < self.length:
            self.kept = self.sent = join(self.kept, self.got, my_bit(self.step - 1))
            last = self.step == self.length - 1
            self.got = near(1)(self.kept) if last else swap(self.kept, self.step)


class Small:
    def __init__(self, tensors):
        self.kept = self.sent = jnp.concatenate(tensors)
        self.step, self.length = 0, lax.axis_size("mp") - 1
        self.length += lax.axis_size("dp").bit_length() - 1
        self.mine = self.kept
        self.issue()

    def issue(self):
        near_by = lax.axis_size("mp") - 1
        if self.step < near_by:
            self.got = give(self.step + 1)(self.mine)
        else:
            self.got = swap(self.kept, self.step - near_by)

    def done(self):
        return self.step == self.length

    def advance(self):
        self.kept = self.sent = self.kept + self.got
        self.step += 1
        if not self.done():
            self.issue()


class Clock:
    def __init__(self, plan, sets):
        self.plan, self.sets = plan, dict(sets)
        self.flows, self.begun, self.past, self.whole = {}, [], [], {}

    def begin(self, name, flow):
        self.flows[name] = flow
        self.begun.append(flow.sent)

    def __call__(self, name, value):
        names = self.plan.get(name, ())
        flows = [self.flows[flow] for flow in names if flow in self.flows]
        ended = [flow for flow in flows if flow.done()]
        flows = [flow for flow in flows if not flow.done()]
        ready = [key for key in names if key in self.whole]
        waited = [flow.got for flow in flows] + [self.whole[key] for key in ready]
        waited += [flow.got for flow in ended]
        value, got = meet(value, waited + self.past)
        self.past = []
        for flow in flows:
            flow.got = got.pop(0)
            flow.advance()
        for key in ready:
            self.whole[key] = got.pop(0)
        for flow in ended:
            flow.got = got.pop(0)
        for key, members in list(self.sets.items()):
            if all(name in self.flows and self.flows[name].done() for name in members):
                self.begun.append(self.gather(key))
        value = meet(value, self.begun + [flow.sent for flow in flows])[0]
        self.begun = []
        return value

    def gather(self, key):
        kept = [self.flows[name].kept for name in self.sets.pop(key)]
        own = jnp.concatenate(kept) if len(kept) > 1 else kept[0]
        self.whole[key] = lax.all_gather(own, "dp")
        return own

    def end(self, names):
        flows = [self.flows[name] for name in names]
        while not all(flow.done() for flow in flows):
            for flow in flows:
                if not flow.done():
                    flow.advance()

    def rows(self, names, whole):
        pieces, at = [], 0
        for flow in (self.flows[name] for name in names):
            own = flow.kept.shape[0]
            pieces.append(in_order(whole[:, at : at + own], flow.order))
            at += own
        return pieces


def grads_kernel(cuts, count, *refs):
    outs = refs[-2:] if count else refs[-1:]
    step = pl.program_id(0)
    keep = True if not count else (step < count) == (refs[0][0] == 0)
    at = 1
    for first, last, terms in cuts:
        inside = (step >= first) & (step < last)
        sources, at = refs[at : at + terms], at + terms

        @pl.when(inside)
        def _(sources=sources):
            if len(sources[1].shape) == 2:
                total = tn(sources[0][...], sources[1][...])
            else:
                left = sources[0][...].T
                total = jnp.concatenate([mm(left, sources[1][part]) for part in range(3)], axis=1)
            if len(sources) > 2:
                total = total + sources[2][...].astype(jnp.float32)
            total = total.astype(jnp.bfloat16)
            if not count:
                outs[0][...] = total
                return

            @pl.when(keep)
            def _():
                outs[0][...] = total

            @pl.when(jnp.logical_not(keep))
            def _():
                outs[1][...] = total


def grads(sources, width, mine=None):
    total = sum(source[2] for source in sources)
    sizes = [value for source in sources for value in source[1:3]]
    if mine is not None:
        sizes.append(total // 2)
    sizes += [source[6] for source in sources if len(source) > 5]
    block = divisor(math.gcd(*sizes), 512)
    cuts, specs, terms, at = [], [], [], 0
    for source in sources:
        left, start, columns, right, panel = source[:5]
        steps = columns // block
        rows = left.shape[0]

        def here(step, at=at, steps=steps):
            return jnp.clip(step - at, 0, steps - 1)

        specs.append(
            pl.BlockSpec((rows, block), lambda i, *m, f=here, s=start // block: (0, s + f(i)))
        )
        if right.ndim == 2:
            specs.append(pl.BlockSpec((rows, width), lambda i, *m, p=panel: (0, p)))
        else:
            specs.append(whole_spec(right))
        terms += [left, right]
        if len(source) > 5:
            other, row, column = source[5:]
            specs.append(
                pl.BlockSpec(
                    (block, width), lambda i, *m, f=here, s=row // block, p=column: (s + f(i), p)
                )
            )
            terms.append(other)
        cuts.append((at, at + steps, 3 if len(source) > 5 else 2))
        at += steps
    count = 0 if mine is None else total // 2 // block
    if count:
        shape = jax.ShapeDtypeStruct((total // 2, width), jnp.bfloat16)
        out_shape = [shape, shape]
        out_specs = [
            pl.BlockSpec((block, width), lambda i, m: (part_of(m[0], i, count, 0), 0)),
            pl.BlockSpec((block, width), lambda i, m: (part_of(1 - m[0], i, count, 0), 0)),
        ]
    else:
        mine = jnp.zeros((1,), jnp.int32)
        out_shape = jax.ShapeDtypeStruct((total, width), jnp.bfloat16)
        out_specs = pl.BlockSpec((block, width), lambda i, m: (i, 0))
    return pl.pallas_call(
        partial(grads_kernel, cuts, count),
        grid_spec=pltpu.PrefetchScalarGridSpec(
            num_scalar_prefetch=1, grid=(at,), in_specs=specs, out_specs=out_specs
        ),
        out_shape=out_shape,
        compiler_params=params(38),
        cost_estimate=light(),
        name="grads",
    )(mine, *terms)


def near(step):
    count = lax.axis_size("mp")
    pairs = [((to + step) % count, to) for to in range(count)]
    return lambda tensor: lax.ppermute(tensor, "mp", pairs)


def give(step):
    count = lax.axis_size("mp")
    pairs = [(start, (start + step) % count) for start in range(count)]
    return lambda tensor: lax.ppermute(tensor, "mp", pairs)


def fetch(tensor):
    return [tensor] + [near(step)(tensor) for step in range(1, lax.axis_size("mp"))]


def total_over_all(terms):
    total = terms[0].astype(jnp.float32)
    for step in range(1, len(terms)):
        total = total + give(step)(terms[step]).astype(jnp.float32)
    return lax.psum(total.astype(jnp.bfloat16), "dp").astype(jnp.float32)


def lower_forward(inputs, weights, bias, later):
    gain_one, weight_qkv, weight_out, gain_two, weight_up, weight_down = weights
    across = norm(inputs, gain_one)
    projections, contexts = [], []
    for share in weight_qkv:
        projected = jnp.einsum(
            "rd,tdc->trc", across, share, preferred_element_type=jnp.float32
        ).astype(jnp.bfloat16)
        projections.append(projected)
        contexts.append(attend(bias, projected))
    hidden, second = outward(contexts, weight_out, inputs, gain_two)
    second, later = meet(second, later)
    result, actives, slopes = feed(second, hidden, weight_up, weight_down)
    stored = (inputs, hidden, across, second, projections, contexts, actives, slopes)
    return result, stored, later


def upper_forward(inputs, weights, bias, clock):
    gain_one, weight_qkv, weight_out, gain_two, weight_up, weight_down = weights
    across, hidden, second, projections, contexts = few(
        inputs, gain_one, gain_two, bias, weight_qkv, weight_out
    )
    if len(weight_qkv) == 2 and lax.axis_size("dp") == 16:
        clock.begin("seconds", Gather(second))
    second = clock("second-feed", second)
    result, actives, slopes = feed(second, hidden, weight_up, weight_down)
    return result, (inputs, hidden, across, second, projections, contexts, actives, slopes)


def low(value):
    return value.astype(jnp.bfloat16)


def project_sources(across, back, others=None):
    source = (across, 0, across.shape[1], back, 0)
    return [source if others is None else source + (others, 0, 0)]


def out_sources(context, grad_branch, wide, others=None, first=0):
    rows = context.shape[1]
    panels = range(grad_branch.shape[1] // wide)
    sources = [(context, 0, rows, grad_branch, panel) for panel in panels]
    if others is None:
        return sources
    return [source + (others, first + at * rows, 0) for at, source in enumerate(sources)]


def upper_backward(grad_out, stored, weights, bias, clock):
    gain_one, weight_qkv, weight_out, gain_two, weight_up, weight_down = weights
    inputs, hidden, across, second, projections, contexts, actives, slopes = stored
    shares = range(len(weight_qkv))
    grad_out = clock("second-back", grad_out)
    grad_hidden, grad_branch, grad_mix, grad_gain_two, inners = feed_back(
        grad_out, hidden, gain_two, slopes, weight_up, weight_down
    )
    quick = len(shares) == 2 and lax.axis_size("dp") == 16
    grad_branch = clock("second-few", grad_branch)
    grad_inputs, grad_gain_one, backs = few_back(
        grad_branch, grad_hidden, inputs, gain_one, bias, projections, weight_qkv, weight_out
    )
    if quick:
        projects = grads(project_sources(across, backs[1]), 3 * contexts[0].shape[1])
        clock.past.append(projects)
        weight_grads = (across, backs, contexts, grad_branch, give(1)(projects))
    else:
        weight_grads = plain_grads(
            across, backs, contexts, grad_branch, second, inners, actives, grad_mix
        )
    return grad_inputs, grad_gain_one, grad_gain_two, weight_grads


def plain_grads(across, backs, contexts, grad_branch, second, inners, actives, grad_mix):
    shares = range(len(contexts))
    pairs = (
        [jnp.concatenate([tn(across, part) for part in backs[at]]) for at in shares],
        [tn(contexts[at], grad_branch) for at in shares],
        [tn(second, inners[at]) for at in shares],
        [tn(actives[at], grad_mix) for at in shares],
    )
    return tuple(total_over_all([low(term) for term in terms]) for terms in pairs)


def lower_backward(grad_out, grad_mix, stored, weights, bias, clock, upper_sources):
    gain_one, weight_qkv, weight_out, gain_two, weight_up, weight_down = weights
    inputs, hidden, across, second, projections, contexts, actives, slopes = stored
    shares = range(len(weight_qkv))
    quick = len(shares) == 2 and lax.axis_size("dp") == 16
    bits = tuple(range(lax.axis_size("dp").bit_length() - 1))
    turned = (1, 0) + bits[2:]
    width, units = weight_up[0].shape
    wide = contexts[0].shape[1]
    if quick:
        upper_across, upper_backs, upper_contexts, upper_branch, project_others = upper_sources
        grad_mix, (project_others,) = meet(clock("down1", grad_mix), [project_others])
        heads = 3 * wide
        sources = [(actives[1], 0, units, grad_mix, 0)]
        others = grads(sources + out_sources(upper_contexts[1], upper_branch, width), width)
        upper_across = meet(upper_across, [others])[0]
        others = give(1)(others)
        sources = project_sources(upper_across, upper_backs[0], project_others)
        halves = grads(sources, heads, my_bit(bits[0]))
        clock.begin("heads", Flow(halves, bits, True))
        grad_mix = meet(grad_mix, halves)[0]
        sources = [(actives[0], 0, units, grad_mix, 0, others, 0, 0)]
        sources += out_sources(upper_contexts[0], upper_branch, width, others, units)
        clock.begin("down", Flow(grads(sources, width, my_bit(turned[0])), turned, True))
    grad_out = clock("feed", grad_out)
    grad_hidden, grad_branch, grad_mix, grad_gain_two, inners = feed_back(
        grad_out, hidden, gain_two, slopes, weight_up, weight_down
    )
    if quick:
        panels = range(units // width)
        grad_branch = clock("up1", grad_branch)
        sources = [(second, 0, width, inners[1], panel) for panel in panels]
        sources += out_sources(contexts[1], grad_branch, width)
        up_others = grads(sources, width)
        grad_branch = meet(grad_branch, [up_others])[0]
        up_others = give(1)(up_others)
    groups = 2 if quick and wide % (4 * HEAD_DIM) == 0 else 1
    backs, grad_contexts = {}, {}
    for group in range(groups):
        for at in reversed(shares):
            if group == 0:
                grad_branch = clock(f"heads{group}{at}", grad_branch)
                grad_contexts[at] = low(nt(grad_branch, weight_out[at]))
            else:
                grad_contexts[at] = clock(f"heads{group}{at}", grad_contexts[at])
            back = attend_back(bias, projections[at], grad_contexts[at], group, groups)
            backs[at, group] = back = clock(f"project{group}{at}", back)
            if quick and at:
                others = grads(project_sources(across, back), 3 * wide // groups)
                clock.past.append(others)
                others = give(at)(others)
            elif quick:
                sources = project_sources(across, back, others)
                order = turned if group else bits
                halves = grads(sources, 3 * wide // groups, my_bit(order[0]))
                clock.past += halves
                clock.begin(f"project-{group}", Flow(halves, order, True))
            if quick and at and group == 0:
                grad_branch = clock("up0", grad_branch)
                for panel in panels:
                    sources = [
                        (second, 0, width, inners[0], panel, up_others, panel * width, 0)
                    ]
                    if panel == len(panels) - 1:
                        sources += out_sources(contexts[0], grad_branch, width, up_others, units)
                    sources[0] = (meet(second, [grad_branch])[0],) + sources[0][1:]
                    order = turned if panel % 2 else bits
                    halves = grads(sources, width, my_bit(order[0]))
                    clock.past += halves
                    clock.begin(f"up-{panel}", Flow(halves, order))
    weight_grads = None
    if not quick:
        whole_backs = [backs[at, 0] for at in shares]
        weight_grads = plain_grads(
            across, whole_backs, contexts, grad_branch, second, inners, actives, grad_mix
        )
    inputs = clock("inward", inputs)
    grad_inputs, grad_gain_one = inward_back(
        [backs[at, group] for at in shares for group in range(groups)],
        [(weight_qkv[at], group) for at in shares for group in range(groups)],
        grad_hidden,
        inputs,
        gain_one,
    )
    return grad_inputs, grad_gain_one, grad_gain_two, weight_grads


PLAN = {
    "learn": ("mixes",),
    "second-back": ("seconds",),
    "second-few": ("seconds",),
    "learner": ("seconds",),
    "up1": ("heads", "down", "seconds"),
    "heads00": ("heads", "down", "seconds"),
    "heads11": ("heads", "down", "up-0", "up-1"),
    "project11": ("up-0", "up-1", "project-0"),
    "heads10": ("heads", "down", "up-0", "up-1"),
    "project10": ("up-0", "up-1", "project-0"),
    "inward": ("heads", "down", "project-0"),
    "tail0": ("heads", "down", "project-0", "project-1"),
    "tail1": ("project-0", "project-1", "small"),
    "tail2": ("project-0", "project-1", "small"),
    "tail3": ("project-0", "project-1", "small", "up-all"),
    "tail4": ("project-1", "small"),
    "again0": ("heads", "down", "project-1", "small"),
    "again1": ("project-1",),
    "tail5": ("heads", "down", "project-1"),
}
SETS = {"up-all": ("up-0", "up-1")}


def finish(clock, input_grad, project, out, up, down, token_up, token_down):
    width, wide, units = project.shape[1], project.shape[2], up.shape[1]
    wider = jnp.float32
    ups = [f"up-{panel}" for panel in range(units // width)]
    seconds, mixes = clock.flows["seconds"], clock.whole["mixes"]
    rows = [seconds.kept, mixes, seconds.got, near(1)(mixes)]
    rows[0] = meet(rows[0], [input_grad])[0]
    for number in range(4):
        rows[0] = clock(f"tail{number}", rows[0])
    panels = clock.rows(ups, clock.whole["up-all"])
    panels, out_grad = panels[:-1] + [panels[-1][:width]], panels[-1][width:]
    patch_upward_grad = jnp.concatenate(panels, axis=1).astype(wider)
    rows[0], late = meet(rows[0], [patch_upward_grad, out_grad])
    patch_upward_grad, out_grad = late
    rows[0] = clock("tail4", rows[0])
    before = ()
    for piece in range(2):
        rows[0] = clock(f"again{piece}", rows[0])
        before = again(piece, 2, rows, token_up, token_down, before)
        rows[0], before = meet(rows[0], before)
    token_upward_grad, token_downward_grad = before
    token_downward_grad = clock("tail5", token_downward_grad)
    clock.end(clock.flows)

    def last(name):
        flow = clock.flows[name]
        return flow.kept, flow.got, my_bit(flow.order[0])

    patch_downward_grad, token_outproj_grad = spread(
        [last("down")], [[(0, 0, units, 0), (1, 0, wide, 0)]], [down.shape, out.shape], wider
    )
    (token_project_grad,) = spread([last("heads")], [[(0, 0, width, 0)]], [project.shape], wider)
    (patch_project_grad,) = spread(
        [last("project-0"), last("project-1")],
        [[(0, 0, width, 0)], [(0, 0, width, 1)]],
        [project.shape],
        wider,
    )
    return (
        (token_project_grad, token_outproj_grad, token_upward_grad, token_downward_grad),
        (patch_project_grad, out_grad.astype(wider), patch_upward_grad, patch_downward_grad),
    )


def local(
    inputs,
    patch_keep,
    patch_gainone,
    patch_project,
    patch_outproj,
    patch_gaintwo,
    patch_upward,
    patch_downward,
    learner_gain,
    learner_weight,
    token_gainone,
    token_project,
    token_outproj,
    token_gaintwo,
    token_upward,
    token_downward,
    output_grad,
):
    shards = lax.axis_size("mp")
    images_here = patch_keep.shape[0] // shards
    local_keep = (
        lax.dynamic_slice_in_dim(patch_keep, lax.axis_index("mp") * images_here, images_here, 0) > 0
    )
    lower_params = (
        patch_gainone,
        fetch(patch_project),
        fetch(patch_outproj),
        patch_gaintwo,
        fetch(patch_upward),
        fetch(patch_downward),
    )
    lower_bias = key_bias(local_keep)
    image = jnp.arange(images_here * S) // S
    upper_bias = jnp.where(image[:, None] == image[None], 0.0, -1e30).astype(jnp.float32)
    token_weights = [token_project, token_outproj, token_upward, token_downward]
    patched, lower_stored, token_weights = lower_forward(
        inputs, lower_params, lower_bias, token_weights
    )
    weight_qkv, weight_out, weight_up, weight_down = (fetch(weight) for weight in token_weights)
    upper_params = (token_gainone, weight_qkv, weight_out, token_gaintwo, weight_up, weight_down)
    maps = learner_weight.T
    clock = Clock(PLAN, SETS)
    if shards == 2 and lax.axis_size("dp") == 16:
        clock.whole["mixes"] = lax.all_gather(low(output_grad), "dp", tiled=True)
    patched = clock("learn", patched)
    tokens, shares = learn(pair_bias(local_keep), patched, learner_gain, maps)
    token_output, upper_stored = upper_forward(tokens, upper_params, upper_bias, clock)
    token_grad, token_gainone_grad, token_gaintwo_grad, token_grads = upper_backward(
        output_grad, upper_stored, upper_params, upper_bias, clock
    )
    patched_grad, patched_low, learner_gain_grad, maps_grad = learn_back(
        shares, clock("learner", token_grad), patched, learner_gain, maps
    )
    input_grad, patch_gainone_grad, patch_gaintwo_grad, patch_grads = lower_backward(
        patched_grad, patched_low, lower_stored, lower_params, lower_bias, clock, token_grads
    )
    gains = (
        patch_gainone_grad,
        patch_gaintwo_grad,
        learner_gain_grad,
        token_gainone_grad,
        token_gaintwo_grad,
    )
    clock.begin("small", Small([maps_grad] + [gain[None] for gain in gains]))
    if patch_grads is None:
        token_grads, patch_grads = finish(
            clock,
            input_grad,
            patch_project,
            patch_outproj,
            patch_upward,
            patch_downward,
            token_upward,
            token_downward,
        )
    else:
        clock.end(["small"])
    small = clock.flows["small"].kept
    token_project_grad, token_outproj_grad, token_upward_grad, token_downward_grad = token_grads
    patch_project_grad, patch_outproj_grad, patch_upward_grad, patch_downward_grad = patch_grads
    return (
        token_output,
        input_grad,
        small[8],
        patch_project_grad.reshape(patch_project.shape),
        patch_outproj_grad,
        small[9],
        patch_upward_grad,
        patch_downward_grad,
        small[10],
        small[:S].T,
        small[11],
        token_project_grad.reshape(token_project.shape),
        token_outproj_grad,
        small[12],
        token_upward_grad,
        token_downward_grad,
    )


def solution(mesh):
    in_specs = (
        P(("dp", "mp"), None),
        P("dp", None),
        P(),
        P(None, None, "mp"),
        P("mp", None),
        P(),
        P(None, "mp"),
        P("mp", None),
        P(),
        P(),
        P(),
        P(None, None, "mp"),
        P("mp", None),
        P(),
        P(None, "mp"),
        P("mp", None),
        P(("dp", "mp"), None),
    )
    out_specs = (
        P(("dp", "mp"), None),
        P(("dp", "mp"), None),
        P(),
        P(None, None, "mp"),
        P("mp", None),
        P(),
        P(None, "mp"),
        P("mp", None),
        P(),
        P(),
        P(),
        P(None, None, "mp"),
        P("mp", None),
        P(),
        P(None, "mp"),
        P("mp", None),
    )
    return jax.shard_map(local, mesh=mesh, in_specs=in_specs, out_specs=out_specs, check_vma=False)
```

time: 1810 us -> 795 us (0.44)
  waiting for transfers between devices: 916 us -> 137 us
  Pallas kernels: 0 us -> 451 us
  matrix products: 415 us -> 19.1 us
  other arithmetic: 167 us -> 11 us
  local copies, waits for them, and re-layouts: 227 us -> 81 us
  starting transfers between devices: 0.95 us -> 69.1 us
  blocking collectives: 54 us -> 0 us
    psum x1 -> x0, waiting for transfers between devices: 768 us -> none  [local(): lax.psum(matrices[0].astype(jnp.bfloat16), 'dp').astype(jnp.float32)]
    pallas_call x0 -> x67, Pallas kernels: none -> 451 us  [the longest x6 79.4 us: attention(): pl.pallas_call(kernel, grid=(pairs,), in_specs=[pl.BlockSpec(bias.shape,...]
    dot_general x42 -> x4, matrix products: 415 us -> 19.1 us  [the longest x2 14.1 us: lower_forward(): jnp.einsum('rd,tdc->trc', across, share, preferred_element_type=jnp.float32)]
    ppermute x0 -> x64, waiting for transfers between devices: none -> 137 us  [the longest x48 133 us: swap(): lax.ppermute(tensor, 'dp', [(place, place ^ 1 << bit) for place in range(...]
    reduce_sum x22 -> x5, other arithmetic: 80 us -> 0.07 us  [the longest x2 0.03 us: feed_back(): return (out[0], out[1], out[2], jnp.sum(out[3], axis=0), out[4:])]
    all_gather x4 -> x2, waiting for transfers between devices: 74.4 us -> 0.03 us  [the longest x1 0.02 us: gather(): self.whole[key] = lax.all_gather(own, 'dp')]
    reduce_scatter x8 -> x0, waiting for transfers between devices: 72.9 us -> none  [local(): lax.psum_scatter(producer(jnp.int32(0), lax.axis_size('mp') * row_count)....]
    ppermute x0 -> x64, starting transfers between devices: none -> 69 us  [the longest x48 66.1 us: swap(): lax.ppermute(tensor, 'dp', [(place, place ^ 1 << bit) for place in range(...]
  transfers between devices with their start and end apart: 13 -> 66, of which waited for: 12 -> 20; matrix products, arithmetic and copies ran while one was open for 6% -> 5% of each run, Pallas kernels for 0% -> 50%
where the time goes in v1:
time: 795 us; the launch traced here: 785 us
  Pallas kernels  451 us (57%)
  waiting for transfers between devices  137 us (17%)
  local copies, waits for them, and re-layouts  81 us (10%)
  starting transfers between devices  69.1 us (9%)
  matrix products  19.1 us (2%)
  between operations  16.1 us (2%)
  other arithmetic  11 us (1%)
    ppermute x48, waiting for transfers between devices, swap(): lax.ppermute(tensor, 'dp', [(place, place ^ 1 << bit) for place in range(...  133 us
    pallas_call x6, Pallas kernels, attention(): pl.pallas_call(kernel, grid=(pairs,), in_specs=[pl.BlockSpec(bias.shape,...  79.4 us
    pallas_call x11, Pallas kernels, grads(): pl.pallas_call(partial(grads_kernel, cuts, count), grid_spec=pltpu.Prefet...  75.9 us
    unnamed x250, local copies, waits for them, and re-layouts  71.8 us
    ppermute x48, starting transfers between devices, swap(): lax.ppermute(tensor, 'dp', [(place, place ^ 1 << bit) for place in range(...  66.1 us
    pallas_call x2, Pallas kernels, feed(): pl.pallas_call(partial(ff_kernel, shares, per), grid=(rows // block, shar...  65.7 us
    pallas_call x2, Pallas kernels, again(): pl.pallas_call(kernel, grid=(units // pieces // size, 2), in_specs=[whole...  59.3 us
    pallas_call x2, Pallas kernels, feed_back(): pl.pallas_call(partial(ff_back_kernel, shares, per), grid=(rows // block,...  58.7 us
  transfers between devices with their start and end apart: 66, of which 20 were waited for; matrix products, arithmetic and copies ran while one was open for 5% of the time, Pallas kernels for 50%

profile of v1, /device:TPU:0, one launch (start us, length us, event | category | flops | bytes accessed | tf_op | source)
XLA Modules:
  0.0 784.9 jit_solution(5283807063357599771)
XLA Ops:
  16.9 6.7 convert_bitcast_fusion.1.qkv_ref
  25.4 7.4 convert_bitcast_fusion.qkv_ref
  32.8 14.0 %attend.2.refs_0_.refs_4_ = bf16[1568,512]{1,0:T(8,128)(2,1)S(1)} custom-call(f32[8,208,1]{2,1,0:T(8,128)S(1)} %copy-done.10, bf16[3,1568,512]{2,1,0:T(8,128)(2,1)S(1)} %copy-done.7), custom_call_target="tpu_custom_call" | custom-call | flops 1000 | bytes 1000 | tf_op jit(solution)/shard_map/attend/pallas_call | solution.py:134
  46.8 14.0 %attend.3.refs_1_.refs_5_ = bf16[1568,512]{1,0:T(8,128)(2,1)S(1)} custom-call(f32[8,208,1]{2,1,0:T(8,128)S(1)} %copy-done.10, bf16[3,1568,512]{2,1,0:T(8,128)(2,1)S(1)} %convert_bitcast_fusion.qkv_ref), custom_call_target="tpu_custom_call" | custom-call | flops 1000 | bytes 1000 | tf_op jit(solution)/shard_map/attend/pallas_call | solution.py:134
  64.2 9.0 %outward.1 = (f32[1568,1024]{1,0:T(8,128)S(1)}, bf16[1568,1024]{1,0:T(8,128)(2,1)S(1)}) custom-call(bf16[1568,512]{1,0:T(8,128)(2,1)S(1)} %attend.2.refs_0_.refs_4_, bf16[1568,512]{1,0:T(8,128)(2,1)S(1)} %attend.3.refs_1_.refs_5_, bf16[512,1024]{1,0:T(8,128)(2,1)S(1)} %copy-done.63, bf16[512,1024]{1,0:T(8,128)(2,1)} %collective-permute-done.1.refs_3_, ...), custom_call_target="tpu_custom_call" | custom-call | flops 1000 | bytes 1000 | tf_op jit(solution)/shard_map/outward/pallas_call | solution.py:303
  79.1 54.4 %feed.2 = (f32[1568,1024]{1,0:T(8,128)}, bf16[1568,2048]{1,0:T(8,128)(2,1)}, bf16[1568,2048]{1,0:T(8,128)(2,1)}, bf16[1568,2048]{1,0:T(8,128)(2,1)}, bf16[1568,2048]{1,0:T(8,128)(2,1)}) custom-call(bf16[1568,1024]{1,0:T(8,128)(2,1)} %copy-done, f32[1568,1024]{1,0:T(8,128)} %copy-done.14, bf16[1024,2048]{1,0:T(8,128)(2,1)} %refs_5_.5, ...), custom_call_target="tpu_custom_call" | custom-call | flops 1000 | bytes 1000 | tf_op jit(solution)/shard_map/feed/pallas_call | solution.py:368
  136.4 5.3 learn.1
  142.4 7.7 few.1
  156.3 3.8 collective-permute-done.8.refs_1_
  163.5 11.3 %feed.3 = (f32[64,1024]{1,0:T(8,128)}, bf16[64,2048]{1,0:T(8,128)(2,1)}, bf16[64,2048]{1,0:T(8,128)(2,1)}, bf16[64,2048]{1,0:T(8,128)(2,1)}, bf16[64,2048]{1,0:T(8,128)(2,1)}) custom-call(bf16[64,1024]{1,0:T(8,128)(2,1)} %copy-done.72, f32[64,1024]{1,0:T(8,128)} %copy-done.56, bf16[1024,2048]{1,0:T(8,128)(2,1)} %refs_4_.11, ...), custom_call_target="tpu_custom_call" | custom-call | flops 1000 | bytes 1000 | tf_op jit(solution)/shard_map/feed/pallas_call | solution.py:368
  176.7 11.2 %feed_back.2 = (f32[64,1024]{1,0:T(8,128)S(1)}, bf16[64,1024]{1,0:T(8,128)(2,1)S(1)}, bf16[64,1024]{1,0:T(8,128)(2,1)}, f32[8,1024]{1,0:T(8,128)S(1)}, bf16[64,2...) custom-call(f32[64,1024]{1,0:T(8,128)S(1)} %copy-done.58, f32[64,1024]{1,0:T(8,128)S(1)} %copy-done.57, f32[1,1024]{1,0:T(1,128)S(1)} %bitcast.70, ...), custom_call_target="tpu_custom_call" | custom-call | flops 1000 | bytes 1000 | tf_op jit(solution)/shard_map/feed_back/pallas_call | solution.py:436
  189.9 9.4 %few_back.1 = (f32[64,1024]{1,0:T(8,128)S(1)}, f32[8,1024]{1,0:T(8,128)S(1)}, bf16[3,64,512]{2,1,0:T(8,128)(2,1)S(1)}, bf16[3,64,512]{2,1,0:T(8,128)(2,1)S(1)}) custom-call(bf16[64,1024]{1,0:T(8,128)(2,1)S(1)} %get-tuple-element.240.refs_0_.refs_4_.refs_5_, f32[64,1024]{1,0:T(8,128)S(1)} %get-tuple-element.241.refs_1_, f32[64,1024]{1,0:T(8,128)S(1)} %copy-done.60, ...), custom_call_target="tpu_custom_call" | custom-call | flops 1000 | bytes 1000 | tf_op jit(solution)/shard_map/few_back/pallas_call | solution.py:729
  205.5 13.0 %collective-permute-done.10.refs_1_ = bf16[256,1024]{1,0:T(8,128)(2,1)} collective-permute-done((bf16[256,1024]{1,0:T(8,128)(2,1)}, bf16[256,1024]{1,0:T(8,128)(2,1)}, u32[]{:S(2)}, u32[]{:S(2)}) %collective-permute-start.10) | collective-permute-done | bytes 524320 | tf_op jit(solution)/shard_map/ppermute | solution.py:807
  225.5 9.8 %learn_back.1 = (f32[1568,1024]{1,0:T(8,128)S(1)}, bf16[1568,1024]{1,0:T(8,128)(2,1)S(1)}, f32[8,1024]{1,0:T(8,128)S(1)}, f32[8,1024]{1,0:T(8,128)S(1)}) custom-call(f32[2,32,784]{2,1,0:T(8,128)S(1)} %copy-done.90, f32[64,1024]{1,0:T(8,128)S(1)} %copy-done.88, f32[1568,1024]{1,0:T(8,128)S(1)} %copy-done.13, f32[1,1024]{1,0:T(1,128)S(1)} %bitcast.78, ...), custom_call_target="tpu_custom_call" | custom-call | flops 1000 | bytes 1000 | tf_op jit(solution)/shard_map/learn_back/pallas_call | solution.py:580
  241.5 9.4 %grads.12 = bf16[2560,1024]{1,0:T(8,128)(2,1)S(1)} custom-call(s32[1]{0:T(128)} %constant.60.clone.1.refs_0_, bf16[1568,2048]{1,0:T(8,128)(2,1)S(1)} %copy-done.38, bf16[1568,1024]{1,0:T(8,128)(2,1)S(1)} %get-tuple-element.261.refs_2_, bf16[64,512]{1,0:T(8,128)(2,1)S(1)} %copy-done.101, bf16[64,1024]{1,0:T(8,128)(2,1)S(1)} %get-tuple-element.240.refs_0_.refs_4_.refs_5_), custom_call_target="tpu_custom_call" | custom-call | flops 1000 | bytes 1000 | tf_op jit(solution)/shard_map/grads/pallas_call | solution.py:1188
  251.0 4.1 grads.13
  255.1 4.5 collective-permute-done.12.refs_3_.refs_6_
  259.6 13.1 %grads.14 = (bf16[1280,1024]{1,0:T(8,128)(2,1)S(1)}, bf16[1280,1024]{1,0:T(8,128)(2,1)}) custom-call(s32[1]{0:T(128)} %bitcast.27.mines_ref.refs_0_.mine_ref, bf16[1568,2048]{1,0:T(8,128)(2,1)} %get-tuple-element.259.refs_1_, bf16[1568,1024]{1,0:T(8,128)(2,1)S(1)} %get-tuple-element.261.refs_2_, ...), custom_call_target="tpu_custom_call" | custom-call | flops 1000 | bytes 1000 | tf_op jit(solution)/shard_map/grads/pallas_call | solution.py:1188
  278.6 47.5 %feed_back.3 = (f32[1568,1024]{1,0:T(8,128)}, bf16[1568,1024]{1,0:T(8,128)(2,1)S(1)}, bf16[1568,1024]{1,0:T(8,128)(2,1)}, f32[8,1024]{1,0:T(8,128)S(1)}, bf16[15...) custom-call(f32[1568,1024]{1,0:T(8,128)} %copy-done.39, f32[1568,1024]{1,0:T(8,128)} %copy-done.14, ...), custom_call_target="tpu_custom_call" | custom-call | flops 1000 | bytes 1000 | tf_op jit(solution)/shard_map/feed_back/pallas_call | solution.py:436
  326.1 7.4 collective-permute-done.14.refs_1_
  336.0 3.9 fold.19
  344.8 14.0 %grads.15 = bf16[2560,1024]{1,0:T(8,128)(2,1)S(1)} custom-call(s32[1]{0:T(128)} %constant.60.clone.1.refs_0_, bf16[1568,1024]{1,0:T(8,128)(2,1)S(1)} %copy-done.1, bf16[1568,2048]{1,0:T(8,128)(2,1)} %get-tuple-element.276.refs_2_.refs_4_, bf16[1568,1024]{1,0:T(8,128)(2,1)S(1)} %copy-done.1, bf16[1568,2048]{1,0:T(8,128)(2,1)} %get-tuple-element.276.refs_2_.refs_4_, ...), custom_call_target="tpu_custom_call" | custom-call | flops 1000 | bytes 1000 | tf_op jit(solution)/shard_map/grads/pallas_call | solution.py:1188
  369.6 13.0 %attend_back.4.refs_2_ = bf16[3,1568,256]{2,1,0:T(8,128)(2,1)S(1)} custom-call(f32[8,208,1]{2,1,0:T(8,128)S(1)} %copy-done.11, bf16[3,1568,512]{2,1,0:T(8,128)(2,1)S(1)} %copy-done.9, bf16[1568,512]{1,0:T(8,128)(2,1)S(1)} %convolution_convert_fusion.1.grad_ref), custom_call_target="tpu_custom_call" | custom-call | flops 1000 | bytes 1000 | tf_op jit(solution)/shard_map/attend_back/pallas_call | solution.py:134
  382.6 4.4 grads.16
  393.8 9.8 %grads.18 = (bf16[768,1024]{1,0:T(8,128)(2,1)S(1)}, bf16[768,1024]{1,0:T(8,128)(2,1)S(1)}) custom-call(s32[1]{0:T(128)} %bitcast.27.mines_ref.refs_0_.mine_ref, bf16[1568,1024]{1,0:T(8,128)(2,1)S(1)} %copy-done.1, bf16[1568,2048]{1,0:T(8,128)(2,1)} %get-tuple-element.280.refs_2_, bf16[2560,1024]{1,0:T(8,128)(2,1)S(1)} %copy-done.5, ...), custom_call_target="tpu_custom_call" | custom-call | flops 1000 | bytes 1000 | tf_op jit(solution)/shard_map/grads/pallas_call | solution.py:1188
  409.0 7.6 grads.17
  427.0 12.6 %attend_back.5.refs_2_.refs_0_ = bf16[3,1568,256]{2,1,0:T(8,128)(2,1)S(1)} custom-call(f32[8,208,1]{2,1,0:T(8,128)S(1)} %copy-done.11, bf16[3,1568,512]{2,1,0:T(8,128)(2,1)S(1)} %bitcast.64, bf16[1568,512]{1,0:T(8,128)(2,1)S(1)} %convolution_convert_fusion.grad_ref), custom_call_target="tpu_custom_call" | custom-call | flops 1000 | bytes 1000 | tf_op jit(solution)/shard_map/attend_back/pallas_call | solution.py:134
  439.7 3.7 grads.19
  451.5 12.8 %attend_back.6.refs_2_.refs_3_ = bf16[3,1568,256]{2,1,0:T(8,128)(2,1)S(1)} custom-call(f32[8,208,1]{2,1,0:T(8,128)S(1)} %copy-done.11, bf16[3,1568,512]{2,1,0:T(8,128)(2,1)S(1)} %bitcast.66, bf16[1568,512]{1,0:T(8,128)(2,1)S(1)} %convolution_convert_fusion.1.grad_ref), custom_call_target="tpu_custom_call" | custom-call | flops 1000 | bytes 1000 | tf_op jit(solution)/shard_map/attend_back/pallas_call | solution.py:134
  465.0 15.8 %collective-permute-done.28.refs_1_ = bf16[384,1024]{1,0:T(8,128)(2,1)S(1)} collective-permute-done((bf16[384,1024]{1,0:T(8,128)(2,1)S(1)}, bf16[384,1024]{1,0:T(8,128)(2,1)S(1)}, u32[]{:S(2)}, u32[]{:S(2)}) %collective-permute-start.28) | collective-permute-done | bytes 786464 | tf_op jit(solution)/shard_map/ppermute | solution.py:807
  491.0 15.5 %collective-permute-done.25 = bf16[64,1536]{1,0:T(8,128)(2,1)S(1)} collective-permute-done((bf16[64,1536]{1,0:T(8,128)(2,1)S(1)}, bf16[64,1536]{1,0:T(8,128)(2,1)S(1)}, u32[]{:S(2)}, u32[]{:S(2)}) %collective-permute-start.25) | collective-permute-done | bytes 196640 | tf_op jit(solution)/shard_map/ppermute | solution.py:807
  512.3 13.0 %attend_back.7.refs_2_.refs_1_ = bf16[3,1568,256]{2,1,0:T(8,128)(2,1)S(1)} custom-call(f32[8,208,1]{2,1,0:T(8,128)S(1)} %copy-done.11, bf16[3,1568,512]{2,1,0:T(8,128)(2,1)S(1)} %bitcast.64, bf16[1568,512]{1,0:T(8,128)(2,1)S(1)} %convolution_convert_fusion.grad_ref), custom_call_target="tpu_custom_call" | custom-call | flops 1000 | bytes 1000 | tf_op jit(solution)/shard_map/attend_back/pallas_call | solution.py:134
  538.1 3.7 grads.21
  543.1 18.8 %collective-permute-done.35.refs_1_ = bf16[64,1536]{1,0:T(8,128)(2,1)S(1)} collective-permute-done((bf16[64,1536]{1,0:T(8,128)(2,1)}, bf16[64,1536]{1,0:T(8,128)(2,1)S(1)}, u32[]{:S(2)}, u32[]{:S(2)}) %collective-permute-start.35) | collective-permute-done | bytes 196640 | tf_op jit(solution)/shard_map/ppermute | solution.py:807
  571.0 22.9 %inward_back.1 = (f32[1568,1024]{1,0:T(8,128)}, f32[8,1024]{1,0:T(8,128)S(1)}) custom-call(bf16[3,1568,256]{2,1,0:T(8,128)(2,1)S(1)} %copy-done.18, bf16[3,1568,256]{2,1,0:T(8,128)(2,1)S(1)} %copy-done.22, bf16[3,1568,256]{2,1,0:T(8,128)(2,1)S(1)} %copy-done.16, bf16[3,1568,256]{2,1,0:T(8,128)(2,1)S(1)} %copy-done.20, bf16[3,1024,512]{2,1,0:T(8,128)(2,1)S(1)} %copy-done.35, ...), custom_call_target="tpu_custom_call" | custom-call | flops 1000 | bytes 1000 | tf_op jit(solution)/shard_map/inward_back/pallas_call | solution.py:640
  593.9 7.2 collective-permute-done.41
  615.1 5.4 collective-permute-done.43.refs_1_
  620.5 5.0 collective-permute-done.44.refs_1_
  631.2 3.8 collective-permute-done.48
  636.0 8.5 %collective-permute-done.47.refs_1_ = bf16[128,768]{1,0:T(8,128)(2,1)S(1)} collective-permute-done((bf16[128,768]{1,0:T(8,128)(2,1)S(1)}, bf16[128,768]{1,0:T(8,128)(2,1)S(1)}, u32[]{:S(2)}, u32[]{:S(2)}) %collective-permute-start.47) | collective-permute-done | bytes 196640 | tf_op jit(solution)/shard_map/ppermute | solution.py:807
  647.4 8.1 %collective-permute-done.51 = f32[13,1024]{1,0:T(8,128)S(1)} collective-permute-done((f32[13,1024]{1,0:T(8,128)S(1)}, f32[13,1024]{1,0:T(8,128)S(1)}, u32[]{:S(2)}, u32[]{:S(2)}) %collective-permute-start.51) | collective-permute-done | bytes 53280 | tf_op jit(solution)/shard_map/ppermute | solution.py:807
  664.4 4.4 maximum_convert_fusion
  671.6 3.9 collective-permute-done.57
  682.9 5.3 collective-permute-start.61
  688.4 29.6 %again.2 = (f32[1024,2048]{1,0:T(8,128)}, f32[2048,1024]{1,0:T(8,128)}) custom-call(bf16[1024,1024]{1,0:T(8,128)(2,1)S(1)} %copy-done.24, bf16[1024,1024]{1,0:T(8,128)(2,1)S(1)} %copy-done.36, bf16[1024,1024]{1,0:T(8,128)(2,1)} %collective-permute-done.18.refs_2_, bf16[1024,1024]{1,0:T(8,128)(2,1)} %collective-permute-done.59.refs_3_, ...), custom_call_target="tpu_custom_call" | custom-call | flops 1000 | bytes 1000 | tf_op jit(solution)/shard_map/again/pallas_call | solution.py:787
  718.0 10.4 %collective-permute-done.60.refs_1_ = bf16[256,768]{1,0:T(8,128)(2,1)S(1)} collective-permute-done((bf16[256,768]{1,0:T(8,128)(2,1)S(1)}, bf16[256,768]{1,0:T(8,128)(2,1)S(1)}, u32[]{:S(2)}, u32[]{:S(2)}) %collective-permute-start.60) | collective-permute-done | bytes 393248 | tf_op jit(solution)/shard_map/ppermute | solution.py:807
  735.4 29.8 %again.3 = (f32[1024,2048]{1,0:T(8,128)}, f32[2048,1024]{1,0:T(8,128)}) custom-call(bf16[1024,1024]{1,0:T(8,128)(2,1)S(1)} %copy-done.24, bf16[1024,1024]{1,0:T(8,128)(2,1)S(1)} %copy-done.36, bf16[1024,1024]{1,0:T(8,128)(2,1)} %collective-permute-done.18.refs_2_, ...), custom_call_target="tpu_custom_call", output_to_operand_aliasing={{0}: (6, {}), {1}: (7, {})} | custom-call | flops 1000 | bytes 1000 | tf_op jit(solution)/shard_map/again/pallas_call | solution.py:787
  765.1 6.0 spread.36
  (458 shorter events, 207.0 us)
Async XLA Ops:
  7.2 126.4 %all-gather.4.cloned.1.call-start = ((), (), s32[]{:S(2)}) async-start(), calls=%async_computation | async-start | bytes 2228224 | tf_op jit(solution)/shard_map/all_gather | solution.py:1504
  7.2 18.2 %collective-permute-start = (bf16[3,1024,512]{2,1,0:T(8,128)(2,1)}, bf16[3,1024,512]{2,1,0:T(8,128)(2,1)}, u32[]{:S(2)}, u32[]{:S(2)}) collective-permute-start(bf16[3,1024,512]{2,1,0:T(8,128)(2,1)} %refs_5_.6), channel_id=1, source_target_pairs={{1,0},{0,1},{3,2},{2,3},{5,4},{4,5},{7,6},{6,7},{9,8},{8,9},{11,10... | collective-permute-start | bytes 9437192 | tf_op jit(solution)/shard_map/ppermute | solution.py:1203
  7.7 53.0 %collective-permute-start.1 = (bf16[512,1024]{1,0:T(8,128)(2,1)}, bf16[512,1024]{1,0:T(8,128)(2,1)}, u32[]{:S(2)}, u32[]{:S(2)}) collective-permute-start(bf16[512,1024]{1,0:T(8,128)(2,1)} %refs_2_.2), channel_id=1, source_target_pairs={{1,0},{0,1},{3,2},{2,3},{5,4},{4,5},{7,6},{6,7},{9,8},{8,9},{11,10... | collective-permute-start | bytes 3145736 | tf_op jit(solution)/shard_map/ppermute | solution.py:1203
  7.8 70.8 %collective-permute-start.2 = (bf16[1024,2048]{1,0:T(8,128)(2,1)}, bf16[1024,2048]{1,0:T(8,128)(2,1)}, u32[]{:S(2)}, u32[]{:S(2)}) collective-permute-start(bf16[1024,2048]{1,0:T(8,128)(2,1)} %refs_5_.5), channel_id=1, source_target_pairs={{1,0},{0,1},{3,2},{2,3},{5,4},{4,5},{7,6},{6,7},{9,8},{8,9},{11,10... | collective-permute-start | bytes 12582920 | tf_op jit(solution)/shard_map/ppermute | solution.py:1203
  8.3 70.8 %collective-permute-start.3 = (bf16[2048,1024]{1,0:T(8,128)(2,1)}, bf16[2048,1024]{1,0:T(8,128)(2,1)}, u32[]{:S(2)}, u32[]{:S(2)}) collective-permute-start(bf16[2048,1024]{1,0:T(8,128)(2,1)} %refs_7_.3), channel_id=1, source_target_pairs={{1,0},{0,1},{3,2},{2,3},{5,4},{4,5},{7,6},{6,7},{9,8},{8,9},{11,10... | collective-permute-start | bytes 12582920 | tf_op jit(solution)/shard_map/ppermute | solution.py:1203
  10.0 645.6 %all-gather.6.cloned.1.call-start = ((), (), s32[]{:S(2)}) async-start(), calls=%async_computation.1 | async-start | bytes 5570560 | tf_op jit(solution)/shard_map/all_gather | solution.py:1091
  77.7 85.8 %collective-permute-start.6 = (bf16[1024,2048]{1,0:T(8,128)(2,1)}, bf16[1024,2048]{1,0:T(8,128)(2,1)}, u32[]{:S(2)}, u32[]{:S(2)}) collective-permute-start(bf16[1024,2048]{1,0:T(8,128)(2,1)} %refs_4_.11), channel_id=1, source_target_pairs={{1,0},{0,1},{3,2},{2,3},{5,4},{4,5},{7,6},{6,7},{9,8},{8,9},{11,10... | collective-permute-start | bytes 12582920 | tf_op jit(solution)/shard_map/ppermute | solution.py:1203
  78.1 85.4 %collective-permute-start.7 = (bf16[2048,1024]{1,0:T(8,128)(2,1)}, bf16[2048,1024]{1,0:T(8,128)(2,1)}, u32[]{:S(2)}, u32[]{:S(2)}) collective-permute-start(bf16[2048,1024]{1,0:T(8,128)(2,1)} %refs_5_.8), channel_id=1, source_target_pairs={{1,0},{0,1},{3,2},{2,3},{5,4},{4,5},{7,6},{6,7},{9,8},{8,9},{11,10... | collective-permute-start | bytes 12582920 | tf_op jit(solution)/shard_map/ppermute | solution.py:1203
  78.2 64.2 %collective-permute-start.4 = (bf16[3,1024,512]{2,1,0:T(8,128)(2,1)}, bf16[3,1024,512]{2,1,0:T(8,128)(2,1)}, u32[]{:S(2)}, u32[]{:S(2)}) collective-permute-start(bf16[3,1024,512]{2,1,0:T(8,128)(2,1)} %refs_7_.2), channel_id=1, source_target_pairs={{1,0},{0,1},{3,2},{2,3},{5,4},{4,5},{7,6},{6,7},{9,8},{8,9},{11,10... | collective-permute-start | bytes 9437192 | tf_op jit(solution)/shard_map/ppermute | solution.py:1203
  78.6 63.8 %collective-permute-start.5 = (bf16[512,1024]{1,0:T(8,128)(2,1)}, bf16[512,1024]{1,0:T(8,128)(2,1)}, u32[]{:S(2)}, u32[]{:S(2)}) collective-permute-start(bf16[512,1024]{1,0:T(8,128)(2,1)} %refs_9_), channel_id=1, source_target_pairs={{1,0},{0,1},{3,2},{2,3},{5,4},{4,5},{7,6},{6,7},{9,8},{8,9},{11,10... | collective-permute-start | bytes 3145736 | tf_op jit(solution)/shard_map/ppermute | solution.py:1203
  161.7 26.2 %collective-permute-start.9 = (bf16[128,1024]{1,0:T(8,128)(2,1)}, bf16[128,1024]{1,0:T(8,128)(2,1)}, u32[]{:S(2)}, u32[]{:S(2)}) collective-permute-start(bf16[128,1024]{1,0:T(8,128)(2,1)} %spread.19.refs_0_), channel_id=1, source_target_pairs={{0,4},{2,6},{4,0},{6,2},{8,12},{10,14},{12,8},{14,10},{16,20},{18,... | collective-permute-start | bytes 786440 | tf_op jit(solution)/shard_map/ppermute | solution.py:807
  203.8 34.9 %collective-permute-start.11 = (bf16[1024,1536]{1,0:T(8,128)(2,1)}, bf16[1024,1536]{1,0:T(8,128)(2,1)}, u32[]{:S(2)}, u32[]{:S(2)}) collective-permute-start(bf16[1024,1536]{1,0:T(8,128)(2,1)} %grads.11), channel_id=1, source_target_pairs={{0,1},{1,0},{2,3},{3,2},{4,5},{5,4},{6,7},{7,6},{8,9},{9,8},{10,11... | collective-permute-start | bytes 9437192 | tf_op jit(solution)/shard_map/ppermute | solution.py:1209
  274.2 59.3 %collective-permute-start.14 = (bf16[1280,1024]{1,0:T(8,128)(2,1)}, bf16[1280,1024]{1,0:T(8,128)(2,1)}, u32[]{:S(2)}, u32[]{:S(2)}) collective-permute-start(bf16[1280,1024]{1,0:T(8,128)(2,1)} %get-tuple-element.263), channel_id=1, source_target_pairs={{0,4},{2,6},{4,0},{6,2},{8,12},{10,14},{12,8},{14,10},{16,20},{18,... | collective-permute-start | bytes 7864328 | tf_op jit(solution)/shard_map/ppermute | solution.py:807
  274.3 51.8 %collective-permute-start.13 = (bf16[512,1536]{1,0:T(8,128)(2,1)}, bf16[512,1536]{1,0:T(8,128)(2,1)}, u32[]{:S(2)}, u32[]{:S(2)}) collective-permute-start(bf16[512,1536]{1,0:T(8,128)(2,1)} %get-tuple-element.258), channel_id=1, source_target_pairs={{0,2},{2,0},{4,6},{6,4},{8,10},{10,8},{12,14},{14,12},{16,18},{18,... | collective-permute-start | bytes 4718600 | tf_op jit(solution)/shard_map/ppermute | solution.py:807
  276.0 50.1 %collective-permute-start.15 = (bf16[512,1024]{1,0:T(8,128)(2,1)}, bf16[512,1024]{1,0:T(8,128)(2,1)}, u32[]{:S(2)}, u32[]{:S(2)}) collective-permute-start(bf16[512,1024]{1,0:T(8,128)(2,1)} %spread.21.refs_0_), channel_id=1, source_target_pairs={{0,16},{2,18},{4,20},{6,22},{8,24},{10,26},{12,28},{14,30},{16,0},... | collective-permute-start | bytes 3145736 | tf_op jit(solution)/shard_map/ppermute | solution.py:807
  361.2 25.8 %collective-permute-start.19 = (bf16[2560,1024]{1,0:T(8,128)(2,1)}, bf16[2560,1024]{1,0:T(8,128)(2,1)S(1)}, u32[]{:S(2)}, u32[]{:S(2)}) collective-permute-start(bf16[2560,1024]{1,0:T(8,128)(2,1)} %copy-done.40), channel_id=1, source_target_pairs={{0,1},{1,0},{2,3},{3,2},{4,5},{5,4},{6,7},{7,6},{8,9},{9,8},{10,11... | collective-permute-start | bytes 15728648 | tf_op jit(solution)/shard_map/ppermute | solution.py:1209
  361.2 56.3 %collective-permute-start.18 = (bf16[1024,1024]{1,0:T(8,128)(2,1)S(1)}, bf16[1024,1024]{1,0:T(8,128)(2,1)}, u32[]{:S(2)}, u32[]{:S(2)}) collective-permute-start(bf16[1024,1024]{1,0:T(8,128)(2,1)S(1)} %spread.22.refs_0_), channel_id=1, source_target_pairs={{1,0},{0,1},{3,2},{2,3},{5,4},{4,5},{7,6},{6,7},{9,8},{8,9},{11,10... | collective-permute-start | bytes 6291464 | tf_op jit(solution)/shard_map/ppermute | solution.py:1203
  361.7 55.8 %collective-permute-start.16 = (bf16[256,1536]{1,0:T(8,128)(2,1)}, bf16[256,1536]{1,0:T(8,128)(2,1)}, u32[]{:S(2)}, u32[]{:S(2)}) collective-permute-start(bf16[256,1536]{1,0:T(8,128)(2,1)} %get-tuple-element.270), channel_id=1, source_target_pairs={{0,4},{2,6},{4,0},{6,2},{8,12},{10,14},{12,8},{14,10},{16,20},{18,... | collective-permute-start | bytes 2359304 | tf_op jit(solution)/shard_map/ppermute | solution.py:807
  362.0 55.5 %collective-permute-start.17 = (bf16[640,1024]{1,0:T(8,128)(2,1)}, bf16[640,1024]{1,0:T(8,128)(2,1)}, u32[]{:S(2)}, u32[]{:S(2)}) collective-permute-start(bf16[640,1024]{1,0:T(8,128)(2,1)} %get-tuple-element.273), channel_id=1, source_target_pairs={{0,2},{2,0},{4,6},{6,4},{8,10},{10,8},{12,14},{14,12},{16,18},{18,... | collective-permute-start | bytes 3932168 | tf_op jit(solution)/shard_map/ppermute | solution.py:807
  387.0 52.7 %collective-permute-start.24 = (bf16[1024,768]{1,0:T(8,128)(2,1)}, bf16[1024,768]{1,0:T(8,128)(2,1)S(1)}, u32[]{:S(2)}, u32[]{:S(2)}) collective-permute-start(bf16[1024,768]{1,0:T(8,128)(2,1)} %grads.16), channel_id=1, source_target_pairs={{0,1},{1,0},{2,3},{3,2},{4,5},{5,4},{6,7},{7,6},{8,9},{9,8},{10,11... | collective-permute-start | bytes 4718600 | tf_op jit(solution)/shard_map/ppermute | solution.py:1209
  404.7 41.6 %collective-permute-start.23 = (bf16[768,1024]{1,0:T(8,128)(2,1)}, bf16[768,1024]{1,0:T(8,128)(2,1)S(1)}, u32[]{:S(2)}, u32[]{:S(2)}) collective-permute-start(bf16[768,1024]{1,0:T(8,128)(2,1)} %copy-done.118), channel_id=1, source_target_pairs={{0,4},{2,6},{4,0},{6,2},{8,12},{10,14},{12,8},{14,10},{16,20},{18,... | collective-permute-start | bytes 4718600 | tf_op jit(solution)/shard_map/ppermute | solution.py:807
  417.5 28.8 %collective-permute-start.22 = (bf16[512,1024]{1,0:T(8,128)(2,1)}, bf16[512,1024]{1,0:T(8,128)(2,1)S(1)}, u32[]{:S(2)}, u32[]{:S(2)}) collective-permute-start(bf16[512,1024]{1,0:T(8,128)(2,1)} %get-tuple-element.282), channel_id=1, source_target_pairs={{0,2},{2,0},{4,6},{6,4},{8,10},{10,8},{12,14},{14,12},{16,18},{18,... | collective-permute-start | bytes 3145736 | tf_op jit(solution)/shard_map/ppermute | solution.py:807
  420.1 26.2 %collective-permute-start.21 = (bf16[320,1024]{1,0:T(8,128)(2,1)}, bf16[320,1024]{1,0:T(8,128)(2,1)}, u32[]{:S(2)}, u32[]{:S(2)}) collective-permute-start(bf16[320,1024]{1,0:T(8,128)(2,1)} %get-tuple-element.291), channel_id=1, source_target_pairs={{0,8},{2,10},{4,12},{6,14},{8,0},{10,2},{12,4},{14,6},{16,24},{18,... | collective-permute-start | bytes 1966088 | tf_op jit(solution)/shard_map/ppermute | solution.py:807
  424.6 21.7 %collective-permute-start.20 = (bf16[128,1536]{1,0:T(8,128)(2,1)}, bf16[128,1536]{1,0:T(8,128)(2,1)}, u32[]{:S(2)}, u32[]{:S(2)}) collective-permute-start(bf16[128,1536]{1,0:T(8,128)(2,1)} %get-tuple-element.288), channel_id=1, source_target_pairs={{0,8},{2,10},{4,12},{6,14},{8,0},{10,2},{12,4},{14,6},{16,24},{18,... | collective-permute-start | bytes 1179656 | tf_op jit(solution)/shard_map/ppermute | solution.py:807
  444.3 20.6 %collective-permute-start.29 = (bf16[512,768]{1,0:T(8,128)(2,1)}, bf16[512,768]{1,0:T(8,128)(2,1)S(1)}, u32[]{:S(2)}, u32[]{:S(2)}) collective-permute-start(bf16[512,768]{1,0:T(8,128)(2,1)} %copy-done.119), channel_id=1, source_target_pairs={{0,2},{2,0},{4,6},{6,4},{8,10},{10,8},{12,14},{14,12},{16,18},{18,... | collective-permute-start | bytes 2359304 | tf_op jit(solution)/shard_map/ppermute | solution.py:807
  446.8 34.0 %collective-permute-start.28 = (bf16[384,1024]{1,0:T(8,128)(2,1)S(1)}, bf16[384,1024]{1,0:T(8,128)(2,1)S(1)}, u32[]{:S(2)}, u32[]{:S(2)}) collective-permute-start(bf16[384,1024]{1,0:T(8,128)(2,1)S(1)} %get-tuple-element.306), channel_id=1, source_target_pairs={{0,2},{2,0},{4,6},{6,4},{8,10},{10,8},{12,14},{14,12},{16,18},{18,... | collective-permute-start | bytes 2359304 | tf_op jit(solution)/shard_map/ppermute | solution.py:807
  481.0 27.0 %collective-permute-start.31 = (bf16[192,1024]{1,0:T(8,128)(2,1)S(1)}, bf16[192,1024]{1,0:T(8,128)(2,1)S(1)}, u32[]{:S(2)}, u32[]{:S(2)}) collective-permute-start(bf16[192,1024]{1,0:T(8,128)(2,1)S(1)} %get-tuple-element.312), channel_id=1, source_target_pairs={{0,8},{2,10},{4,12},{6,14},{8,0},{10,2},{12,4},{14,6},{16,24},{18,... | collective-permute-start | bytes 1179656 | tf_op jit(solution)/shard_map/ppermute | solution.py:807
  482.3 24.2 %collective-permute-start.26 = (bf16[160,1024]{1,0:T(8,128)(2,1)S(1)}, bf16[160,1024]{1,0:T(8,128)(2,1)S(1)}, u32[]{:S(2)}, u32[]{:S(2)}) collective-permute-start(bf16[160,1024]{1,0:T(8,128)(2,1)S(1)} %get-tuple-element.300), channel_id=1, source_target_pairs={{0,16},{2,18},{4,20},{6,22},{8,24},{10,26},{12,28},{14,30},{16,0},... | collective-permute-start | bytes 983048 | tf_op jit(solution)/shard_map/ppermute | solution.py:807
  485.1 23.0 %collective-permute-start.30 = (bf16[128,1024]{1,0:T(8,128)(2,1)S(1)}, bf16[128,1024]{1,0:T(8,128)(2,1)S(1)}, u32[]{:S(2)}, u32[]{:S(2)}) collective-permute-start(bf16[128,1024]{1,0:T(8,128)(2,1)S(1)} %get-tuple-element.309), channel_id=1, source_target_pairs={{0,8},{2,10},{4,12},{6,14},{8,0},{10,2},{12,4},{14,6},{16,24},{18,... | collective-permute-start | bytes 786440 | tf_op jit(solution)/shard_map/ppermute | solution.py:807
  485.9 20.6 %collective-permute-start.25 = (bf16[64,1536]{1,0:T(8,128)(2,1)S(1)}, bf16[64,1536]{1,0:T(8,128)(2,1)S(1)}, u32[]{:S(2)}, u32[]{:S(2)}) collective-permute-start(bf16[64,1536]{1,0:T(8,128)(2,1)S(1)} %get-tuple-element.297), channel_id=1, source_target_pairs={{0,16},{2,18},{4,20},{6,22},{8,24},{10,26},{12,28},{14,30},{16,0},... | collective-permute-start | bytes 589832 | tf_op jit(solution)/shard_map/ppermute | solution.py:807
  486.5 40.2 %collective-permute-start.34 = (bf16[256,768]{1,0:T(8,128)(2,1)S(1)}, bf16[256,768]{1,0:T(8,128)(2,1)S(1)}, u32[]{:S(2)}, u32[]{:S(2)}) collective-permute-start(bf16[256,768]{1,0:T(8,128)(2,1)S(1)} %get-tuple-element.315), channel_id=1, source_target_pairs={{0,4},{2,6},{4,0},{6,2},{8,12},{10,14},{12,8},{14,10},{16,20},{18,... | collective-permute-start | bytes 1179656 | tf_op jit(solution)/shard_map/ppermute | solution.py:807
  508.2 19.3 %collective-permute-start.32 = (bf16[64,1024]{1,0:T(8,128)(2,1)S(1)}, bf16[64,1024]{1,0:T(8,128)(2,1)S(1)}, u32[]{:S(2)}, u32[]{:S(2)}) collective-permute-start(bf16[64,1024]{1,0:T(8,128)(2,1)S(1)} %get-tuple-element.324), channel_id=1, source_target_pairs={{0,16},{2,18},{4,20},{6,22},{8,24},{10,26},{12,28},{14,30},{16,0},... | collective-permute-start | bytes 393224 | tf_op jit(solution)/shard_map/ppermute | solution.py:807
  510.3 17.2 %collective-permute-start.33 = (bf16[96,1024]{1,0:T(8,128)(2,1)S(1)}, bf16[96,1024]{1,0:T(8,128)(2,1)S(1)}, u32[]{:S(2)}, u32[]{:S(2)}) collective-permute-start(bf16[96,1024]{1,0:T(8,128)(2,1)S(1)} %get-tuple-element.327), channel_id=1, source_target_pairs={{0,16},{2,18},{4,20},{6,22},{8,24},{10,26},{12,28},{14,30},{16,0},... | collective-permute-start | bytes 589832 | tf_op jit(solution)/shard_map/ppermute | solution.py:807
  528.4 33.5 %collective-permute-start.36 = (bf16[160,1024]{1,0:T(8,128)(2,1)S(1)}, bf16[160,1024]{1,0:T(8,128)(2,1)S(1)}, u32[]{:S(2)}, u32[]{:S(2)}) collective-permute-start(bf16[160,1024]{1,0:T(8,128)(2,1)S(1)} %add_convert_fusion.refs_0_), channel_id=1, source_target_pairs={{0,16},{2,18},{4,20},{6,22},{8,24},{10,26},{12,28},{14,30},{16,0},... | collective-permute-start | bytes 983048 | tf_op jit(solution)/shard_map/ppermute | solution.py:807
  530.4 31.5 %collective-permute-start.35 = (bf16[64,1536]{1,0:T(8,128)(2,1)}, bf16[64,1536]{1,0:T(8,128)(2,1)S(1)}, u32[]{:S(2)}, u32[]{:S(2)}) collective-permute-start(bf16[64,1536]{1,0:T(8,128)(2,1)} %add_convert_fusion.2.refs_0_), channel_id=1, source_target_pairs={{0,16},{2,18},{4,20},{6,22},{8,24},{10,26},{12,28},{14,30},{16,0},... | collective-permute-start | bytes 589832 | tf_op jit(solution)/shard_map/ppermute | solution.py:807
  533.6 28.3 %collective-permute-start.37 = (bf16[128,768]{1,0:T(8,128)(2,1)S(1)}, bf16[128,768]{1,0:T(8,128)(2,1)S(1)}, u32[]{:S(2)}, u32[]{:S(2)}) collective-permute-start(bf16[128,768]{1,0:T(8,128)(2,1)S(1)} %get-tuple-element.336), channel_id=1, source_target_pairs={{0,8},{2,10},{4,12},{6,14},{8,0},{10,2},{12,4},{14,6},{16,24},{18,... | collective-permute-start | bytes 589832 | tf_op jit(solution)/shard_map/ppermute | solution.py:807
  541.9 62.7 %collective-permute-start.42 = (bf16[512,768]{1,0:T(8,128)(2,1)S(1)}, bf16[512,768]{1,0:T(8,128)(2,1)S(1)}, u32[]{:S(2)}, u32[]{:S(2)}) collective-permute-start(bf16[512,768]{1,0:T(8,128)(2,1)S(1)} %get-tuple-element.340), channel_id=1, source_target_pairs={{0,4},{2,6},{4,0},{6,2},{8,12},{10,14},{12,8},{14,10},{16,20},{18,... | collective-permute-start | bytes 2359304 | tf_op jit(solution)/shard_map/ppermute | solution.py:807
  562.0 41.7 %collective-permute-start.40 = (bf16[320,1024]{1,0:T(8,128)(2,1)S(1)}, bf16[320,1024]{1,0:T(8,128)(2,1)S(1)}, u32[]{:S(2)}, u32[]{:S(2)}) collective-permute-start(bf16[320,1024]{1,0:T(8,128)(2,1)S(1)} %spread.24.refs_0_), channel_id=1, source_target_pairs={{0,8},{2,10},{4,12},{6,14},{8,0},{10,2},{12,4},{14,6},{16,24},{18,... | collective-permute-start | bytes 1966088 | tf_op jit(solution)/shard_map/ppermute | solution.py:807
  562.3 40.7 %collective-permute-start.39 = (bf16[128,1536]{1,0:T(8,128)(2,1)S(1)}, bf16[128,1536]{1,0:T(8,128)(2,1)S(1)}, u32[]{:S(2)}, u32[]{:S(2)}) collective-permute-start(bf16[128,1536]{1,0:T(8,128)(2,1)S(1)} %spread.23.refs_0_), channel_id=1, source_target_pairs={{0,8},{2,10},{4,12},{6,14},{8,0},{10,2},{12,4},{14,6},{16,24},{18,... | collective-permute-start | bytes 1179656 | tf_op jit(solution)/shard_map/ppermute | solution.py:807
  564.4 36.7 %collective-permute-start.41 = (bf16[64,768]{1,0:T(8,128)(2,1)S(1)}, bf16[64,768]{1,0:T(8,128)(2,1)S(1)}, u32[]{:S(2)}, u32[]{:S(2)}) collective-permute-start(bf16[64,768]{1,0:T(8,128)(2,1)S(1)} %get-tuple-element.346), channel_id=1, source_target_pairs={{0,16},{2,18},{4,20},{6,22},{8,24},{10,26},{12,28},{14,30},{16,0},... | collective-permute-start | bytes 294920 | tf_op jit(solution)/shard_map/ppermute | solution.py:807
  605.6 19.9 %collective-permute-start.44 = (bf16[256,768]{1,0:T(8,128)(2,1)}, bf16[256,768]{1,0:T(8,128)(2,1)}, u32[]{:S(2)}, u32[]{:S(2)}) collective-permute-start(bf16[256,768]{1,0:T(8,128)(2,1)} %get-tuple-element.362), channel_id=1, source_target_pairs={{0,2},{2,0},{4,6},{6,4},{8,10},{10,8},{12,14},{14,12},{16,18},{18,... | collective-permute-start | bytes 1179656 | tf_op jit(solution)/shard_map/ppermute | solution.py:807
  630.7 40.9 %collective-permute-start.55 = (bf16[640,1024]{1,0:T(8,128)(2,1)}, bf16[640,1024]{1,0:T(8,128)(2,1)}, u32[]{:S(2)}, u32[]{:S(2)}) collective-permute-start(bf16[640,1024]{1,0:T(8,128)(2,1)} %spread.26.refs_0_), channel_id=1, source_target_pairs={{0,2},{2,0},{4,6},{6,4},{8,10},{10,8},{12,14},{14,12},{16,18},{18,... | collective-permute-start | bytes 3932168 | tf_op jit(solution)/shard_map/ppermute | solution.py:807
  647.4 41.0 %collective-permute-start.59 = (bf16[1024,1024]{1,0:T(8,128)(2,1)S(1)}, bf16[1024,1024]{1,0:T(8,128)(2,1)}, u32[]{:S(2)}, u32[]{:S(2)}) collective-permute-start(bf16[1024,1024]{1,0:T(8,128)(2,1)S(1)} %copy-done.36), channel_id=1, source_target_pairs={{1,0},{0,1},{3,2},{2,3},{5,4},{4,5},{7,6},{6,7},{9,8},{8,9},{11,10... | collective-permute-start | bytes 6291464 | tf_op jit(solution)/shard_map/ppermute | solution.py:1203
  679.2 85.9 %collective-permute-start.62 = (bf16[1280,1024]{1,0:T(8,128)(2,1)S(1)}, bf16[1280,1024]{1,0:T(8,128)(2,1)S(1)}, u32[]{:S(2)}, u32[]{:S(2)}) collective-permute-start(bf16[1280,1024]{1,0:T(8,128)(2,1)S(1)} %spread.33.refs_0_), channel_id=1, source_target_pairs={{0,4},{2,6},{4,0},{6,2},{8,12},{10,14},{12,8},{14,10},{16,20},{18,... | collective-permute-start | bytes 7864328 | tf_op jit(solution)/shard_map/ppermute | solution.py:807
  682.9 82.3 %collective-permute-start.61 = (bf16[512,1536]{1,0:T(8,128)(2,1)S(1)}, bf16[512,1536]{1,0:T(8,128)(2,1)S(1)}, u32[]{:S(2)}, u32[]{:S(2)}) collective-permute-start(bf16[512,1536]{1,0:T(8,128)(2,1)S(1)} %spread.32.refs_0_), channel_id=1, source_target_pairs={{0,2},{2,0},{4,6},{6,4},{8,10},{10,8},{12,14},{14,12},{16,18},{18,... | collective-permute-start | bytes 4718600 | tf_op jit(solution)/shard_map/ppermute | solution.py:807
  688.3 40.1 %collective-permute-start.60 = (bf16[256,768]{1,0:T(8,128)(2,1)S(1)}, bf16[256,768]{1,0:T(8,128)(2,1)S(1)}, u32[]{:S(2)}, u32[]{:S(2)}) collective-permute-start(bf16[256,768]{1,0:T(8,128)(2,1)S(1)} %spread.31.refs_0_), channel_id=1, source_target_pairs={{0,2},{2,0},{4,6},{6,4},{8,10},{10,8},{12,14},{14,12},{16,18},{18,... | collective-permute-start | bytes 1179656 | tf_op jit(solution)/shard_map/ppermute | solution.py:807
  728.5 36.7 %collective-permute-start.63 = (bf16[512,768]{1,0:T(8,128)(2,1)S(1)}, bf16[512,768]{1,0:T(8,128)(2,1)S(1)}, u32[]{:S(2)}, u32[]{:S(2)}) collective-permute-start(bf16[512,768]{1,0:T(8,128)(2,1)S(1)} %spread.34.refs_2_), channel_id=1, source_target_pairs={{0,4},{2,6},{4,0},{6,2},{8,12},{10,14},{12,8},{14,10},{16,20},{18,... | collective-permute-start | bytes 2359304 | tf_op jit(solution)/shard_map/ppermute | solution.py:807
  729.2 44.8 %collective-permute-start.58 = (bf16[512,768]{1,0:T(8,128)(2,1)S(1)}, bf16[512,768]{1,0:T(8,128)(2,1)S(1)}, u32[]{:S(2)}, u32[]{:S(2)}) collective-permute-start(bf16[512,768]{1,0:T(8,128)(2,1)S(1)} %spread.29.refs_0_), channel_id=1, source_target_pairs={{0,2},{2,0},{4,6},{6,4},{8,10},{10,8},{12,14},{14,12},{16,18},{18,... | collective-permute-start | bytes 2359304 | tf_op jit(solution)/shard_map/ppermute | solution.py:807
  (143 other events, 1467.4 us)
Sparse Core Ops, SparseCore 0:
  11.4 63.4 all-gather.3
  528.5 124.3 all-gather.5

commit v2 on v1

--- a/solution.py
+++ b/solution.py
@@ -142,7 +142,7 @@
         out_specs=triple if grads else plane,
         out_shape=jax.ShapeDtypeStruct((3,) + shape if grads else shape, jnp.bfloat16),
         compiler_params=params(14),
-        cost_estimate=light(),
+        cost_estimate=light() if grads else cost(16 * rows * 1024 * columns, 8 * rows * columns),
         name="attend_back" if grads else "attend",
     )(bias, projected, *grads)
     return out[..., : rows - spare, :] if spare else out
@@ -242,6 +242,10 @@
     return pl.CostEstimate(flops=1000, bytes_accessed=1000, transcendentals=0)
 
 
+def cost(flops, moved):
+    return pl.CostEstimate(flops=int(flops), bytes_accessed=int(moved), transcendentals=0)
+
+
 def params(mebibytes):
     return pltpu.CompilerParams(vmem_limit_bytes=mebibytes * 1024 * 1024)
 
@@ -274,7 +278,7 @@
         out_specs=line,
         out_shape=jax.ShapeDtypeStruct((rows, width), jnp.bfloat16),
         compiler_params=params(8),
-        cost_estimate=light(),
+        cost_estimate=cost(0, 8 * rows * width),
         name="norm",
     )(inputs, gain)
 
@@ -312,7 +316,7 @@
             jax.ShapeDtypeStruct((rows, width), jnp.bfloat16),
         ],
         compiler_params=params(16),
-        cost_estimate=light(),
+        cost_estimate=cost(4 * rows * width * width, 12 * rows * width),
         name="outward",
     )(*contexts, *weights, inputs, gain)
 
@@ -332,7 +336,7 @@
 
         @pl.when((chunk >= share * per) & (chunk < (share + 1) * per))
         def _():
-            ranges = spans(second_ref.shape[0], 400)
+            ranges = spans(second_ref.shape[0], 272)
             up, down = up_refs[share][...], down_refs[share][...]
             ahead = mm(second_ref[ranges[0][0] : ranges[0][1], :], up)
             for at, (start, end) in enumerate(ranges):
@@ -362,7 +366,7 @@
 
 def feed(second, hidden, ups, downs):
     rows, shares = second.shape[0], len(ups)
-    block, width, units, size, per = ff_sizes(rows, ups, 1024)
+    block, width, units, size, per = ff_sizes(rows, ups, 512)
     line = pl.BlockSpec((block, width), lambda at, chunk: (at, 0))
     piece = [share_spec((block, size), 2, share, per) for share in range(shares)]
     out = pl.pallas_call(
@@ -375,7 +379,7 @@
         out_shape=[jax.ShapeDtypeStruct((rows, width), jnp.float32)]
         + [jax.ShapeDtypeStruct((rows, units), jnp.bfloat16)] * (2 * shares),
         compiler_params=params(56),
-        cost_estimate=light(),
+        cost_estimate=cost(5 * rows * width * units * shares * (rows > 128), 20 * rows * width),
         name="feed",
     )(second, hidden, *ups, *downs)
     return out[0], out[1 : 1 + shares], out[1 + shares :]
@@ -511,7 +515,7 @@
         ],
         scratch_shapes=[pltpu.VMEM((span, width), jnp.bfloat16)] * 2,
         compiler_params=params(24),
-        cost_estimate=light(),
+        cost_estimate=cost(0, 12 * rows * width),
         name="learn",
     )(bias, patched, gain, maps)
 
@@ -743,19 +747,23 @@
 def again_kernel(rows_refs, up_ref, down_ref, up_grad_ref, down_grad_ref):
     def work(second_ref, grad_ref, begin):
         second, grad = second_ref[...], grad_ref[...]
-        up, down = up_ref[...], down_ref[...]
+        size = up_ref.shape[1]
+        tile = min(256, size)
+
+        def products(start):
+            span = slice(start, start + tile)
+            return mm(second, up_ref[:, span]), nt(grad, down_ref[span, :])
+
         actives, inners = [], []
-        ranges = spans(second.shape[0], 256)
-        ahead = mm(second[ranges[0][0] : ranges[0][1]], up)
-        for at, (start, end) in enumerate(ranges):
-            upward = ahead
-            grad_active = nt(grad[start:end], down)
-            if at + 1 < len(ranges):
-                ahead = mm(second[ranges[at + 1][0] : ranges[at + 1][1]], up)
+        ahead = products(0)
+        for start in range(0, size, tile):
+            upward, grad_active = ahead
+            if start + tile < size:
+                ahead = products(start + tile)
             active, slope = gelu_pair(upward)
             actives.append(active)
             inners.append((grad_active * slope.astype(jnp.float32)).astype(jnp.bfloat16))
-        active, inner = jnp.concatenate(actives), jnp.concatenate(inners)
+        active, inner = jnp.concatenate(actives, axis=1), jnp.concatenate(inners, axis=1)
         if begin:
             down_grad_ref[...] = tn(active, grad)
             up_grad_ref[...] = tn(second, inner)
@@ -1002,14 +1010,6 @@
             self.got = swap(self.sent, bit)
 
 
-def in_order(gathered, order):
-    count = len(order)
-    rows, width = gathered.shape[1:]
-    split = gathered.reshape((2,) * count + (rows, width))
-    axes = tuple(count - 1 - bit for bit in order) + (count, count + 1)
-    return jnp.transpose(split, axes).reshape(-1, width)
-
-
 class Gather:
     def __init__(self, rows):
         self.step, self.length = 0, lax.axis_size("dp").bit_length()
@@ -1040,7 +1040,7 @@
         if self.step < near_by:
             self.got = give(self.step + 1)(self.mine)
         else:
-            self.got = swap(self.kept, self.step - near_by)
+            self.got = swap(self.kept, self.length - 1 - self.step)
 
     def done(self):
         return self.step == self.length
@@ -1053,8 +1053,8 @@
 
 
 class Clock:
-    def __init__(self, plan, sets):
-        self.plan, self.sets = plan, dict(sets)
+    def __init__(self, plan):
+        self.plan = plan
         self.flows, self.begun, self.past, self.whole = {}, [], [], {}
 
     def begin(self, name, flow):
@@ -1078,18 +1078,9 @@
             self.whole[key] = got.pop(0)
         for flow in ended:
             flow.got = got.pop(0)
-        for key, members in list(self.sets.items()):
-            if all(name in self.flows and self.flows[name].done() for name in members):
-                self.begun.append(self.gather(key))
         value = meet(value, self.begun + [flow.sent for flow in flows])[0]
         self.begun = []
         return value
-
-    def gather(self, key):
-        kept = [self.flows[name].kept for name in self.sets.pop(key)]
-        own = jnp.concatenate(kept) if len(kept) > 1 else kept[0]
-        self.whole[key] = lax.all_gather(own, "dp")
-        return own
 
     def end(self, names):
         flows = [self.flows[name] for name in names]
@@ -1097,14 +1088,6 @@
             for flow in flows:
                 if not flow.done():
                     flow.advance()
-
-    def rows(self, names, whole):
-        pieces, at = [], 0
-        for flow in (self.flows[name] for name in names):
-            own = flow.kept.shape[0]
-            pieces.append(in_order(whole[:, at : at + own], flow.order))
-            at += own
-        return pieces
 
 
 def grads_kernel(cuts, count, *refs):
@@ -1302,7 +1285,9 @@
     return tuple(total_over_all([low(term) for term in terms]) for terms in pairs)
 
 
-def lower_backward(grad_out, grad_mix, stored, weights, bias, clock, upper_sources):
+def lower_backward(
+    grad_out, grad_mix, stored, weights, bias, clock, upper_sources, between
+):
     gain_one, weight_qkv, weight_out, gain_two, weight_up, weight_down = weights
     inputs, hidden, across, second, projections, contexts, actives, slopes = stored
     shares = range(len(weight_qkv))
@@ -1355,10 +1340,11 @@
                 others = give(at)(others)
             elif quick:
                 sources = project_sources(across, back, others)
-                order = turned if group else bits
-                halves = grads(sources, 3 * wide // groups, my_bit(order[0]))
+                halves = grads(sources, 3 * wide // groups, my_bit(bits[0]))
                 clock.past += halves
-                clock.begin(f"project-{group}", Flow(halves, order, True))
+                clock.begin(f"project-{group}", Flow(halves, bits, True))
+                if group == 0:
+                    between(clock)
             if quick and at and group == 0:
                 grad_branch = clock("up0", grad_branch)
                 for panel in panels:
@@ -1371,7 +1357,7 @@
                     order = turned if panel % 2 else bits
                     halves = grads(sources, width, my_bit(order[0]))
                     clock.past += halves
-                    clock.begin(f"up-{panel}", Flow(halves, order))
+                    clock.begin(f"up-{panel}", Flow(halves, order, True))
     weight_grads = None
     if not quick:
         whole_backs = [backs[at, 0] for at in shares]
@@ -1393,58 +1379,68 @@
     "learn": ("mixes",),
     "second-back": ("seconds",),
     "second-few": ("seconds",),
-    "learner": ("seconds",),
+    "down1": ("seconds",),
     "up1": ("heads", "down", "seconds"),
-    "heads00": ("heads", "down", "seconds"),
-    "heads11": ("heads", "down", "up-0", "up-1"),
-    "project11": ("up-0", "up-1", "project-0"),
-    "heads10": ("heads", "down", "up-0", "up-1"),
+    "up0": ("heads", "down", "seconds"),
+    "heads00": ("heads", "down"),
+    "again0": ("heads", "down"),
+    "heads11": ("heads", "down", "up-0", "up-1", "project-0"),
+    "heads10": ("heads", "down", "up-0", "up-1", "project-0"),
     "project10": ("up-0", "up-1", "project-0"),
-    "inward": ("heads", "down", "project-0"),
-    "tail0": ("heads", "down", "project-0", "project-1"),
-    "tail1": ("project-0", "project-1", "small"),
+    "inward": ("heads", "down", "up-0", "up-1"),
+    "again1": ("up-0", "up-1", "project-0", "project-1"),
+    "tail0": ("up-0", "up-1", "project-0", "project-1", "small"),
+    "tail1": ("heads", "down", "up-0", "up-1", "project-0", "project-1", "small"),
     "tail2": ("project-0", "project-1", "small"),
-    "tail3": ("project-0", "project-1", "small", "up-all"),
-    "tail4": ("project-1", "small"),
-    "again0": ("heads", "down", "project-1", "small"),
-    "again1": ("project-1",),
-    "tail5": ("heads", "down", "project-1"),
+    "tail3": ("project-1",),
+    "tail4": ("up-0", "up-1", "project-1", "small"),
+    "tail5": ("project-0", "project-1", "small"),
 }
-SETS = {"up-all": ("up-0", "up-1")}
+
+
+def again_part(clock, piece, token_up, token_down):
+    if piece == 0:
+        seconds, mixes = clock.flows["seconds"], clock.whole["mixes"]
+        clock.rows = [seconds.kept, mixes, seconds.got, near(1)(mixes)]
+        clock.ready = ()
+    clock.rows[0] = clock(f"again{piece}", clock.rows[0])
+    clock.ready = again(piece, 2, clock.rows, token_up, token_down, clock.ready)
+    clock.past += clock.ready
 
 
 def finish(clock, input_grad, project, out, up, down, token_up, token_down):
     width, wide, units = project.shape[1], project.shape[2], up.shape[1]
     wider = jnp.float32
-    ups = [f"up-{panel}" for panel in range(units // width)]
-    seconds, mixes = clock.flows["seconds"], clock.whole["mixes"]
-    rows = [seconds.kept, mixes, seconds.got, near(1)(mixes)]
-    rows[0] = meet(rows[0], [input_grad])[0]
-    for number in range(4):
-        rows[0] = clock(f"tail{number}", rows[0])
-    panels = clock.rows(ups, clock.whole["up-all"])
-    panels, out_grad = panels[:-1] + [panels[-1][:width]], panels[-1][width:]
-    patch_upward_grad = jnp.concatenate(panels, axis=1).astype(wider)
-    rows[0], late = meet(rows[0], [patch_upward_grad, out_grad])
-    patch_upward_grad, out_grad = late
-    rows[0] = clock("tail4", rows[0])
-    before = ()
-    for piece in range(2):
-        rows[0] = clock(f"again{piece}", rows[0])
-        before = again(piece, 2, rows, token_up, token_down, before)
-        rows[0], before = meet(rows[0], before)
-    token_upward_grad, token_downward_grad = before
-    token_downward_grad = clock("tail5", token_downward_grad)
-    clock.end(clock.flows)
+    clock.past.append(input_grad)
+    again_part(clock, 1, token_up, token_down)
+    token_upward_grad, token_downward_grad = clock.ready
 
     def last(name):
         flow = clock.flows[name]
         return flow.kept, flow.got, my_bit(flow.order[0])
 
+    def tail(number, value):
+        value = clock(f"tail{number}", value)
+        clock.past.append(value)
+        return value
+
+    token_downward_grad = tail(0, token_downward_grad)
+    token_downward_grad = tail(1, token_downward_grad)
     patch_downward_grad, token_outproj_grad = spread(
         [last("down")], [[(0, 0, units, 0), (1, 0, wide, 0)]], [down.shape, out.shape], wider
     )
+    patch_downward_grad = tail(2, patch_downward_grad)
     (token_project_grad,) = spread([last("heads")], [[(0, 0, width, 0)]], [project.shape], wider)
+    token_project_grad = tail(3, token_project_grad)
+    token_project_grad = tail(4, token_project_grad)
+    ups = range(units // width)
+    layouts = [[(0, 0, width, panel)] for panel in ups]
+    layouts[-1].append((1, 0, wide, 0))
+    patch_upward_grad, patch_outproj_grad = spread(
+        [last(f"up-{panel}") for panel in ups], layouts, [up.shape, out.shape], wider
+    )
+    patch_upward_grad = tail(5, patch_upward_grad)
+    clock.end(clock.flows)
     (patch_project_grad,) = spread(
         [last("project-0"), last("project-1")],
         [[(0, 0, width, 0)], [(0, 0, width, 1)]],
@@ -1453,7 +1449,7 @@
     )
     return (
         (token_project_grad, token_outproj_grad, token_upward_grad, token_downward_grad),
-        (patch_project_grad, out_grad.astype(wider), patch_upward_grad, patch_downward_grad),
+        (patch_project_grad, patch_outproj_grad, patch_upward_grad, patch_downward_grad),
     )
 
 
@@ -1499,7 +1495,7 @@
     weight_qkv, weight_out, weight_up, weight_down = (fetch(weight) for weight in token_weights)
     upper_params = (token_gainone, weight_qkv, weight_out, token_gaintwo, weight_up, weight_down)
     maps = learner_weight.T
-    clock = Clock(PLAN, SETS)
+    clock = Clock(PLAN)
     if shards == 2 and lax.axis_size("dp") == 16:
         clock.whole["mixes"] = lax.all_gather(low(output_grad), "dp", tiled=True)
     patched = clock("learn", patched)
@@ -1512,7 +1508,14 @@
         shares, clock("learner", token_grad), patched, learner_gain, maps
     )
     input_grad, patch_gainone_grad, patch_gaintwo_grad, patch_grads = lower_backward(
-        patched_grad, patched_low, lower_stored, lower_params, lower_bias, clock, token_grads
+        patched_grad,
+        patched_low,
+        lower_stored,
+        lower_params,
+        lower_bias,
+        clock,
+        token_grads,
+        lambda clock: again_part(clock, 0, token_upward, token_downward),
     )
     gains = (
         patch_gainone_grad,

time: 795 us -> 772 us (0.971)
  waiting for transfers between devices: 137 us -> 111 us
  Pallas kernels: 451 us -> 466 us
    ppermute x48 -> x56, waiting for transfers between devices: 133 us -> 106 us  [swap(): lax.ppermute(tensor, 'dp', [(place, place ^ 1 << bit) for place in range(...]
    pallas_call x19 -> x26, Pallas kernels: 27.4 us -> 38.9 us  [spread(): pl.pallas_call(partial(spread_kernel, cuts, parts), grid_spec=pltpu.Prefe...]
    ppermute x48 -> x56, starting transfers between devices: 66.1 us -> 64.1 us  [swap(): lax.ppermute(tensor, 'dp', [(place, place ^ 1 << bit) for place in range(...]
    unnamed x250 -> x242, local copies, waits for them, and re-layouts: 71.8 us -> 71.1 us
  transfers between devices with their start and end apart: 66 -> 73, of which waited for: 20 -> 17; matrix products, arithmetic and copies ran while one was open for 5% -> 4% of each run, Pallas kernels for 50% -> 52%
where the time goes in v2:
time: 772 us; the launch traced here: 762 us
  Pallas kernels  466 us (60%)
  waiting for transfers between devices  111 us (14%)
  local copies, waits for them, and re-layouts  77.1 us (10%)
  starting transfers between devices  67.6 us (9%)
  matrix products  18.1 us (2%)
  between operations  15.9 us (2%)
    ppermute x56, waiting for transfers between devices, swap(): lax.ppermute(tensor, 'dp', [(place, place ^ 1 << bit) for place in range(...  106 us
    pallas_call x11, Pallas kernels, grads(): pl.pallas_call(partial(grads_kernel, cuts, count), grid_spec=pltpu.Prefet...  81.3 us
    pallas_call x6, Pallas kernels, attention(): pl.pallas_call(kernel, grid=(pairs,), in_specs=[pl.BlockSpec(bias.shape,...  79 us
    unnamed x242, local copies, waits for them, and re-layouts  71.1 us
    pallas_call x2, Pallas kernels, feed(): pl.pallas_call(partial(ff_kernel, shares, per), grid=(rows // block, shar...  64.7 us
    ppermute x56, starting transfers between devices, swap(): lax.ppermute(tensor, 'dp', [(place, place ^ 1 << bit) for place in range(...  64.1 us
    pallas_call x2, Pallas kernels, feed_back(): pl.pallas_call(partial(ff_back_kernel, shares, per), grid=(rows // block,...  59.1 us
    pallas_call x2, Pallas kernels, again(): pl.pallas_call(kernel, grid=(units // pieces // size, 2), in_specs=[whole...  53.4 us
  transfers between devices with their start and end apart: 73, of which 17 were waited for; matrix products, arithmetic and copies ran while one was open for 4% of the time, Pallas kernels for 52%

profile of v2, /device:TPU:0, one launch (start us, length us, event | category | flops | bytes accessed | tf_op | source)
XLA Modules:
  0.0 762.3 jit_solution(14672956637819724499)
XLA Ops:
  19.3 5.3 convert_bitcast_fusion.1.qkv_ref
  24.7 14.0 %attend.2.refs_0_.refs_4_ = bf16[1568,512]{1,0:T(8,128)(2,1)S(1)} custom-call(f32[8,208,1]{2,1,0:T(8,128)S(1)} %copy-done.16, bf16[3,1568,512]{2,1,0:T(8,128)(2,1)S(1)} %convert_bitcast_fusion.1.qkv_ref), custom_call_target="tpu_custom_call" | custom-call | flops 13153337344 | bytes 6422528 | tf_op jit(solution)/shard_map/attend/pallas_call | solution.py:134
  38.7 7.8 %convert_bitcast_fusion.qkv_ref = bf16[3,1568,512]{2,1,0:T(8,128)(2,1)S(1)} fusion(bf16[3,1024,512]{2,1,0:T(8,128)(2,1)} %collective-permute-done.refs_6_.refs_7_, bf16[1568,1024]{1,0:T(8,128)(2,1)S(1)} %norm.1.refs_1_), kind=kOutput, calls=%fused_computation | convolution fusion | flops 4934909952 | bytes 11173888 | tf_op jit(solution)/shard_map/rd,tdc->trc/dot_general | solution.py:1211
  46.6 14.0 %attend.3.refs_1_.refs_5_ = bf16[1568,512]{1,0:T(8,128)(2,1)S(1)} custom-call(f32[8,208,1]{2,1,0:T(8,128)S(1)} %copy-done.16, bf16[3,1568,512]{2,1,0:T(8,128)(2,1)S(1)} %convert_bitcast_fusion.qkv_ref), custom_call_target="tpu_custom_call" | custom-call | flops 13153337344 | bytes 6422528 | tf_op jit(solution)/shard_map/attend/pallas_call | solution.py:134
  60.6 9.6 %outward.1 = (f32[1568,1024]{1,0:T(8,128)S(1)}, bf16[1568,1024]{1,0:T(8,128)(2,1)S(1)}) custom-call(bf16[1568,512]{1,0:T(8,128)(2,1)S(1)} %attend.2.refs_0_.refs_4_, bf16[1568,512]{1,0:T(8,128)(2,1)S(1)} %attend.3.refs_1_.refs_5_, bf16[512,1024]{1,0:T(8,128)(2,1)S(1)} %copy-done.110, bf16[512,1024]{1,0:T(8,128)(2,1)} %collective-permute-done.1.refs_3_, ...), custom_call_target="tpu_custom_call" | custom-call | flops 6576668672 | bytes 19267584 | tf_op jit(solution)/shard_map/outward/pallas_call | solution.py:307
  76.1 53.4 %feed.2 = (f32[1568,1024]{1,0:T(8,128)}, bf16[1568,2048]{1,0:T(8,128)(2,1)}, bf16[1568,2048]{1,0:T(8,128)(2,1)}, bf16[1568,2048]{1,0:T(8,128)(2,1)}, bf16[1568,2048]{1,0:T(8,128)(2,1)}) custom-call(bf16[1568,1024]{1,0:T(8,128)(2,1)} %copy-done, f32[1568,1024]{1,0:T(8,128)} %copy-done.36, bf16[1024,2048]{1,0:T(8,128)(2,1)} %refs_5_.5, ...), custom_call_target="tpu_custom_call" | custom-call | flops 32883343360 | bytes 32112640 | tf_op jit(solution)/shard_map/feed/pallas_call | solution.py:372
  132.4 4.9 learn.1
  137.3 6.5 few.1
  150.1 3.8 collective-permute-done.8.refs_1_
  157.3 11.3 %feed.3 = (f32[64,1024]{1,0:T(8,128)}, bf16[64,2048]{1,0:T(8,128)(2,1)}, bf16[64,2048]{1,0:T(8,128)(2,1)}, bf16[64,2048]{1,0:T(8,128)(2,1)}, bf16[64,2048]{1,0:T(8,128)(2,1)}) custom-call(bf16[64,1024]{1,0:T(8,128)(2,1)} %copy-done.71, f32[64,1024]{1,0:T(8,128)} %copy-done.54, bf16[1024,2048]{1,0:T(8,128)(2,1)} %refs_4_.11, ...), custom_call_target="tpu_custom_call" | custom-call | bytes 1310720 | tf_op jit(solution)/shard_map/feed/pallas_call | solution.py:372
  170.6 11.9 %feed_back.2 = (f32[64,1024]{1,0:T(8,128)S(1)}, bf16[64,1024]{1,0:T(8,128)(2,1)S(1)}, bf16[64,1024]{1,0:T(8,128)(2,1)}, f32[8,1024]{1,0:T(8,128)S(1)}, bf16[64,2...) custom-call(f32[64,1024]{1,0:T(8,128)S(1)} %copy-done.56, f32[64,1024]{1,0:T(8,128)S(1)} %copy-done.55, f32[1,1024]{1,0:T(1,128)S(1)} %bitcast.65, ...), custom_call_target="tpu_custom_call" | custom-call | flops 1000 | bytes 1000 | tf_op jit(solution)/shard_map/feed_back/pallas_call | solution.py:440
  184.3 8.2 %few_back.1 = (f32[64,1024]{1,0:T(8,128)S(1)}, f32[8,1024]{1,0:T(8,128)S(1)}, bf16[3,64,512]{2,1,0:T(8,128)(2,1)S(1)}, bf16[3,64,512]{2,1,0:T(8,128)(2,1)S(1)}) custom-call(bf16[64,1024]{1,0:T(8,128)(2,1)S(1)} %get-tuple-element.241.refs_0_.refs_4_.refs_5_, f32[64,1024]{1,0:T(8,128)S(1)} %get-tuple-element.242.refs_1_, f32[64,1024]{1,0:T(8,128)S(1)} %copy-done.58, ...), custom_call_target="tpu_custom_call" | custom-call | flops 1000 | bytes 1000 | tf_op jit(solution)/shard_map/few_back/pallas_call | solution.py:733
  202.6 9.8 %learn_back.1 = (f32[1568,1024]{1,0:T(8,128)S(1)}, bf16[1568,1024]{1,0:T(8,128)(2,1)S(1)}, f32[8,1024]{1,0:T(8,128)S(1)}, f32[8,1024]{1,0:T(8,128)S(1)}) custom-call(f32[2,32,784]{2,1,0:T(8,128)S(1)} %copy-done.83, f32[64,1024]{1,0:T(8,128)S(1)} %copy-done.81, f32[1568,1024]{1,0:T(8,128)S(1)} %copy-done.7, f32[1,1024]{1,0:T(1,128)S(1)} %bitcast.71, ...), custom_call_target="tpu_custom_call" | custom-call | flops 1000 | bytes 1000 | tf_op jit(solution)/shard_map/learn_back/pallas_call | solution.py:584
  220.2 9.7 %grads.12 = bf16[2560,1024]{1,0:T(8,128)(2,1)S(1)} custom-call(s32[1]{0:T(128)} %constant.60.clone.1.refs_0_, bf16[1568,2048]{1,0:T(8,128)(2,1)S(1)} %copy-done.35, bf16[1568,1024]{1,0:T(8,128)(2,1)S(1)} %get-tuple-element.263.refs_2_, bf16[64,512]{1,0:T(8,128)(2,1)S(1)} %copy-done.95, bf16[64,1024]{1,0:T(8,128)(2,1)S(1)} %get-tuple-element.241.refs_0_.refs_4_.refs_5_), custom_call_target="tpu_custom_call" | custom-call | flops 1000 | bytes 1000 | tf_op jit(solution)/shard_map/grads/pallas_call | solution.py:1171
  232.6 4.1 grads.13
  236.7 4.6 collective-permute-done.12.refs_3_.refs_6_
  241.2 13.2 %grads.14 = (bf16[1280,1024]{1,0:T(8,128)(2,1)S(1)}, bf16[1280,1024]{1,0:T(8,128)(2,1)}) custom-call(s32[1]{0:T(128)} %bitcast.27.mines_ref.refs_0_.mine_ref, bf16[1568,2048]{1,0:T(8,128)(2,1)} %get-tuple-element.261.refs_1_, bf16[1568,1024]{1,0:T(8,128)(2,1)S(1)} %get-tuple-element.263.refs_2_, ...), custom_call_target="tpu_custom_call" | custom-call | flops 1000 | bytes 1000 | tf_op jit(solution)/shard_map/grads/pallas_call | solution.py:1171
  260.3 47.3 %feed_back.3 = (f32[1568,1024]{1,0:T(8,128)}, bf16[1568,1024]{1,0:T(8,128)(2,1)S(1)}, bf16[1568,1024]{1,0:T(8,128)(2,1)}, f32[8,1024]{1,0:T(8,128)S(1)}, bf16[15...) custom-call(f32[1568,1024]{1,0:T(8,128)} %copy-done.37, f32[1568,1024]{1,0:T(8,128)} %copy-done.36, ...), custom_call_target="tpu_custom_call" | custom-call | flops 1000 | bytes 1000 | tf_op jit(solution)/shard_map/feed_back/pallas_call | solution.py:440
  307.6 7.7 %collective-permute-done.14.refs_1_ = bf16[1280,1024]{1,0:T(8,128)(2,1)} collective-permute-done((bf16[1280,1024]{1,0:T(8,128)(2,1)}, bf16[1280,1024]{1,0:T(8,128)(2,1)}, u32[]{:S(2)}, u32[]{:S(2)}) %collective-permute-start.14) | collective-permute-done | bytes 2621472 | tf_op jit(solution)/shard_map/ppermute | solution.py:815
  317.8 3.8 fold.19
  327.2 14.3 %grads.15 = bf16[2560,1024]{1,0:T(8,128)(2,1)S(1)} custom-call(s32[1]{0:T(128)} %constant.60.clone.1.refs_0_, bf16[1568,1024]{1,0:T(8,128)(2,1)S(1)} %copy-done.1, bf16[1568,2048]{1,0:T(8,128)(2,1)} %get-tuple-element.278.refs_2_.refs_4_, bf16[1568,1024]{1,0:T(8,128)(2,1)S(1)} %copy-done.1, bf16[1568,2048]{1,0:T(8,128)(2,1)} %get-tuple-element.278.refs_2_.refs_4_, ...), custom_call_target="tpu_custom_call" | custom-call | flops 1000 | bytes 1000 | tf_op jit(solution)/shard_map/grads/pallas_call | solution.py:1171
  352.2 12.6 %attend_back.4.refs_2_ = bf16[3,1568,256]{2,1,0:T(8,128)(2,1)S(1)} custom-call(f32[8,208,1]{2,1,0:T(8,128)S(1)} %copy-done.17, bf16[3,1568,512]{2,1,0:T(8,128)(2,1)S(1)} %copy-done.20, bf16[1568,512]{1,0:T(8,128)(2,1)S(1)} %convolution_convert_fusion.1.grad_ref), custom_call_target="tpu_custom_call" | custom-call | flops 1000 | bytes 1000 | tf_op jit(solution)/shard_map/attend_back/pallas_call | solution.py:134
  366.0 4.6 grads.16
  371.1 4.6 collective-permute-done.17.refs_1_
  387.7 10.7 %grads.18 = (bf16[768,1024]{1,0:T(8,128)(2,1)S(1)}, bf16[768,1024]{1,0:T(8,128)(2,1)}) custom-call(s32[1]{0:T(128)} %bitcast.27.mines_ref.refs_0_.mine_ref, bf16[1568,1024]{1,0:T(8,128)(2,1)S(1)} %copy-done.1, bf16[1568,2048]{1,0:T(8,128)(2,1)} %get-tuple-element.289.refs_2_, bf16[2560,1024]{1,0:T(8,128)(2,1)S(1)} %copy-done.3, ...), custom_call_target="tpu_custom_call" | custom-call | flops 1000 | bytes 1000 | tf_op jit(solution)/shard_map/grads/pallas_call | solution.py:1171
  402.6 7.6 grads.17
  420.4 12.6 %attend_back.5.refs_2_.refs_0_ = bf16[3,1568,256]{2,1,0:T(8,128)(2,1)S(1)} custom-call(f32[8,208,1]{2,1,0:T(8,128)S(1)} %copy-done.17, bf16[3,1568,512]{2,1,0:T(8,128)(2,1)S(1)} %bitcast.57, bf16[1568,512]{1,0:T(8,128)(2,1)S(1)} %convolution_convert_fusion.grad_ref), custom_call_target="tpu_custom_call" | custom-call | flops 1000 | bytes 1000 | tf_op jit(solution)/shard_map/attend_back/pallas_call | solution.py:134
  433.0 6.6 grads.19
  443.2 26.9 %again.2 = (f32[1024,2048]{1,0:T(8,128)}, f32[2048,1024]{1,0:T(8,128)}) custom-call(bf16[1024,1024]{1,0:T(8,128)(2,1)S(1)} %spread.29.refs_0_, bf16[1024,1024]{1,0:T(8,128)(2,1)S(1)} %copy-done.30, bf16[1024,1024]{1,0:T(8,128)(2,1)} %collective-permute-done.18.refs_2_, bf16[1024,1024]{1,0:T(8,128)(2,1)} %collective-permute-done.30.refs_3_, ...), custom_call_target="tpu_custom_call" | custom-call | flops 1000 | bytes 1000 | tf_op jit(solution)/shard_map/again/pallas_call | solution.py:795
  487.2 13.0 %attend_back.6.refs_2_.refs_3_ = bf16[3,1568,256]{2,1,0:T(8,128)(2,1)S(1)} custom-call(f32[8,208,1]{2,1,0:T(8,128)S(1)} %copy-done.17, bf16[3,1568,512]{2,1,0:T(8,128)(2,1)S(1)} %bitcast.61, bf16[1568,512]{1,0:T(8,128)(2,1)S(1)} %copy-done.34), custom_call_target="tpu_custom_call" | custom-call | flops 1000 | bytes 1000 | tf_op jit(solution)/shard_map/attend_back/pallas_call | solution.py:134
  500.3 3.6 grads.20
  517.2 12.8 %attend_back.7.refs_2_.refs_1_ = bf16[3,1568,256]{2,1,0:T(8,128)(2,1)S(1)} custom-call(f32[8,208,1]{2,1,0:T(8,128)S(1)} %copy-done.17, bf16[3,1568,512]{2,1,0:T(8,128)(2,1)S(1)} %bitcast.59, bf16[1568,512]{1,0:T(8,128)(2,1)S(1)} %convolution_convert_fusion.grad_ref), custom_call_target="tpu_custom_call" | custom-call | flops 1000 | bytes 1000 | tf_op jit(solution)/shard_map/attend_back/pallas_call | solution.py:134
  533.5 4.7 grads.21
  538.1 8.4 %collective-permute-done.41 = bf16[64,1024]{1,0:T(8,128)(2,1)S(1)} collective-permute-done((bf16[64,1024]{1,0:T(8,128)(2,1)S(1)}, bf16[64,1024]{1,0:T(8,128)(2,1)S(1)}, u32[]{:S(2)}, u32[]{:S(2)}) %collective-permute-start.41) | collective-permute-done | bytes 131104 | tf_op jit(solution)/shard_map/ppermute | solution.py:815
  556.5 8.2 %collective-permute-done.46 = bf16[64,768]{1,0:T(8,128)(2,1)S(1)} collective-permute-done((bf16[64,768]{1,0:T(8,128)(2,1)S(1)}, bf16[64,768]{1,0:T(8,128)(2,1)S(1)}, u32[]{:S(2)}, u32[]{:S(2)}) %collective-permute-start.46) | collective-permute-done | bytes 98336 | tf_op jit(solution)/shard_map/ppermute | solution.py:815
  578.2 23.0 %inward_back.1 = (f32[1568,1024]{1,0:T(8,128)}, f32[8,1024]{1,0:T(8,128)S(1)}) custom-call(bf16[3,1568,256]{2,1,0:T(8,128)(2,1)S(1)} %copy-done.11, bf16[3,1568,256]{2,1,0:T(8,128)(2,1)S(1)} %copy-done.15, bf16[3,1568,256]{2,1,0:T(8,128)(2,1)S(1)} %copy-done.9, bf16[3,1568,256]{2,1,0:T(8,128)(2,1)S(1)} %copy-done.13, bf16[3,1024,512]{2,1,0:T(8,128)(2,1)S(1)} %copy-done.27, ...), custom_call_target="tpu_custom_call" | custom-call | flops 1000 | bytes 1000 | tf_op jit(solution)/shard_map/inward_back/pallas_call | solution.py:644
  612.1 7.9 %collective-permute-done.50.refs_1_ = bf16[64,768]{1,0:T(8,128)(2,1)S(1)} collective-permute-done((bf16[64,768]{1,0:T(8,128)(2,1)S(1)}, bf16[64,768]{1,0:T(8,128)(2,1)S(1)}, u32[]{:S(2)}, u32[]{:S(2)}) %collective-permute-start.50) | collective-permute-done | bytes 98336 | tf_op jit(solution)/shard_map/ppermute | solution.py:815
  624.6 26.5 %again.3 = (f32[1024,2048]{1,0:T(8,128)}, f32[2048,1024]{1,0:T(8,128)}) custom-call(bf16[1024,1024]{1,0:T(8,128)(2,1)S(1)} %copy-done.22, bf16[1024,1024]{1,0:T(8,128)(2,1)S(1)} %copy-done.31, bf16[1024,1024]{1,0:T(8,128)(2,1)} %collective-permute-done.18.refs_2_, ...), custom_call_target="tpu_custom_call", output_to_operand_aliasing={{0}: (6, {}), {1}: (7, {})} | custom-call | flops 1000 | bytes 1000 | tf_op jit(solution)/shard_map/again/pallas_call | solution.py:795
  653.6 5.0 collective-permute-done.57
  658.8 5.7 collective-permute-done.55.refs_1_
  664.5 5.7 collective-permute-done.56.refs_1_
  677.1 9.4 %spread.41 = (f32[2048,1024]{1,0:T(8,128)}, f32[512,1024]{1,0:T(8,128)}) custom-call(s32[1]{0:T(128)} %bitcast.27.mines_ref.refs_0_.mine_ref, bf16[1280,1024]{1,0:T(8,128)(2,1)} %spread.35.refs_0_, bf16[1280,1024]{1,0:T(8,128)(2,1)} %collective-permute-done.59.refs_1_), custom_call_target="tpu_custom_call" | custom-call | flops 1000 | bytes 1000 | tf_op jit(solution)/shard_map/spread/pallas_call | solution.py:964
  686.5 27.2 %collective-permute-done.60.refs_1_ = bf16[256,768]{1,0:T(8,128)(2,1)S(1)} collective-permute-done((bf16[256,768]{1,0:T(8,128)(2,1)S(1)}, bf16[256,768]{1,0:T(8,128)(2,1)S(1)}, u32[]{:S(2)}, u32[]{:S(2)}) %collective-permute-start.60) | collective-permute-done | bytes 393248 | tf_op jit(solution)/shard_map/ppermute | solution.py:815
  715.4 4.8 spread.45
  722.5 3.7 collective-permute-done.65
  729.5 6.6 spread.48
  738.1 13.3 %collective-permute-done.71.refs_3_ = bf16[512,768]{1,0:T(8,128)(2,1)S(1)} collective-permute-done((bf16[512,768]{1,0:T(8,128)(2,1)S(1)}, bf16[512,768]{1,0:T(8,128)(2,1)S(1)}, u32[]{:S(2)}, u32[]{:S(2)}) %collective-permute-start.71) | collective-permute-done | bytes 786464 | tf_op jit(solution)/shard_map/ppermute | solution.py:815
  751.3 3.6 spread.51
  (464 shorter events, 202.2 us)
Async XLA Ops:
  7.2 122.3 %all-gather.2.cloned.1.call-start = ((), (), s32[]{:S(2)}) async-start(), calls=%async_computation | async-start | bytes 2228224 | tf_op jit(solution)/shard_map/all_gather | solution.py:1500
  7.2 31.4 %collective-permute-start = (bf16[3,1024,512]{2,1,0:T(8,128)(2,1)}, bf16[3,1024,512]{2,1,0:T(8,128)(2,1)}, u32[]{:S(2)}, u32[]{:S(2)}) collective-permute-start(bf16[3,1024,512]{2,1,0:T(8,128)(2,1)} %refs_5_.7), channel_id=1, source_target_pairs={{1,0},{0,1},{3,2},{2,3},{5,4},{4,5},{7,6},{6,7},{9,8},{8,9},{11,10... | collective-permute-start | bytes 9437192 | tf_op jit(solution)/shard_map/ppermute | solution.py:1186
  7.7 52.8 %collective-permute-start.1 = (bf16[512,1024]{1,0:T(8,128)(2,1)}, bf16[512,1024]{1,0:T(8,128)(2,1)}, u32[]{:S(2)}, u32[]{:S(2)}) collective-permute-start(bf16[512,1024]{1,0:T(8,128)(2,1)} %refs_2_.2), channel_id=1, source_target_pairs={{1,0},{0,1},{3,2},{2,3},{5,4},{4,5},{7,6},{6,7},{9,8},{8,9},{11,10... | collective-permute-start | bytes 3145736 | tf_op jit(solution)/shard_map/ppermute | solution.py:1186
  7.8 68.1 %collective-permute-start.2 = (bf16[1024,2048]{1,0:T(8,128)(2,1)}, bf16[1024,2048]{1,0:T(8,128)(2,1)}, u32[]{:S(2)}, u32[]{:S(2)}) collective-permute-start(bf16[1024,2048]{1,0:T(8,128)(2,1)} %refs_5_.5), channel_id=1, source_target_pairs={{1,0},{0,1},{3,2},{2,3},{5,4},{4,5},{7,6},{6,7},{9,8},{8,9},{11,10... | collective-permute-start | bytes 12582920 | tf_op jit(solution)/shard_map/ppermute | solution.py:1186
  8.3 67.8 %collective-permute-start.3 = (bf16[2048,1024]{1,0:T(8,128)(2,1)}, bf16[2048,1024]{1,0:T(8,128)(2,1)}, u32[]{:S(2)}, u32[]{:S(2)}) collective-permute-start(bf16[2048,1024]{1,0:T(8,128)(2,1)} %refs_7_.3), channel_id=1, source_target_pairs={{1,0},{0,1},{3,2},{2,3},{5,4},{4,5},{7,6},{6,7},{9,8},{8,9},{11,10... | collective-permute-start | bytes 12582920 | tf_op jit(solution)/shard_map/ppermute | solution.py:1186
  74.6 82.7 %collective-permute-start.6 = (bf16[1024,2048]{1,0:T(8,128)(2,1)}, bf16[1024,2048]{1,0:T(8,128)(2,1)}, u32[]{:S(2)}, u32[]{:S(2)}) collective-permute-start(bf16[1024,2048]{1,0:T(8,128)(2,1)} %refs_4_.11), channel_id=1, source_target_pairs={{1,0},{0,1},{3,2},{2,3},{5,4},{4,5},{7,6},{6,7},{9,8},{8,9},{11,10... | collective-permute-start | bytes 12582920 | tf_op jit(solution)/shard_map/ppermute | solution.py:1186
  75.1 82.2 %collective-permute-start.7 = (bf16[2048,1024]{1,0:T(8,128)(2,1)}, bf16[2048,1024]{1,0:T(8,128)(2,1)}, u32[]{:S(2)}, u32[]{:S(2)}) collective-permute-start(bf16[2048,1024]{1,0:T(8,128)(2,1)} %refs_5_.8), channel_id=1, source_target_pairs={{1,0},{0,1},{3,2},{2,3},{5,4},{4,5},{7,6},{6,7},{9,8},{8,9},{11,10... | collective-permute-start | bytes 12582920 | tf_op jit(solution)/shard_map/ppermute | solution.py:1186
  75.4 61.9 %collective-permute-start.4 = (bf16[3,1024,512]{2,1,0:T(8,128)(2,1)}, bf16[3,1024,512]{2,1,0:T(8,128)(2,1)}, u32[]{:S(2)}, u32[]{:S(2)}) collective-permute-start(bf16[3,1024,512]{2,1,0:T(8,128)(2,1)} %refs_7_.2), channel_id=1, source_target_pairs={{1,0},{0,1},{3,2},{2,3},{5,4},{4,5},{7,6},{6,7},{9,8},{8,9},{11,10... | collective-permute-start | bytes 9437192 | tf_op jit(solution)/shard_map/ppermute | solution.py:1186
  76.0 61.3 %collective-permute-start.5 = (bf16[512,1024]{1,0:T(8,128)(2,1)}, bf16[512,1024]{1,0:T(8,128)(2,1)}, u32[]{:S(2)}, u32[]{:S(2)}) collective-permute-start(bf16[512,1024]{1,0:T(8,128)(2,1)} %refs_9_), channel_id=1, source_target_pairs={{1,0},{0,1},{3,2},{2,3},{5,4},{4,5},{7,6},{6,7},{9,8},{8,9},{11,10... | collective-permute-start | bytes 3145736 | tf_op jit(solution)/shard_map/ppermute | solution.py:1186
  155.5 26.9 %collective-permute-start.9 = (bf16[128,1024]{1,0:T(8,128)(2,1)}, bf16[128,1024]{1,0:T(8,128)(2,1)}, u32[]{:S(2)}, u32[]{:S(2)}) collective-permute-start(bf16[128,1024]{1,0:T(8,128)(2,1)} %spread.26.refs_0_), channel_id=1, source_target_pairs={{0,4},{2,6},{4,0},{6,2},{8,12},{10,14},{12,8},{14,10},{16,20},{18,... | collective-permute-start | bytes 786440 | tf_op jit(solution)/shard_map/ppermute | solution.py:815
  196.3 21.1 %collective-permute-start.11 = (bf16[1024,1536]{1,0:T(8,128)(2,1)}, bf16[1024,1536]{1,0:T(8,128)(2,1)}, u32[]{:S(2)}, u32[]{:S(2)}) collective-permute-start(bf16[1024,1536]{1,0:T(8,128)(2,1)} %grads.11), channel_id=1, source_target_pairs={{0,1},{1,0},{2,3},{3,2},{4,5},{5,4},{6,7},{7,6},{8,9},{9,8},{10,11... | collective-permute-start | bytes 9437192 | tf_op jit(solution)/shard_map/ppermute | solution.py:1192
  256.0 59.3 %collective-permute-start.14 = (bf16[1280,1024]{1,0:T(8,128)(2,1)}, bf16[1280,1024]{1,0:T(8,128)(2,1)}, u32[]{:S(2)}, u32[]{:S(2)}) collective-permute-start(bf16[1280,1024]{1,0:T(8,128)(2,1)} %get-tuple-element.265), channel_id=1, source_target_pairs={{0,4},{2,6},{4,0},{6,2},{8,12},{10,14},{12,8},{14,10},{16,20},{18,... | collective-permute-start | bytes 7864328 | tf_op jit(solution)/shard_map/ppermute | solution.py:815
  256.2 51.4 %collective-permute-start.13 = (bf16[512,1536]{1,0:T(8,128)(2,1)}, bf16[512,1536]{1,0:T(8,128)(2,1)}, u32[]{:S(2)}, u32[]{:S(2)}) collective-permute-start(bf16[512,1536]{1,0:T(8,128)(2,1)} %get-tuple-element.260), channel_id=1, source_target_pairs={{0,2},{2,0},{4,6},{6,4},{8,10},{10,8},{12,14},{14,12},{16,18},{18,... | collective-permute-start | bytes 4718600 | tf_op jit(solution)/shard_map/ppermute | solution.py:815
  257.7 49.9 %collective-permute-start.15 = (bf16[512,1024]{1,0:T(8,128)(2,1)}, bf16[512,1024]{1,0:T(8,128)(2,1)}, u32[]{:S(2)}, u32[]{:S(2)}) collective-permute-start(bf16[512,1024]{1,0:T(8,128)(2,1)} %spread.28.refs_0_), channel_id=1, source_target_pairs={{0,16},{2,18},{4,20},{6,22},{8,24},{10,26},{12,28},{14,30},{16,0},... | collective-permute-start | bytes 3145736 | tf_op jit(solution)/shard_map/ppermute | solution.py:815
  343.8 39.0 %collective-permute-start.21 = (bf16[2560,1024]{1,0:T(8,128)(2,1)}, bf16[2560,1024]{1,0:T(8,128)(2,1)S(1)}, u32[]{:S(2)}, u32[]{:S(2)}) collective-permute-start(bf16[2560,1024]{1,0:T(8,128)(2,1)} %copy-done.38), channel_id=1, source_target_pairs={{0,1},{1,0},{2,3},{3,2},{4,5},{5,4},{6,7},{7,6},{8,9},{9,8},{10,11... | collective-permute-start | bytes 15728648 | tf_op jit(solution)/shard_map/ppermute | solution.py:1192
  343.8 31.9 %collective-permute-start.18 = (bf16[1024,1024]{1,0:T(8,128)(2,1)S(1)}, bf16[1024,1024]{1,0:T(8,128)(2,1)}, u32[]{:S(2)}, u32[]{:S(2)}) collective-permute-start(bf16[1024,1024]{1,0:T(8,128)(2,1)S(1)} %spread.29.refs_0_), channel_id=1, source_target_pairs={{1,0},{0,1},{3,2},{2,3},{5,4},{4,5},{7,6},{6,7},{9,8},{8,9},{11,10... | collective-permute-start | bytes 6291464 | tf_op jit(solution)/shard_map/ppermute | solution.py:1186
  344.3 26.3 %collective-permute-start.16 = (bf16[256,1536]{1,0:T(8,128)(2,1)}, bf16[256,1536]{1,0:T(8,128)(2,1)}, u32[]{:S(2)}, u32[]{:S(2)}) collective-permute-start(bf16[256,1536]{1,0:T(8,128)(2,1)} %get-tuple-element.272), channel_id=1, source_target_pairs={{0,4},{2,6},{4,0},{6,2},{8,12},{10,14},{12,8},{14,10},{16,20},{18,... | collective-permute-start | bytes 2359304 | tf_op jit(solution)/shard_map/ppermute | solution.py:815
  344.6 31.1 %collective-permute-start.17 = (bf16[640,1024]{1,0:T(8,128)(2,1)}, bf16[640,1024]{1,0:T(8,128)(2,1)}, u32[]{:S(2)}, u32[]{:S(2)}) collective-permute-start(bf16[640,1024]{1,0:T(8,128)(2,1)} %get-tuple-element.275), channel_id=1, source_target_pairs={{0,2},{2,0},{4,6},{6,4},{8,10},{10,8},{12,14},{14,12},{16,18},{18,... | collective-permute-start | bytes 3932168 | tf_op jit(solution)/shard_map/ppermute | solution.py:815
  370.6 46.1 %collective-permute-start.24 = (bf16[1024,768]{1,0:T(8,128)(2,1)}, bf16[1024,768]{1,0:T(8,128)(2,1)}, u32[]{:S(2)}, u32[]{:S(2)}) collective-permute-start(bf16[1024,768]{1,0:T(8,128)(2,1)} %grads.16), channel_id=1, source_target_pairs={{0,1},{1,0},{2,3},{3,2},{4,5},{5,4},{6,7},{7,6},{8,9},{9,8},{10,11... | collective-permute-start | bytes 4718600 | tf_op jit(solution)/shard_map/ppermute | solution.py:1192
  370.6 72.2 %collective-permute-start.30 = (bf16[1024,1024]{1,0:T(8,128)(2,1)}, bf16[1024,1024]{1,0:T(8,128)(2,1)}, u32[]{:S(2)}, u32[]{:S(2)}) collective-permute-start(bf16[1024,1024]{1,0:T(8,128)(2,1)} %all-gather.2.cloned.1.call-done.refs_1_), channel_id=1, source_target_pairs={{1,0},{0,1},{3,2},{2,3},{5,4},{4,5},{7,6},{6,7},{9,8},{8,9},{11,10... | collective-permute-start | bytes 6291464 | tf_op jit(solution)/shard_map/ppermute | solution.py:1186
  378.0 33.1 %collective-permute-start.20 = (bf16[320,1024]{1,0:T(8,128)(2,1)}, bf16[320,1024]{1,0:T(8,128)(2,1)}, u32[]{:S(2)}, u32[]{:S(2)}) collective-permute-start(bf16[320,1024]{1,0:T(8,128)(2,1)} %get-tuple-element.286), channel_id=1, source_target_pairs={{0,8},{2,10},{4,12},{6,14},{8,0},{10,2},{12,4},{14,6},{16,24},{18,... | collective-permute-start | bytes 1966088 | tf_op jit(solution)/shard_map/ppermute | solution.py:815
  381.3 29.9 %collective-permute-start.19 = (bf16[128,1536]{1,0:T(8,128)(2,1)}, bf16[128,1536]{1,0:T(8,128)(2,1)}, u32[]{:S(2)}, u32[]{:S(2)}) collective-permute-start(bf16[128,1536]{1,0:T(8,128)(2,1)} %get-tuple-element.283), channel_id=1, source_target_pairs={{0,8},{2,10},{4,12},{6,14},{8,0},{10,2},{12,4},{14,6},{16,24},{18,... | collective-permute-start | bytes 1179656 | tf_op jit(solution)/shard_map/ppermute | solution.py:815
  398.3 71.8 %collective-permute-start.28 = (bf16[768,1024]{1,0:T(8,128)(2,1)}, bf16[768,1024]{1,0:T(8,128)(2,1)}, u32[]{:S(2)}, u32[]{:S(2)}) collective-permute-start(bf16[768,1024]{1,0:T(8,128)(2,1)} %get-tuple-element.293), channel_id=1, source_target_pairs={{0,4},{2,6},{4,0},{6,2},{8,12},{10,14},{12,8},{14,10},{16,20},{18,... | collective-permute-start | bytes 4718600 | tf_op jit(solution)/shard_map/ppermute | solution.py:815
  412.5 27.1 %collective-permute-start.22 = (bf16[64,1536]{1,0:T(8,128)(2,1)S(1)}, bf16[64,1536]{1,0:T(8,128)(2,1)S(1)}, u32[]{:S(2)}, u32[]{:S(2)}) collective-permute-start(bf16[64,1536]{1,0:T(8,128)(2,1)S(1)} %get-tuple-element.297), channel_id=1, source_target_pairs={{0,16},{2,18},{4,20},{6,22},{8,24},{10,26},{12,28},{14,30},{16,0},... | collective-permute-start | bytes 589832 | tf_op jit(solution)/shard_map/ppermute | solution.py:815
  416.3 23.6 %collective-permute-start.23 = (bf16[160,1024]{1,0:T(8,128)(2,1)S(1)}, bf16[160,1024]{1,0:T(8,128)(2,1)S(1)}, u32[]{:S(2)}, u32[]{:S(2)}) collective-permute-start(bf16[160,1024]{1,0:T(8,128)(2,1)S(1)} %get-tuple-element.300), channel_id=1, source_target_pairs={{0,16},{2,18},{4,20},{6,22},{8,24},{10,26},{12,28},{14,30},{16,0},... | collective-permute-start | bytes 983048 | tf_op jit(solution)/shard_map/ppermute | solution.py:815
  416.7 53.4 %collective-permute-start.27 = (bf16[512,1024]{1,0:T(8,128)(2,1)}, bf16[512,1024]{1,0:T(8,128)(2,1)}, u32[]{:S(2)}, u32[]{:S(2)}) collective-permute-start(bf16[512,1024]{1,0:T(8,128)(2,1)} %get-tuple-element.291), channel_id=1, source_target_pairs={{0,2},{2,0},{4,6},{6,4},{8,10},{10,8},{12,14},{14,12},{16,18},{18,... | collective-permute-start | bytes 3145736 | tf_op jit(solution)/shard_map/ppermute | solution.py:815
  439.6 30.5 %collective-permute-start.29 = (bf16[512,768]{1,0:T(8,128)(2,1)}, bf16[512,768]{1,0:T(8,128)(2,1)}, u32[]{:S(2)}, u32[]{:S(2)}) collective-permute-start(bf16[512,768]{1,0:T(8,128)(2,1)} %get-tuple-element.304), channel_id=1, source_target_pairs={{0,2},{2,0},{4,6},{6,4},{8,10},{10,8},{12,14},{14,12},{16,18},{18,... | collective-permute-start | bytes 2359304 | tf_op jit(solution)/shard_map/ppermute | solution.py:815
  440.1 30.0 %collective-permute-start.26 = (bf16[160,1024]{1,0:T(8,128)(2,1)S(1)}, bf16[160,1024]{1,0:T(8,128)(2,1)S(1)}, u32[]{:S(2)}, u32[]{:S(2)}) collective-permute-start(bf16[160,1024]{1,0:T(8,128)(2,1)S(1)} %add_convert_fusion.refs_0_), channel_id=1, source_target_pairs={{0,16},{2,18},{4,20},{6,22},{8,24},{10,26},{12,28},{14,30},{16,0},... | collective-permute-start | bytes 983048 | tf_op jit(solution)/shard_map/ppermute | solution.py:815
  442.8 27.3 %collective-permute-start.25 = (bf16[64,1536]{1,0:T(8,128)(2,1)S(1)}, bf16[64,1536]{1,0:T(8,128)(2,1)S(1)}, u32[]{:S(2)}, u32[]{:S(2)}) collective-permute-start(bf16[64,1536]{1,0:T(8,128)(2,1)S(1)} %add_convert_fusion.2.refs_0_), channel_id=1, source_target_pairs={{0,16},{2,18},{4,20},{6,22},{8,24},{10,26},{12,28},{14,30},{16,0},... | collective-permute-start | bytes 589832 | tf_op jit(solution)/shard_map/ppermute | solution.py:815
  475.0 29.6 %collective-permute-start.34 = (bf16[384,1024]{1,0:T(8,128)(2,1)}, bf16[384,1024]{1,0:T(8,128)(2,1)S(1)}, u32[]{:S(2)}, u32[]{:S(2)}) collective-permute-start(bf16[384,1024]{1,0:T(8,128)(2,1)} %get-tuple-element.319), channel_id=1, source_target_pairs={{0,2},{2,0},{4,6},{6,4},{8,10},{10,8},{12,14},{14,12},{16,18},{18,... | collective-permute-start | bytes 2359304 | tf_op jit(solution)/shard_map/ppermute | solution.py:815
  476.8 27.0 %collective-permute-start.31 = (bf16[128,1536]{1,0:T(8,128)(2,1)S(1)}, bf16[128,1536]{1,0:T(8,128)(2,1)S(1)}, u32[]{:S(2)}, u32[]{:S(2)}) collective-permute-start(bf16[128,1536]{1,0:T(8,128)(2,1)S(1)} %spread.30.refs_0_), channel_id=1, source_target_pairs={{0,8},{2,10},{4,12},{6,14},{8,0},{10,2},{12,4},{14,6},{16,24},{18,... | collective-permute-start | bytes 1179656 | tf_op jit(solution)/shard_map/ppermute | solution.py:815
  477.4 27.2 %collective-permute-start.32 = (bf16[320,1024]{1,0:T(8,128)(2,1)S(1)}, bf16[320,1024]{1,0:T(8,128)(2,1)S(1)}, u32[]{:S(2)}, u32[]{:S(2)}) collective-permute-start(bf16[320,1024]{1,0:T(8,128)(2,1)S(1)} %spread.31.refs_0_), channel_id=1, source_target_pairs={{0,8},{2,10},{4,12},{6,14},{8,0},{10,2},{12,4},{14,6},{16,24},{18,... | collective-permute-start | bytes 1966088 | tf_op jit(solution)/shard_map/ppermute | solution.py:815
  482.4 22.2 %collective-permute-start.33 = (bf16[256,1024]{1,0:T(8,128)(2,1)}, bf16[256,1024]{1,0:T(8,128)(2,1)}, u32[]{:S(2)}, u32[]{:S(2)}) collective-permute-start(bf16[256,1024]{1,0:T(8,128)(2,1)} %get-tuple-element.317), channel_id=1, source_target_pairs={{0,4},{2,6},{4,0},{6,2},{8,12},{10,14},{12,8},{14,10},{16,20},{18,... | collective-permute-start | bytes 1572872 | tf_op jit(solution)/shard_map/ppermute | solution.py:815
  504.6 28.8 %collective-permute-start.43 = (bf16[1024,768]{1,0:T(8,128)(2,1)S(1)}, bf16[1024,768]{1,0:T(8,128)(2,1)S(1)}, u32[]{:S(2)}, u32[]{:S(2)}) collective-permute-start(bf16[1024,768]{1,0:T(8,128)(2,1)S(1)} %grads.20), channel_id=1, source_target_pairs={{0,1},{1,0},{2,3},{3,2},{4,5},{5,4},{6,7},{7,6},{8,9},{9,8},{10,11... | collective-permute-start | bytes 4718600 | tf_op jit(solution)/shard_map/ppermute | solution.py:1192
  505.7 40.9 %collective-permute-start.40 = (bf16[640,1024]{1,0:T(8,128)(2,1)S(1)}, bf16[640,1024]{1,0:T(8,128)(2,1)S(1)}, u32[]{:S(2)}, u32[]{:S(2)}) collective-permute-start(bf16[640,1024]{1,0:T(8,128)(2,1)S(1)} %spread.33.refs_0_), channel_id=1, source_target_pairs={{0,2},{2,0},{4,6},{6,4},{8,10},{10,8},{12,14},{14,12},{16,18},{18,... | collective-permute-start | bytes 3932168 | tf_op jit(solution)/shard_map/ppermute | solution.py:815
  507.2 39.4 %collective-permute-start.39 = (bf16[256,1536]{1,0:T(8,128)(2,1)S(1)}, bf16[256,1536]{1,0:T(8,128)(2,1)S(1)}, u32[]{:S(2)}, u32[]{:S(2)}) collective-permute-start(bf16[256,1536]{1,0:T(8,128)(2,1)S(1)} %spread.32.refs_0_), channel_id=1, source_target_pairs={{0,4},{2,6},{4,0},{6,2},{8,12},{10,14},{12,8},{14,10},{16,20},{18,... | collective-permute-start | bytes 2359304 | tf_op jit(solution)/shard_map/ppermute | solution.py:815
  548.6 121.6 %collective-permute-start.59 = (bf16[1280,1024]{1,0:T(8,128)(2,1)}, bf16[1280,1024]{1,0:T(8,128)(2,1)}, u32[]{:S(2)}, u32[]{:S(2)}) collective-permute-start(bf16[1280,1024]{1,0:T(8,128)(2,1)} %spread.35.refs_0_), channel_id=1, source_target_pairs={{0,4},{2,6},{4,0},{6,2},{8,12},{10,14},{12,8},{14,10},{16,20},{18,... | collective-permute-start | bytes 7864328 | tf_op jit(solution)/shard_map/ppermute | solution.py:815
  550.2 54.0 %collective-permute-start.47 = (bf16[512,768]{1,0:T(8,128)(2,1)}, bf16[512,768]{1,0:T(8,128)(2,1)}, u32[]{:S(2)}, u32[]{:S(2)}) collective-permute-start(bf16[512,768]{1,0:T(8,128)(2,1)} %get-tuple-element.350), channel_id=1, source_target_pairs={{0,2},{2,0},{4,6},{6,4},{8,10},{10,8},{12,14},{14,12},{16,18},{18,... | collective-permute-start | bytes 2359304 | tf_op jit(solution)/shard_map/ppermute | solution.py:815
  553.1 51.0 %collective-permute-start.45 = (bf16[96,1024]{1,0:T(8,128)(2,1)S(1)}, bf16[96,1024]{1,0:T(8,128)(2,1)}, u32[]{:S(2)}, u32[]{:S(2)}) collective-permute-start(bf16[96,1024]{1,0:T(8,128)(2,1)S(1)} %add_convert_fusion.1.refs_0_), channel_id=1, source_target_pairs={{0,16},{2,18},{4,20},{6,22},{8,24},{10,26},{12,28},{14,30},{16,0},... | collective-permute-start | bytes 589832 | tf_op jit(solution)/shard_map/ppermute | solution.py:815
  556.1 114.1 %collective-permute-start.58 = (bf16[512,1536]{1,0:T(8,128)(2,1)}, bf16[512,1536]{1,0:T(8,128)(2,1)}, u32[]{:S(2)}, u32[]{:S(2)}) collective-permute-start(bf16[512,1536]{1,0:T(8,128)(2,1)} %spread.34.refs_0_), channel_id=1, source_target_pairs={{0,2},{2,0},{4,6},{6,4},{8,10},{10,8},{12,14},{14,12},{16,18},{18,... | collective-permute-start | bytes 4718600 | tf_op jit(solution)/shard_map/ppermute | solution.py:815
  565.3 38.8 %collective-permute-start.44 = (bf16[64,1024]{1,0:T(8,128)(2,1)S(1)}, bf16[64,1024]{1,0:T(8,128)(2,1)}, u32[]{:S(2)}, u32[]{:S(2)}) collective-permute-start(bf16[64,1024]{1,0:T(8,128)(2,1)S(1)} %add_convert_fusion.3.refs_0_), channel_id=1, source_target_pairs={{0,16},{2,18},{4,20},{6,22},{8,24},{10,26},{12,28},{14,30},{16,0},... | collective-permute-start | bytes 393224 | tf_op jit(solution)/shard_map/ppermute | solution.py:815
  606.5 44.7 %collective-permute-start.49 = (bf16[192,1024]{1,0:T(8,128)(2,1)S(1)}, bf16[192,1024]{1,0:T(8,128)(2,1)S(1)}, u32[]{:S(2)}, u32[]{:S(2)}) collective-permute-start(bf16[192,1024]{1,0:T(8,128)(2,1)S(1)} %spread.37.refs_0_), channel_id=1, source_target_pairs={{0,8},{2,10},{4,12},{6,14},{8,0},{10,2},{12,4},{14,6},{16,24},{18,... | collective-permute-start | bytes 1179656 | tf_op jit(solution)/shard_map/ppermute | solution.py:815
  608.8 42.3 %collective-permute-start.51 = (bf16[256,768]{1,0:T(8,128)(2,1)S(1)}, bf16[256,768]{1,0:T(8,128)(2,1)S(1)}, u32[]{:S(2)}, u32[]{:S(2)}) collective-permute-start(bf16[256,768]{1,0:T(8,128)(2,1)S(1)} %get-tuple-element.372), channel_id=1, source_target_pairs={{0,4},{2,6},{4,0},{6,2},{8,12},{10,14},{12,8},{14,10},{16,20},{18,... | collective-permute-start | bytes 1179656 | tf_op jit(solution)/shard_map/ppermute | solution.py:815
  620.0 31.2 %collective-permute-start.48 = (bf16[128,1024]{1,0:T(8,128)(2,1)S(1)}, bf16[128,1024]{1,0:T(8,128)(2,1)S(1)}, u32[]{:S(2)}, u32[]{:S(2)}) collective-permute-start(bf16[128,1024]{1,0:T(8,128)(2,1)S(1)} %spread.36.refs_0_), channel_id=1, source_target_pairs={{0,8},{2,10},{4,12},{6,14},{8,0},{10,2},{12,4},{14,6},{16,24},{18,... | collective-permute-start | bytes 786440 | tf_op jit(solution)/shard_map/ppermute | solution.py:815
  670.4 56.5 %collective-permute-start.67 = (bf16[768,1024]{1,0:T(8,128)(2,1)S(1)}, bf16[768,1024]{1,0:T(8,128)(2,1)S(1)}, u32[]{:S(2)}, u32[]{:S(2)}) collective-permute-start(bf16[768,1024]{1,0:T(8,128)(2,1)S(1)} %spread.44.refs_2_), channel_id=1, source_target_pairs={{0,4},{2,6},{4,0},{6,2},{8,12},{10,14},{12,8},{14,10},{16,20},{18,... | collective-permute-start | bytes 4718600 | tf_op jit(solution)/shard_map/ppermute | solution.py:815
  672.0 54.9 %collective-permute-start.66 = (bf16[512,1024]{1,0:T(8,128)(2,1)S(1)}, bf16[512,1024]{1,0:T(8,128)(2,1)S(1)}, u32[]{:S(2)}, u32[]{:S(2)}) collective-permute-start(bf16[512,1024]{1,0:T(8,128)(2,1)S(1)} %spread.43.refs_0_), channel_id=1, source_target_pairs={{0,2},{2,0},{4,6},{6,4},{8,10},{10,8},{12,14},{14,12},{16,18},{18,... | collective-permute-start | bytes 3145736 | tf_op jit(solution)/shard_map/ppermute | solution.py:815
  673.9 39.8 %collective-permute-start.60 = (bf16[256,768]{1,0:T(8,128)(2,1)S(1)}, bf16[256,768]{1,0:T(8,128)(2,1)S(1)}, u32[]{:S(2)}, u32[]{:S(2)}) collective-permute-start(bf16[256,768]{1,0:T(8,128)(2,1)S(1)} %spread.42.refs_0_), channel_id=1, source_target_pairs={{0,4},{2,6},{4,0},{6,2},{8,12},{10,14},{12,8},{14,10},{16,20},{18,... | collective-permute-start | bytes 1179656 | tf_op jit(solution)/shard_map/ppermute | solution.py:815
  714.0 22.1 %collective-permute-start.70 = (bf16[512,768]{1,0:T(8,128)(2,1)S(1)}, bf16[512,768]{1,0:T(8,128)(2,1)S(1)}, u32[]{:S(2)}, u32[]{:S(2)}) collective-permute-start(bf16[512,768]{1,0:T(8,128)(2,1)S(1)} %spread.46.refs_0_), channel_id=1, source_target_pairs={{0,2},{2,0},{4,6},{6,4},{8,10},{10,8},{12,14},{14,12},{16,18},{18,... | collective-permute-start | bytes 2359304 | tf_op jit(solution)/shard_map/ppermute | solution.py:815
  (146 other events, 1491.7 us)
Sparse Core Ops, SparseCore 0:
  11.4 63.4 all-gather.1
